TPU v7x, 128 devices: a whole 4x4x4 slice. The times are simulated.
128 devices in a mesh: dp: 16 (over y, x), expert: 8 (over z, core).
Axes of the slice: x: 4, y: 4, z: 4, core: 2. Of those that a mesh axis runs over, the one named last changes fastest.
Arguments:
- tokens: bfloat16 [16384, 4096], P(('dp', 'expert')), may hold values from -6 to 6
- expert_ids: int32 [16384, 8], P(('dp', 'expert')), may hold values from 0 to 127, all different within a row; in each aligned block of 128 rows (0 to 127, 128 to 255, ...) at most 16 rows name the same one
- gates: float32 [16384, 8], P(('dp', 'expert')), may hold values from 0.1 to 1
- cotangent: bfloat16 [16384, 4096], P(('dp', 'expert')), may hold values from -6 to 6
- w_gate: bfloat16 [8, 4096, 768], P('expert', 'dp'), may hold values from -0.09375 to 0.09375
- w_up: bfloat16 [8, 4096, 768], P('expert', 'dp'), may hold values from -0.09375 to 0.09375
- w_down: bfloat16 [8, 4096, 768], P('expert', 'dp'), may hold values from -0.21875 to 0.21875
Outputs:
- mixed: bfloat16 [16384, 4096], P(('dp', 'expert'))
- grad_tokens: bfloat16 [16384, 4096], P(('dp', 'expert'))
- grad_gates: float32 [16384, 8], P(('dp', 'expert'))
- grad_w_gate: float32 [8, 4096, 768], P('expert', 'dp')
- grad_w_up: float32 [8, 4096, 768], P('expert', 'dp')
- grad_w_down: float32 [8, 4096, 768], P('expert', 'dp')
Inputs may be any that keep to these rules, and one draw needn't show every extreme that they name: `expert_ids`: each token names 8 different experts; among the tokens of one device no expert is named more than 16 times.
All inputs are finite; a program needn't handle non-finite values.
Results may differ from a plain program's by a relative error of at most 0.015.
Values may be sent and summed in bfloat16 or wider, within the bound.
No kernel may reach another device: no remote copies, remote signals or barrier semaphores. Data moves between devices by JAX's collectives and lax.ppermute only.
A program may use at most 128 MiB of HBM per device.

v0:
```python
import jax
import jax.numpy as jnp
from jax import lax
from jax.sharding import PartitionSpec as P

CAP = 16


def partner(array, axis, apart):
    return lax.ppermute(array, axis, [(i, i ^ 1 << apart) for i in range(lax.axis_size(axis))])


def exchange_rows(blocks):
    count = blocks.shape[0]
    order = jnp.bitwise_xor(jnp.arange(count, dtype=jnp.int32), lax.axis_index("expert"))
    placed = jnp.take(blocks, order, axis=0)
    for level in range(count.bit_length() - 1):
        low = 1 << level
        shaped = placed.reshape((count // (2 * low), 2, low) + blocks.shape[1:])
        arrived = partner(shaped[:, 1], "expert", level)
        placed = jnp.stack([shaped[:, 0], arrived], axis=1).reshape(blocks.shape)
    return jnp.take(placed, order, axis=0)


def contract_first(left, right):
    return lax.dot_general(
        left, right, (((0,), (0,)), ((), ())), preferred_element_type=jnp.float32
    )


def contract_last(left, right):
    return lax.dot_general(
        left, right, (((1,), (1,)), ((), ())), preferred_element_type=jnp.float32
    )


def per_device(tokens, expert_ids, gates, cotangent, w_gate, w_up, w_down):
    experts_here = lax.axis_size("expert")
    tok_rows, width = tokens.shape
    total_slots = experts_here * CAP
    labels = jnp.arange(experts_here, dtype=jnp.int32)
    hit = expert_ids[:, :, None] == labels[None, None, :]
    used = jnp.sum(hit.astype(jnp.int32), axis=1)
    weight_of = jnp.sum(jnp.where(hit, gates[:, :, None], jnp.float32(0.0)), axis=1)
    position = jnp.cumsum(used, axis=0) - used
    slot_ids = jnp.arange(CAP, dtype=jnp.int32)
    chosen = (used.T[:, None, :] == 1) & (position.T[:, None, :] == slot_ids[None, :, None])
    dispatch = chosen.reshape(total_slots, tok_rows)
    dispatch_b = dispatch.astype(jnp.bfloat16)
    combine = jnp.where(chosen, weight_of.T[:, None, :], jnp.float32(0.0)).reshape(
        total_slots, tok_rows
    )
    weight_slot = jnp.sum(combine, axis=1)
    outgoing = jnp.dot(dispatch_b, tokens, preferred_element_type=jnp.float32).astype(jnp.bfloat16)
    arrived = exchange_rows(outgoing.reshape(experts_here, CAP, width)).reshape(total_slots, width)
    full_gate, full_up, full_down = (
        lax.all_gather(w_gate, "dp", axis=1, tiled=True),
        lax.all_gather(w_up, "dp", axis=1, tiled=True),
        lax.all_gather(w_down, "dp", axis=1, tiled=True),
    )
    wg = full_gate[0]
    wu = full_up[0]
    wd = full_down[0]
    gate_pre = jnp.dot(arrived, wg, preferred_element_type=jnp.float32)
    up_pre = jnp.dot(arrived, wu, preferred_element_type=jnp.float32)
    sig = jax.nn.sigmoid(gate_pre)
    act = gate_pre * sig
    hidden = (act * up_pre).astype(jnp.bfloat16)
    produced = contract_last(hidden, wd).astype(jnp.bfloat16)
    returned = exchange_rows(produced.reshape(experts_here, CAP, width)).reshape(total_slots, width)
    scaled = weight_slot[:, None] * returned.astype(jnp.float32)
    upper_part = scaled.astype(jnp.bfloat16)
    lower_part = (scaled - upper_part.astype(jnp.float32)).astype(jnp.bfloat16)
    mixed = contract_first(dispatch_b, upper_part) + contract_first(dispatch_b, lower_part)
    scores = contract_last(returned, cotangent).reshape(experts_here, CAP, tok_rows)
    per_expert = jnp.sum(jnp.where(chosen, scores, jnp.float32(0.0)), axis=1)
    grad_gates = jnp.sum(jnp.where(hit, per_expert.T[:, None, :], jnp.float32(0.0)), axis=2)
    picked_grad = jnp.dot(dispatch_b, cotangent, preferred_element_type=jnp.float32)
    grad_send = (weight_slot[:, None] * picked_grad).astype(jnp.bfloat16)
    grad_out = exchange_rows(grad_send.reshape(experts_here, CAP, width)).reshape(
        total_slots, width
    )
    grad_hidden = jnp.dot(grad_out, wd, preferred_element_type=jnp.float32)
    grad_gate_pre = (grad_hidden * up_pre * sig * (1.0 + gate_pre * (1.0 - sig))).astype(
        jnp.bfloat16
    )
    grad_up_pre = (grad_hidden * act).astype(jnp.bfloat16)
    grad_rows = (contract_last(grad_gate_pre, wg) + contract_last(grad_up_pre, wu)).astype(
        jnp.bfloat16
    )
    grad_back = exchange_rows(grad_rows.reshape(experts_here, CAP, width)).reshape(
        total_slots, width
    )
    grad_tokens = contract_first(dispatch_b, grad_back).astype(jnp.bfloat16)
    part_gate = contract_first(arrived, grad_gate_pre)
    part_up = contract_first(arrived, grad_up_pre)
    part_down = contract_first(grad_out, hidden)
    sum_gate, sum_up, sum_down = (
        lax.psum_scatter(
            part_gate.astype(jnp.bfloat16), "dp", scatter_dimension=0, tiled=True
        ).astype(jnp.float32),
        lax.psum_scatter(
            part_up.astype(jnp.bfloat16), "dp", scatter_dimension=0, tiled=True
        ).astype(jnp.float32),
        lax.psum_scatter(
            part_down.astype(jnp.bfloat16), "dp", scatter_dimension=0, tiled=True
        ).astype(jnp.float32),
    )
    grad_w_gate = sum_gate[None]
    grad_w_up = sum_up[None]
    grad_w_down = sum_down[None]
    return (
        mixed.astype(jnp.bfloat16),
        grad_tokens,
        grad_gates,
        grad_w_gate,
        grad_w_up,
        grad_w_down,
    )


def solution(mesh):
    in_specs = (
        P(("dp", "expert"), None),
        P(("dp", "expert"), None),
        P(("dp", "expert"), None),
        P(("dp", "expert"), None),
        P("expert", "dp", None),
        P("expert", "dp", None),
        P("expert", "dp", None),
    )
    out_specs = (
        P(("dp", "expert"), None),
        P(("dp", "expert"), None),
        P(("dp", "expert"), None),
        P("expert", "dp", None),
        P("expert", "dp", None),
        P("expert", "dp", None),
    )
    return jax.shard_map(
        per_device, mesh=mesh, in_specs=in_specs, out_specs=out_specs, check_vma=False
    )
```

profile of v0, /device:TPU:1, one launch (start us, length us, event | category | flops | bytes accessed | tf_op | source)
XLA Modules:
  0.0 541.1 jit_solution(14670467382392663981)
XLA Ops:
  10.7 1.7 convolution_convert_fusion.3
  13.3 1.5 collective-permute-start
  14.8 1.5 collective-permute-done
  16.4 1.8 collective-permute-start.1
  18.2 12.0 %collective-permute-done.1 = bf16[2,2,16,4096]{3,2,0,1:T(8,128)(2,1)S(1)} collective-permute-done((bf16[2,2,16,4096]{3,2,0,1:T(8,128)(2,1)S(1)}, bf16[2,2,16,4096]{3,2,0,1:T(8,128)(2,1)S(1)}, u32[]{:S(2)}, u32[]{:S(2)}) %collective-permute-start.1) | collective-permute-done | bytes 524320 | tf_op jit(solution)/shard_map/ppermute | solution.py:10
  30.4 3.2 collective-permute-start.2
  33.6 11.1 %collective-permute-done.2 = bf16[1,4,16,4096]{3,2,1,0:T(8,128)(2,1)S(1)} collective-permute-done((bf16[1,4,16,4096]{3,2,1,0:T(8,128)(2,1)S(1)}, bf16[1,4,16,4096]{3,2,1,0:T(8,128)(2,1)S(1)}, u32[]{:S(2)}, u32[]{:S(2)}) %collective-permute-start.2) | collective-permute-done | bytes 524320 | tf_op jit(solution)/shard_map/ppermute | solution.py:10
  45.6 29.1 %all-gather.4.cloned.1.call-done = bf16[1,4096,768]{2,1,0:T(8,128)(2,1)} async-done(((bf16[1,256,768]{2,1,0:T(8,128)(2,1)}), bf16[1,4096,768]{2,1,0:T(8,128)(2,1)}) %all-gather.4.cloned.1.call-update) | async-done | bytes 6291472 | tf_op jit(solution)/shard_map/all_gather | solution.py:57
  74.6 3.8 fusion.10
  78.4 59.3 %all-gather.6.cloned.1.call-done = bf16[1,4096,768]{2,1,0:T(8,128)(2,1)} async-done(((bf16[1,256,768]{2,1,0:T(8,128)(2,1)}), bf16[1,4096,768]{2,1,0:T(8,128)(2,1)}) %all-gather.6.cloned.1.call-update) | async-done | bytes 6291472 | tf_op jit(solution)/shard_map/all_gather | solution.py:58
  137.7 4.5 multiply_convert_fusion.2
  142.3 58.6 %all-gather.8.cloned.1.call-done = bf16[1,4096,768]{2,1,0:T(8,128)(2,1)} async-done(((bf16[1,256,768]{2,1,0:T(8,128)(2,1)}), bf16[1,4096,768]{2,1,0:T(8,128)(2,1)}) %all-gather.8.cloned.1.call-update) | async-done | bytes 6291472 | tf_op jit(solution)/shard_map/all_gather | solution.py:59
  200.8 4.9 fusion.22
  205.8 1.6 gather_fusion.2
  207.3 1.4 broadcast_select_fusion.5
  209.6 1.5 collective-permute-done.3
  211.2 1.4 collective-permute-start.4
  212.6 11.9 %collective-permute-done.4 = bf16[2,2,16,4096]{3,2,0,1:T(8,128)(2,1)S(1)} collective-permute-done((bf16[2,2,16,4096]{3,2,0,1:T(8,128)(2,1)S(1)}, bf16[2,2,16,4096]{3,2,0,1:T(8,128)(2,1)S(1)}, u32[]{:S(2)}, u32[]{:S(2)}) %collective-permute-start.4) | collective-permute-done | bytes 524320 | tf_op jit(solution)/shard_map/ppermute | solution.py:10
  224.6 3.0 collective-permute-start.5
  227.6 10.8 %collective-permute-done.5 = bf16[1,4,16,4096]{3,2,1,0:T(8,128)(2,1)S(1)} collective-permute-done((bf16[1,4,16,4096]{3,2,1,0:T(8,128)(2,1)S(1)}, bf16[1,4,16,4096]{3,2,1,0:T(8,128)(2,1)S(1)}, u32[]{:S(2)}, u32[]{:S(2)}) %collective-permute-start.5) | collective-permute-done | bytes 524320 | tf_op jit(solution)/shard_map/ppermute | solution.py:10
  239.5 1.8 gather_fusion.3
  242.7 1.4 fusion.20
  244.1 1.8 gather_fusion.4
  246.2 2.2 collective-permute-start.6
  248.4 1.5 collective-permute-done.6
  250.0 1.4 collective-permute-start.7
  251.4 11.9 %collective-permute-done.7 = bf16[2,2,16,4096]{3,2,0,1:T(8,128)(2,1)S(1)} collective-permute-done((bf16[2,2,16,4096]{3,2,0,1:T(8,128)(2,1)S(1)}, bf16[2,2,16,4096]{3,2,0,1:T(8,128)(2,1)S(1)}, u32[]{:S(2)}, u32[]{:S(2)}) %collective-permute-start.7) | collective-permute-done | bytes 524320 | tf_op jit(solution)/shard_map/ppermute | solution.py:10
  263.4 3.0 collective-permute-start.8
  266.4 10.8 %collective-permute-done.8 = bf16[1,4,16,4096]{3,2,1,0:T(8,128)(2,1)S(1)} collective-permute-done((bf16[1,4,16,4096]{3,2,1,0:T(8,128)(2,1)S(1)}, bf16[1,4,16,4096]{3,2,1,0:T(8,128)(2,1)S(1)}, u32[]{:S(2)}, u32[]{:S(2)}) %collective-permute-start.8) | collective-permute-done | bytes 524320 | tf_op jit(solution)/shard_map/ppermute | solution.py:10
  278.1 4.4 convolution_convert_fusion
  282.9 3.9 multiply_convert_fusion.1
  286.7 4.5 convolution_convert_fusion.2
  291.3 4.5 convolution_convert_fusion.1
  295.8 5.1 fusion.4
  300.9 2.2 fusion.17
  304.2 2.3 collective-permute-start.9
  306.5 1.5 collective-permute-done.9
  309.5 12.0 %collective-permute-done.10 = bf16[2,2,16,4096]{3,2,0,1:T(8,128)(2,1)S(1)} collective-permute-done((bf16[2,2,16,4096]{3,2,0,1:T(8,128)(2,1)S(1)}, bf16[2,2,16,4096]{3,2,0,1:T(8,128)(2,1)S(1)}, u32[]{:S(2)}, u32[]{:S(2)}) %collective-permute-start.10) | collective-permute-done | bytes 524320 | tf_op jit(solution)/shard_map/ppermute | solution.py:10
  321.7 3.0 collective-permute-start.11
  325.2 1.6 fusion.16
  326.7 8.8 %collective-permute-done.11 = bf16[1,4,16,4096]{3,2,1,0:T(8,128)(2,1)S(1)} collective-permute-done((bf16[1,4,16,4096]{3,2,1,0:T(8,128)(2,1)S(1)}, bf16[1,4,16,4096]{3,2,1,0:T(8,128)(2,1)S(1)}, u32[]{:S(2)}, u32[]{:S(2)}) %collective-permute-start.11) | collective-permute-done | bytes 524320 | tf_op jit(solution)/shard_map/ppermute | solution.py:10
  336.4 1.5 fusion.21
  337.9 26.3 %reduce-scatter.8.cloned.1.call-done = bf16[256,768]{1,0:T(8,128)(2,1)} async-done(((bf16[4096,768]{1,0:T(8,128)(2,1)}), bf16[256,768]{1,0:T(8,128)(2,1)}) %reduce-scatter.8.cloned.1.call-update) | async-done | bytes 393232 | tf_op jit(solution)/shard_map/reduce_scatter | solution.py:105
  364.2 1.9 bitcast_convert_fusion
  366.1 82.1 %reduce-scatter.4.cloned.1.call-done = bf16[256,768]{1,0:T(8,128)(2,1)} async-done(((bf16[4096,768]{1,0:T(8,128)(2,1)}), bf16[256,768]{1,0:T(8,128)(2,1)}) %reduce-scatter.4.cloned.1.call-update) | async-done | bytes 393232 | tf_op jit(solution)/shard_map/reduce_scatter | solution.py:99
  448.3 1.9 bitcast_convert_fusion.2
  450.2 82.1 %reduce-scatter.6.cloned.1.call-done = bf16[256,768]{1,0:T(8,128)(2,1)} async-done(((bf16[4096,768]{1,0:T(8,128)(2,1)}), bf16[256,768]{1,0:T(8,128)(2,1)}) %reduce-scatter.6.cloned.1.call-update) | async-done | bytes 393232 | tf_op jit(solution)/shard_map/reduce_scatter | solution.py:102
  532.3 1.9 bitcast_convert_fusion.1
  (86 shorter events, 14.8 us)
Async XLA Ops:
  7.2 234.2 %copy-start = (bf16[128,4096]{1,0:T(8,128)(2,1)S(1)}, bf16[128,4096]{1,0:T(8,128)(2,1)}, u32[]{:S(2)}) copy-start(bf16[128,4096]{1,0:T(8,128)(2,1)} %param.12) | copy-start | bytes 3145732
  7.2 67.4 %all-gather.4.cloned.1.call-start = ((), (), s32[]{:S(2)}) async-start(), calls=%async_computation.3 | async-start | bytes 6684672 | tf_op jit(solution)/shard_map/all_gather | solution.py:57
  7.9 129.8 %all-gather.6.cloned.1.call-start = ((), (), s32[]{:S(2)}) async-start(), calls=%async_computation.4 | async-start | bytes 6684672 | tf_op jit(solution)/shard_map/all_gather | solution.py:58
  8.7 192.2 %all-gather.8.cloned.1.call-start = ((), (), s32[]{:S(2)}) async-start(), calls=%async_computation.5 | async-start | bytes 6684672 | tf_op jit(solution)/shard_map/all_gather | solution.py:59
  9.4 354.8 %reduce-scatter.8.cloned.1.call-start = ((), (), s32[]{:S(2)}) async-start(), calls=%async_computation.8 | async-start | bytes 6684672 | tf_op jit(solution)/shard_map/reduce_scatter | solution.py:105
  10.7 266.6 %copy-start.7 = (s32[1024]{0:T(1024)}, s32[1024]{0:T(1024)S(1)}, u32[]{:S(2)}) copy-start(s32[1024]{0:T(1024)S(1)} %pad_clamp_fusion) | copy-start | bytes 12292
  13.3 3.0 collective-permute-start
  16.4 13.8 %collective-permute-start.1 = (bf16[2,2,16,4096]{3,2,0,1:T(8,128)(2,1)S(1)}, bf16[2,2,16,4096]{3,2,0,1:T(8,128)(2,1)S(1)}, u32[]{:S(2)}, u32[]{:S(2)}) collective-permute-start(bf16[2,2,16,4096]{3,2,0,1:T(8,128)(2,1)S(1)} %get-tuple-element.30), channel_id=1, source_target_pairs={{0,2},{1,3},{2,0},{3,1},{4,6},{5,7},{6,4},{7,5},{8,10},{9,11},{10,... | collective-permute-start | bytes 1572872 | tf_op jit(solution)/shard_map/ppermute | solution.py:10
  30.4 14.3 %collective-permute-start.2 = (bf16[1,4,16,4096]{3,2,1,0:T(8,128)(2,1)S(1)}, bf16[1,4,16,4096]{3,2,1,0:T(8,128)(2,1)S(1)}, u32[]{:S(2)}, u32[]{:S(2)}) collective-permute-start(bf16[1,4,16,4096]{3,2,1,0:T(8,128)(2,1)S(1)} %get-tuple-element.28), channel_id=1, source_target_pairs={{0,4},{1,5},{2,6},{3,7},{4,0},{5,1},{6,2},{7,3},{8,12},{9,13},{10,... | collective-permute-start | bytes 1572872 | tf_op jit(solution)/shard_map/ppermute | solution.py:10
  78.4 63.9 %copy-start.4 = (f32[128,768]{1,0:T(8,128)}, f32[128,768]{1,0:T(8,128)S(1)}, u32[]{:S(2)}) copy-start(f32[128,768]{1,0:T(8,128)S(1)} %fusion.10) | copy-start | bytes 1179652
  208.8 2.3 collective-permute-start.3
  211.1 30.7 %copy-start.8 = (s32[128,8]{0,1:T(8,128)S(1)}, s32[128,8]{0,1:T(8,128)}, u32[]{:S(2)}) copy-start(s32[128,8]{0,1:T(8,128)} %param.10) | copy-start | bytes 12292
  211.1 30.8 %copy-start.9 = (f32[128,8]{0,1:T(8,128)S(1)}, f32[128,8]{0,1:T(8,128)}, u32[]{:S(2)}) copy-start(f32[128,8]{0,1:T(8,128)} %param.11) | copy-start | bytes 12292
  211.2 13.2 %collective-permute-start.4 = (bf16[2,2,16,4096]{3,2,0,1:T(8,128)(2,1)S(1)}, bf16[2,2,16,4096]{3,2,0,1:T(8,128)(2,1)S(1)}, u32[]{:S(2)}, u32[]{:S(2)}) collective-permute-start(bf16[2,2,16,4096]{3,2,0,1:T(8,128)(2,1)S(1)} %get-tuple-element.24), channel_id=1, source_target_pairs={{0,2},{1,3},{2,0},{3,1},{4,6},{5,7},{6,4},{7,5},{8,10},{9,11},{10,... | collective-permute-start | bytes 1572872 | tf_op jit(solution)/shard_map/ppermute | solution.py:10
  224.6 13.8 %collective-permute-start.5 = (bf16[1,4,16,4096]{3,2,1,0:T(8,128)(2,1)S(1)}, bf16[1,4,16,4096]{3,2,1,0:T(8,128)(2,1)S(1)}, u32[]{:S(2)}, u32[]{:S(2)}) collective-permute-start(bf16[1,4,16,4096]{3,2,1,0:T(8,128)(2,1)S(1)} %get-tuple-element.22), channel_id=1, source_target_pairs={{0,4},{1,5},{2,6},{3,7},{4,0},{5,1},{6,2},{7,3},{8,12},{9,13},{10,... | collective-permute-start | bytes 1572872 | tf_op jit(solution)/shard_map/ppermute | solution.py:10
  241.3 8.7 %copy-start.2 = (bf16[8,16,4096]{2,1,0:T(8,128)(2,1)}, bf16[8,16,4096]{2,1,0:T(8,128)(2,1)S(1)}, u32[]{:S(2)}) copy-start(bf16[8,16,4096]{2,1,0:T(8,128)(2,1)S(1)} %gather_fusion.3) | copy-start | bytes 3145732
  246.2 3.7 collective-permute-start.6
  250.0 13.2 %collective-permute-start.7 = (bf16[2,2,16,4096]{3,2,0,1:T(8,128)(2,1)S(1)}, bf16[2,2,16,4096]{3,2,0,1:T(8,128)(2,1)S(1)}, u32[]{:S(2)}, u32[]{:S(2)}) collective-permute-start(bf16[2,2,16,4096]{3,2,0,1:T(8,128)(2,1)S(1)} %get-tuple-element.18), channel_id=1, source_target_pairs={{0,2},{1,3},{2,0},{3,1},{4,6},{5,7},{6,4},{7,5},{8,10},{9,11},{10,... | collective-permute-start | bytes 1572872 | tf_op jit(solution)/shard_map/ppermute | solution.py:10
  263.4 13.8 %collective-permute-start.8 = (bf16[1,4,16,4096]{3,2,1,0:T(8,128)(2,1)S(1)}, bf16[1,4,16,4096]{3,2,1,0:T(8,128)(2,1)S(1)}, u32[]{:S(2)}, u32[]{:S(2)}) collective-permute-start(bf16[1,4,16,4096]{3,2,1,0:T(8,128)(2,1)S(1)} %get-tuple-element.16), channel_id=1, source_target_pairs={{0,4},{1,5},{2,6},{3,7},{4,0},{5,1},{6,2},{7,3},{8,12},{9,13},{10,... | collective-permute-start | bytes 1572872 | tf_op jit(solution)/shard_map/ppermute | solution.py:10
  278.1 4.7 copy-start.5
  278.1 4.7 copy-start.6
  282.6 165.7 %reduce-scatter.4.cloned.1.call-start = ((), (), s32[]{:S(2)}) async-start(), calls=%async_computation.6 | async-start | bytes 6684672 | tf_op jit(solution)/shard_map/reduce_scatter | solution.py:99
  291.2 241.1 %reduce-scatter.6.cloned.1.call-start = ((), (), s32[]{:S(2)}) async-start(), calls=%async_computation.7 | async-start | bytes 6684672 | tf_op jit(solution)/shard_map/reduce_scatter | solution.py:102
  295.8 5.1 slice-start
  295.8 5.1 slice-start.1
  303.1 21.5 %copy-start.3 = (bf16[8,16,4096]{2,1,0:T(8,128)(2,1)S(1)}, bf16[8,16,4096]{2,1,0:T(8,128)(2,1)}, u32[]{:S(2)}) copy-start(bf16[8,16,4096]{2,1,0:T(8,128)(2,1)} %copy-done.2) | copy-start | bytes 3145732
  304.2 3.8 collective-permute-start.9
  308.2 13.3 %collective-permute-start.10 = (bf16[2,2,16,4096]{3,2,0,1:T(8,128)(2,1)S(1)}, bf16[2,2,16,4096]{3,2,0,1:T(8,128)(2,1)S(1)}, u32[]{:S(2)}, u32[]{:S(2)}) collective-permute-start(bf16[2,2,16,4096]{3,2,0,1:T(8,128)(2,1)S(1)} %get-tuple-element.12), channel_id=1, source_target_pairs={{0,2},{1,3},{2,0},{3,1},{4,6},{5,7},{6,4},{7,5},{8,10},{9,11},{10,... | collective-permute-start | bytes 1572872 | tf_op jit(solution)/shard_map/ppermute | solution.py:10
  321.7 13.9 %collective-permute-start.11 = (bf16[1,4,16,4096]{3,2,1,0:T(8,128)(2,1)S(1)}, bf16[1,4,16,4096]{3,2,1,0:T(8,128)(2,1)S(1)}, u32[]{:S(2)}, u32[]{:S(2)}) collective-permute-start(bf16[1,4,16,4096]{3,2,1,0:T(8,128)(2,1)S(1)} %get-tuple-element.10), channel_id=1, source_target_pairs={{0,4},{1,5},{2,6},{3,7},{4,0},{5,1},{6,2},{7,3},{8,12},{9,13},{10,... | collective-permute-start | bytes 1572872 | tf_op jit(solution)/shard_map/ppermute | solution.py:10
  324.6 209.6 %copy-start.1 = (bf16[128,4096]{1,0:T(8,128)(2,1)S(1)}, bf16[128,4096]{1,0:T(8,128)(2,1)}, u32[]{:S(2)}) copy-start(bf16[128,4096]{1,0:T(8,128)(2,1)} %param.12) | copy-start | bytes 3145732
Sparse Core Ops, SparseCore 0:
  10.2 64.4 all-gather.3
  76.8 60.9 all-gather.5
  139.9 60.9 all-gather.7
  282.7 81.4 reduce-scatter.7
  367.5 80.7 reduce-scatter.3
  451.5 80.7 reduce-scatter.5
where the time goes:
time: 542 us; the launch traced here: 541 us
  waiting for transfers between devices  435 us (80%)
  matrix products  44.9 us (8%)
  starting transfers between devices  25.1 us (5%)
  between operations  14.6 us (3%)
  other arithmetic  11.8 us (2%)
  local copies, waits for them, and re-layouts  9.75 us (2%)
    ppermute x12, waiting for transfers between devices, partner(): lax.ppermute(array, axis, [(i, i ^ 1 << apart) for i in range(lax.axis_si...  95.4 us
    reduce_scatter x1, waiting for transfers between devices, per_device(): lax.psum_scatter(part_gate.astype(jnp.bfloat16), 'dp', scatter_dimension=...  82.1 us
    reduce_scatter x1, waiting for transfers between devices, per_device(): lax.psum_scatter(part_up.astype(jnp.bfloat16), 'dp', scatter_dimension=0,...  82.1 us
    all_gather x1, waiting for transfers between devices, per_device(): lax.all_gather(w_up, 'dp', axis=1, tiled=True)  59.3 us
    all_gather x1, waiting for transfers between devices, per_device(): lax.all_gather(w_down, 'dp', axis=1, tiled=True)  58.6 us
    all_gather x1, waiting for transfers between devices, per_device(): lax.all_gather(w_gate, 'dp', axis=1, tiled=True)  29.1 us
    reduce_scatter x1, waiting for transfers between devices, per_device(): lax.psum_scatter(part_down.astype(jnp.bfloat16), 'dp', scatter_dimension=...  26.3 us
    ppermute x12, starting transfers between devices, partner(): lax.ppermute(array, axis, [(i, i ^ 1 << apart) for i in range(lax.axis_si...  24.7 us
  transfers between devices with their start and end apart: 18, of which 18 were waited for; matrix products, arithmetic and copies ran while one was open for 8% of the time, Pallas kernels for 0%

commit v1 on v0

v1 whole, which is shorter than its diff:
```python
import jax
import jax.numpy as jnp
from jax import lax
from jax.experimental import pallas as pl
from jax.experimental.pallas import tpu as pltpu
from jax.sharding import PartitionSpec as P

CAP = 16
SIDE = 4
AXES = ("dp", "expert")
BF = jnp.bfloat16
F32 = jnp.float32
REL = 8
COLS = 256
FW = 768
VMEM = 56 * 2**20


def _dev(y, x, z, c):
    return ((y % SIDE) * SIDE + x % SIDE) * 8 + (z % SIDE) * 2 + c % 2


def _perm(move):
    pairs = []
    for i in range(128):
        y, x, z, c = i // 32, i // 8 % 4, i // 2 % 4, i % 2
        pairs.append((i, _dev(*move(y, x, z, c))))
    return pairs


def shift_a(v, s):
    return lax.ppermute(
        v, AXES, _perm(lambda y, x, z, c: (y, x + s, z, c) if c == 0 else (y + s, x, z, c))
    )


def shift_b(v, s):
    return lax.ppermute(
        v, AXES, _perm(lambda y, x, z, c: (y + s, x, z, c) if c == 0 else (y, x + s, z, c))
    )


def shift_z(v, dz, dc):
    return lax.ppermute(v, AXES, _perm(lambda y, x, z, c: (y, x, z + dz, c + dc)))


def dot(left, right):
    return jnp.dot(left, right, preferred_element_type=F32)


def dot_last(left, right):
    return lax.dot_general(left, right, (((1,), (1,)), ((), ())), preferred_element_type=F32)


def dot_first(left, right):
    return lax.dot_general(left, right, (((0,), (0,)), ((), ())), preferred_element_type=F32)


def call(kernel, outs, ins, flops, smem=0):
    vm = pl.BlockSpec(memory_space=pltpu.VMEM)
    sm = pl.BlockSpec(memory_space=pltpu.SMEM)
    moved = sum(v.size * v.dtype.itemsize for v in list(ins[smem:]) + list(outs))
    return pl.pallas_call(
        kernel,
        out_shape=tuple(outs),
        in_specs=[sm] * smem + [vm] * (len(ins) - smem),
        out_specs=tuple([vm] * len(outs)),
        compiler_params=pltpu.CompilerParams(vmem_limit_bytes=VMEM),
        cost_estimate=pl.CostEstimate(flops=flops, bytes_accessed=moved, transcendentals=0),
    )(*ins)


def shape(dims, dtype=BF):
    return jax.ShapeDtypeStruct(dims, dtype)


def routing(place, ids, gates):
    tok = ids.shape[1]
    z, c = place[2], place[3]
    labels, used, weight = [], [], []
    for r in range(REL):
        label = ((z + r % 4) & 3) * 2 + (c ^ (r // 4))
        hit = ids == label
        labels.append(label)
        used.append(jnp.sum(jnp.where(hit, 1.0, 0.0), axis=0, keepdims=True))
        weight.append(jnp.sum(jnp.where(hit, gates, 0.0), axis=0, keepdims=True))
    used_all = jnp.concatenate(used, axis=0)
    before = lax.broadcasted_iota(jnp.int32, (tok, tok), 0) < lax.broadcasted_iota(
        jnp.int32, (tok, tok), 1
    )
    position = dot(used_all.astype(BF), jnp.where(before, 1.0, 0.0).astype(BF))
    slot = lax.broadcasted_iota(jnp.int32, (CAP, tok), 0).astype(F32)
    chosen, scale = [], []
    for r in range(REL):
        mask = (position[r : r + 1] == slot) & (used[r] > 0.5)
        chosen.append(jnp.where(mask, 1.0, 0.0))
        scale.append(jnp.sum(jnp.where(mask, weight[r], 0.0), axis=1, keepdims=True))
    return labels, jnp.concatenate(chosen, axis=0), jnp.concatenate(scale, axis=0)


def block_place(place, dc, yb, xb):
    y, x, c = place[0], place[1], place[3]
    dy, dx = (yb - y + 4) & 3, (xb - x + 4) & 3
    flip = c ^ dc
    sb = jnp.where(flip == 0, dy, dx)
    sa = (4 - jnp.where(flip == 0, dx, dy)) & 3
    return sb, sa


def dispatch_kernel(place, ids, gates, tokens, cotangent, *outs):
    _, chosen, scale = routing(place, ids[...], gates[...])
    chosen = chosen.astype(BF)
    for blk in range(16):
        cols = slice(blk * COLS, blk * COLS + COLS)
        rows = dot(chosen, tokens[:, cols]).astype(BF)
        grads = (scale * dot(chosen, cotangent[:, cols])).astype(BF)
        for dc in range(2):
            sb, sa = block_place(place, dc, blk // 4, blk % 4)
            lanes = pl.ds(pl.multiple_of(sa * COLS, COLS), COLS)
            for dz in range(4):
                r = dc * 4 + dz
                outs[r][0, sb, :, lanes] = rows[r * CAP : r * CAP + CAP]
                outs[r][1, sb, :, lanes] = grads[r * CAP : r * CAP + CAP]


def to_b_kernel(*refs):
    ins, outs = refs[:REL], refs[REL:]
    for s in range(SIDE):
        for r in range(REL):
            for kind in range(2):
                outs[s][kind, r * CAP : r * CAP + CAP, :] = ins[r][kind, s]


def to_z_kernel(*refs):
    ins, outs = refs[:SIDE], refs[SIDE:]
    for s in range(SIDE):
        for r in range(REL):
            for kind in range(2):
                outs[r][kind, s] = ins[s][kind, r * CAP : r * CAP + CAP, :]


def stacked(pieces, kind, cols=slice(None)):
    return jnp.concatenate([p[kind, :, cols] for p in pieces], axis=0)


def partial_kernel(*refs):
    xs, ws, own, outs = refs[:4], refs[4:8], refs[8], refs[9:]
    rows = xs[0].shape[1]
    for which in range(3):
        left = stacked(xs, 0 if which < 2 else 1)
        for n in range(FW // COLS):
            cols = slice(n * COLS, n * COLS + COLS)
            at = slice(which * FW + n * COLS, which * FW + n * COLS + COLS)
            got = dot(left, stacked(ws, which, cols))
            own[:, at] = got[:rows]
            for p in range(1, SIDE):
                outs[p - 1][:, at] = got[p * rows : p * rows + rows].astype(BF)


def hidden_kernel(own, p1, p2, p3, out):
    def full(which):
        at = slice(which * FW, which * FW + FW)
        return (own[:, at] + p1[:, at].astype(F32)) + (
            p2[:, at].astype(F32) + p3[:, at].astype(F32)
        )

    gate, up, grad = full(0), full(1), full(2)
    sig = jax.nn.sigmoid(gate)
    act = gate * sig
    out[:, :FW] = (act * up).astype(BF)
    out[:, FW : 2 * FW] = (grad * up * sig * (1.0 + gate * (1.0 - sig))).astype(BF)
    out[:, 2 * FW :] = (grad * act).astype(BF)


def rows_kernel(*refs):
    hs, ws, outs = refs[:4], refs[4:8], refs[8:]
    rows = hs[0].shape[0]
    hidden, ggate, gup = (
        jnp.concatenate([h[:, k * FW : k * FW + FW] for h in hs], axis=0) for k in range(3)
    )
    for a in range(SIDE):
        cols = slice(a * COLS, a * COLS + COLS)
        made = dot_last(hidden, ws[a][2]).astype(BF)
        back = (dot_last(ggate, ws[a][0]) + dot_last(gup, ws[a][1])).astype(BF)
        for p in range(SIDE):
            outs[p][0, :, cols] = made[p * rows : p * rows + rows]
            outs[p][1, :, cols] = back[p * rows : p * rows + rows]


def weights_kernel(*refs):
    hs, xs, own, outs = refs[:4], refs[4:8], refs[8], refs[9:]
    hidden, ggate, gup = (
        jnp.concatenate([h[:, k * FW : k * FW + FW] for h in hs], axis=0) for k in range(3)
    )
    for a in range(SIDE):
        cols = slice(a * COLS, a * COLS + COLS)
        x, g = stacked(xs, 0, cols), stacked(xs, 1, cols)
        for k, (left, right) in enumerate(((x, ggate), (x, gup), (g, hidden))):
            got = dot_first(left, right)
            if a == 0:
                own[k] = got
            else:
                outs[a - 1][k] = got.astype(BF)


def total_kernel(own, p1, p2, p3, *outs):
    for k in range(3):
        outs[k][0] = (own[k] + p1[k].astype(F32)) + (p2[k].astype(F32) + p3[k].astype(F32))


def combine_kernel(place, ids, gates, cotangent, *refs):
    backs, (mixed, gtok, ggates) = refs[:REL], refs[REL:]
    labels, chosen, scale = routing(place, ids[...], gates[...])
    spread = chosen.T.astype(BF)
    scores = jnp.zeros(chosen.shape, F32)
    for blk in range(16):
        cols = slice(blk * COLS, blk * COLS + COLS)
        made, grads = [], []
        for dc in range(2):
            sb, sa = block_place(place, dc, blk // 4, blk % 4)
            lanes = pl.ds(pl.multiple_of(sa * COLS, COLS), COLS)
            for dz in range(4):
                made.append(backs[dc * 4 + dz][0, sb, :, lanes])
                grads.append(backs[dc * 4 + dz][1, sb, :, lanes])
        made, grads = jnp.concatenate(made, axis=0), jnp.concatenate(grads, axis=0)
        scaled = scale * made.astype(F32)
        upper = scaled.astype(BF)
        lower = (scaled - upper.astype(F32)).astype(BF)
        mixed[:, cols] = (dot(spread, upper) + dot(spread, lower)).astype(BF)
        gtok[:, cols] = dot(spread, grads).astype(BF)
        scores += dot_last(made, cotangent[:, cols])
    picked = chosen * scores
    total = jnp.zeros(ids.shape, F32)
    for r in range(REL):
        mine = jnp.sum(picked[r * CAP : r * CAP + CAP], axis=0, keepdims=True)
        total += jnp.where(ids[...] == labels[r], mine, 0.0)
    ggates[...] = total


def per_device(tokens, expert_ids, gates, cotangent, w_gate, w_up, w_down):
    tok, width = tokens.shape
    dp, ex = lax.axis_index("dp"), lax.axis_index("expert")
    place = jnp.stack([dp // 4, dp % 4, ex // 2, ex % 2]).astype(jnp.int32)
    ids_t, gates_t = expert_ids.T, gates.T
    chunk = width // SIDE

    held = jnp.concatenate([w_gate, w_up, w_down], axis=0)
    ws = [held] + [shift_a(held, s) for s in (1, 2, 3)]

    sends = call(
        dispatch_kernel,
        [shape((2, SIDE, CAP, chunk))] * REL,
        (place, ids_t, gates_t, tokens, cotangent),
        4 * tok * tok * width,
        smem=1,
    )
    came = [sends[0]] + [shift_z(sends[r], r % 4, r // 4) for r in range(1, REL)]
    turned = call(to_b_kernel, [shape((2, REL * CAP, chunk))] * SIDE, came, 0)
    xs = [turned[0]] + [shift_b(turned[s], s) for s in (1, 2, 3)]

    rows = REL * CAP
    parts = call(
        partial_kernel,
        [shape((rows, 3 * FW), F32)] + [shape((rows, 3 * FW))] * 3,
        (*xs, *ws),
        2 * SIDE * rows * chunk * 3 * FW,
    )
    others = [shift_b(parts[s], -s) for s in (1, 2, 3)]
    (mid,) = call(hidden_kernel, [shape((rows, 3 * FW))], (parts[0], *others), 0)
    hs = [mid] + [shift_b(mid, s) for s in (1, 2, 3)]

    outs = call(
        rows_kernel,
        [shape((2, rows, chunk))] * SIDE,
        (*hs, *ws),
        2 * SIDE * rows * chunk * 3 * FW,
    )
    home = [outs[0]] + [shift_b(outs[s], -s) for s in (1, 2, 3)]
    grads = call(
        weights_kernel,
        [shape((3, COLS, FW), F32)] + [shape((3, COLS, FW))] * 3,
        (*hs, *xs),
        2 * SIDE * rows * chunk * 3 * FW,
    )
    others_w = [shift_a(grads[s], -s) for s in (1, 2, 3)]
    split = call(to_z_kernel, [shape((2, SIDE, CAP, chunk))] * REL, home, 0)
    backs = [split[0]] + [shift_z(split[r], -(r % 4), r // 4) for r in range(1, REL)]
    gw = call(total_kernel, [shape((1, COLS, FW), F32)] * 3, (grads[0], *others_w), 0)
    mixed, gtok, gg_t = call(
        combine_kernel,
        [shape((tok, width)), shape((tok, width)), shape(ids_t.shape, F32)],
        (place, ids_t, gates_t, cotangent, *backs),
        8 * tok * tok * width,
        smem=1,
    )
    return mixed, gtok, gg_t.T, *gw


def solution(mesh):
    rows, cut = P(("dp", "expert"), None), P("expert", "dp", None)
    return jax.shard_map(
        per_device,
        mesh=mesh,
        in_specs=(rows,) * 4 + (cut,) * 3,
        out_specs=(rows,) * 3 + (cut,) * 3,
        check_vma=False,
    )
```

time: 542 us -> 215 us (0.40)
  waiting for transfers between devices: 435 us -> 91.1 us
  starting transfers between devices: 25.1 us -> 73.6 us
  matrix products: 44.9 us -> 0 us
  Pallas kernels: 0 us -> 41.3 us
  between operations: 14.6 us -> 0.93 us
  other arithmetic: 11.8 us -> 0.59 us
    reduce_scatter x3 -> x0, waiting for transfers between devices: 191 us -> none  [the longest x1 82.1 us: per_device(): lax.psum_scatter(part_gate.astype(jnp.bfloat16), 'dp', scatter_dimension=...]
    all_gather x3 -> x0, waiting for transfers between devices: 147 us -> none  [the longest x1 59.3 us: per_device(): lax.all_gather(w_up, 'dp', axis=1, tiled=True)]
    ppermute x12 -> x32, starting transfers between devices: 24.7 us -> 73.6 us  [the longest x14 57.1 us: shift_z(): lax.ppermute(v, AXES, _perm(lambda y, x, z, c: (y, x, z + dz, c + dc)))]
    dot_general x15 -> x0, matrix products: 44.9 us -> none  [the longest x6 17 us: contract_first(): lax.dot_general(left, right, (((0,), (0,)), ((), ())), preferred_element_...]
    pallas_call x0 -> x9, Pallas kernels: none -> 41.3 us  [call(): pl.pallas_call(kernel, out_shape=tuple(outs), in_specs=[sm] * smem + [vm]...]
    gather x8 -> x0, local copies, waits for them, and re-layouts: 8.71 us -> none  [the longest x4 4.9 us: exchange_rows(): placed = jnp.take(blocks, order, axis=0)]
    unnamed x28 -> x74, local copies, waits for them, and re-layouts: 0.4 us -> 6.78 us
    broadcast_in_dim x3 -> x0, other arithmetic: 5.78 us -> none  [the longest x1 1.93 us: per_device(): grad_w_down = sum_down[None]]
  transfers between devices with their start and end apart: 18 -> 32, of which waited for: 18 -> 17; matrix products, arithmetic and copies ran while one was open for 8% -> 0% of each run, Pallas kernels for 0% -> 8%
where the time goes in v1:
time: 215 us; the launch traced here: 214 us
  waiting for transfers between devices  91.1 us (42%)
  starting transfers between devices  73.6 us (34%)
  Pallas kernels  41.3 us (19%)
  local copies, waits for them, and re-layouts  6.81 us (3%)
    ppermute x12, waiting for transfers between devices, shift_b(): lax.ppermute(v, AXES, _perm(lambda y, x, z, c: (y + s, x, z, c) if c == 0...  64.4 us
    ppermute x14, starting transfers between devices, shift_z(): lax.ppermute(v, AXES, _perm(lambda y, x, z, c: (y, x, z + dz, c + dc)))  57.1 us
    pallas_call x9, Pallas kernels, call(): pl.pallas_call(kernel, out_shape=tuple(outs), in_specs=[sm] * smem + [vm]...  41.3 us
    ppermute x14, waiting for transfers between devices, shift_z(): lax.ppermute(v, AXES, _perm(lambda y, x, z, c: (y, x, z + dz, c + dc)))  25.7 us
    ppermute x12, starting transfers between devices, shift_b(): lax.ppermute(v, AXES, _perm(lambda y, x, z, c: (y + s, x, z, c) if c == 0...  9.79 us
    unnamed x74, local copies, waits for them, and re-layouts  6.78 us
    ppermute x6, starting transfers between devices, shift_a(): lax.ppermute(v, AXES, _perm(lambda y, x, z, c: (y, x + s, z, c) if c == 0...  6.69 us
  transfers between devices with their start and end apart: 32, of which 17 were waited for; matrix products, arithmetic and copies ran while one was open for 0% of the time, Pallas kernels for 8%

profile of v1, /device:TPU:1, one launch (start us, length us, event | category | flops | bytes accessed | tf_op | source)
XLA Modules:
  0.0 214.3 jit_solution(914814663828591959)
XLA Ops:
  1.3 3.8 %shard_map.118 = (bf16[2,4,16,1024]{3,2,1,0:T(8,128)(2,1)}, bf16[2,4,16,1024]{3,2,1,0:T(8,128)(2,1)}, bf16[2,4,16,1024]{3,2,1,0:T(8,128)(2,1)}, bf16[2,4,16,1024...) custom-call(s32[4]{0:T(128)} %pad_add_fusion.place, ...), custom_call_target="tpu_custom_call" | custom-call | flops 268435456 | bytes 4202496 | tf_op jit(solution)/shard_map/pallas_call | solution.py:63
  5.0 2.5 %collective-permute-start = (bf16[2,4,16,1024]{3,2,1,0:T(8,128)(2,1)}, bf16[2,4,16,1024]{3,2,1,0:T(8,128)(2,1)S(1)}, u32[]{:S(2)}, u32[]{:S(2)}) collective-permute-start(bf16[2,4,16,1024]{3,2,1,0:T(8,128)(2,1)} %get-tuple-element.45), channel_id=1, source_target_pairs={{0,2},{1,3},{2,4},{3,5},{4,6},{5,7},{6,0},{7,1},{8,10},{9,11},{10,... | collective-permute-start | bytes 786440 | tf_op jit(solution)/shard_map/ppermute | solution.py:44
  7.5 3.3 %collective-permute-start.1 = (bf16[2,4,16,1024]{3,2,1,0:T(8,128)(2,1)}, bf16[2,4,16,1024]{3,2,1,0:T(8,128)(2,1)S(1)}, u32[]{:S(2)}, u32[]{:S(2)}) collective-permute-start(bf16[2,4,16,1024]{3,2,1,0:T(8,128)(2,1)} %get-tuple-element.46), channel_id=1, source_target_pairs={{0,4},{1,5},{2,6},{3,7},{4,0},{5,1},{6,2},{7,3},{8,12},{9,13},{10,... | collective-permute-start | bytes 786440 | tf_op jit(solution)/shard_map/ppermute | solution.py:44
  10.8 0.7 collective-permute-start.2
  11.5 1.5 collective-permute-start.3
  13.7 2.2 %collective-permute-done.refs_1_ = bf16[2,4,16,1024]{3,2,1,0:T(8,128)(2,1)S(1)} collective-permute-done((bf16[2,4,16,1024]{3,2,1,0:T(8,128)(2,1)}, bf16[2,4,16,1024]{3,2,1,0:T(8,128)(2,1)S(1)}, u32[]{:S(2)}, u32[]{:S(2)}) %collective-permute-start) | collective-permute-done | bytes 262176 | tf_op jit(solution)/shard_map/ppermute | solution.py:44
  15.9 9.1 %collective-permute-start.5 = (bf16[2,4,16,1024]{3,2,1,0:T(8,128)(2,1)}, bf16[2,4,16,1024]{3,2,1,0:T(8,128)(2,1)S(1)}, u32[]{:S(2)}, u32[]{:S(2)}) collective-permute-start(bf16[2,4,16,1024]{3,2,1,0:T(8,128)(2,1)} %get-tuple-element.50), channel_id=1, source_target_pairs={{0,5},{1,4},{2,7},{3,6},{4,1},{5,0},{6,3},{7,2},{8,13},{9,12},{10,... | collective-permute-start | bytes 786440 | tf_op jit(solution)/shard_map/ppermute | solution.py:44
  25.2 2.8 %collective-permute-start.12 = (bf16[3,256,768]{2,1,0:T(8,128)(2,1)S(1)}, bf16[3,256,768]{2,1,0:T(8,128)(2,1)S(1)}, u32[]{:S(2)}, u32[]{:S(2)}) collective-permute-start(bf16[3,256,768]{2,1,0:T(8,128)(2,1)S(1)} %constant_dynamic-update-slice_fusion.refs_4_), channel_id=1, source_target_pairs={{0,24},{1,97},{2,26},{3,99},{4,28},{5,101},{6,30},{7,103},{8,0},{9... | collective-permute-start | bytes 3538952 | tf_op jit(solution)/shard_map/ppermute | solution.py:32
  28.3 1.2 collective-permute-start.10
  29.5 5.2 %collective-permute-done.5.refs_6_ = bf16[2,4,16,1024]{3,2,1,0:T(8,128)(2,1)S(1)} collective-permute-done((bf16[2,4,16,1024]{3,2,1,0:T(8,128)(2,1)}, bf16[2,4,16,1024]{3,2,1,0:T(8,128)(2,1)S(1)}, u32[]{:S(2)}, u32[]{:S(2)}) %collective-permute-start.5) | collective-permute-done | bytes 262176 | tf_op jit(solution)/shard_map/ppermute | solution.py:44
  35.6 2.8 %shard_map.119 = (bf16[2,128,1024]{2,1,0:T(8,128)(2,1)}, bf16[2,128,1024]{2,1,0:T(8,128)(2,1)}, bf16[2,128,1024]{2,1,0:T(8,128)(2,1)}, bf16[2,128,1024]{2,1,0:T(8,128)(2,1)}) custom-call(bf16[2,4,16,1024]{3,2,1,0:T(8,128)(2,1)} %get-tuple-element.44.refs_0_, bf16[2,4,16,1024]{3,2,1,0:T(8,128)(2,1)} %copy-done.12, bf16[2,4,16,1024]{3,2,1,0:T(8,128)(2,1)} %copy-done.13, ...), custom_call_target="tpu_custom_call" | custom-call | bytes 4194304 | tf_op jit(solution)/shard_map/pallas_call | solution.py:63
  38.4 0.9 collective-permute-start.7
  39.3 2.5 %collective-permute-start.8 = (bf16[2,128,1024]{2,1,0:T(8,128)(2,1)}, bf16[2,128,1024]{2,1,0:T(8,128)(2,1)S(1)}, u32[]{:S(2)}, u32[]{:S(2)}) collective-permute-start(bf16[2,128,1024]{2,1,0:T(8,128)(2,1)} %get-tuple-element.54), channel_id=1, source_target_pairs={{0,64},{1,17},{2,66},{3,19},{4,68},{5,21},{6,70},{7,23},{8,72},{9,... | collective-permute-start | bytes 1572872 | tf_op jit(solution)/shard_map/ppermute | solution.py:38
  41.8 17.4 %collective-permute-done.7.refs_1_.refs_5_ = bf16[2,128,1024]{2,1,0:T(8,128)(2,1)S(1)} collective-permute-done((bf16[2,128,1024]{2,1,0:T(8,128)(2,1)}, bf16[2,128,1024]{2,1,0:T(8,128)(2,1)S(1)}, u32[]{:S(2)}, u32[]{:S(2)}) %collective-permute-start.7) | collective-permute-done | bytes 524320 | tf_op jit(solution)/shard_map/ppermute | solution.py:38
  59.2 6.6 %collective-permute-done.8.refs_2_.refs_6_ = bf16[2,128,1024]{2,1,0:T(8,128)(2,1)S(1)} collective-permute-done((bf16[2,128,1024]{2,1,0:T(8,128)(2,1)}, bf16[2,128,1024]{2,1,0:T(8,128)(2,1)S(1)}, u32[]{:S(2)}, u32[]{:S(2)}) %collective-permute-start.8) | collective-permute-done | bytes 524320 | tf_op jit(solution)/shard_map/ppermute | solution.py:38
  65.8 1.9 collective-permute-done.9.refs_3_.refs_7_
  67.7 1.0 collective-permute-done.10.refs_5_
  69.7 7.1 %shard_map.120 = (f32[128,2304]{1,0:T(8,128)}, bf16[128,2304]{1,0:T(8,128)(2,1)}, bf16[128,2304]{1,0:T(8,128)(2,1)}, bf16[128,2304]{1,0:T(8,128)(2,1)}) custom-call(bf16[2,128,1024]{2,1,0:T(8,128)(2,1)} %get-tuple-element.52.refs_0_.refs_4_, bf16[2,128,1024]{2,1,0:T(8,128)(2,1)} %copy-done.33, bf16[2,128,1024]{2,1,0:T(8,128)(2,1)} %copy-done.34, ...), custom_call_target="tpu_custom_call" | custom-call | flops 2415919104 | bytes 9764864 | tf_op jit(solution)/shard_map/pallas_call | solution.py:63
  76.8 2.2 %collective-permute-start.13 = (bf16[128,2304]{1,0:T(8,128)(2,1)}, bf16[128,2304]{1,0:T(8,128)(2,1)S(1)}, u32[]{:S(2)}, u32[]{:S(2)}) collective-permute-start(bf16[128,2304]{1,0:T(8,128)(2,1)} %get-tuple-element.57), channel_id=1, source_target_pairs={{0,96},{1,25},{2,98},{3,27},{4,100},{5,29},{6,102},{7,31},{8,104},... | collective-permute-start | bytes 1769480 | tf_op jit(solution)/shard_map/ppermute | solution.py:38
  80.1 12.4 %collective-permute-done.13.p1 = bf16[128,2304]{1,0:T(8,128)(2,1)S(1)} collective-permute-done((bf16[128,2304]{1,0:T(8,128)(2,1)}, bf16[128,2304]{1,0:T(8,128)(2,1)S(1)}, u32[]{:S(2)}, u32[]{:S(2)}) %collective-permute-start.13) | collective-permute-done | bytes 589856 | tf_op jit(solution)/shard_map/ppermute | solution.py:38
  92.5 3.6 %collective-permute-done.15.p3 = bf16[128,2304]{1,0:T(8,128)(2,1)S(1)} collective-permute-done((bf16[128,2304]{1,0:T(8,128)(2,1)}, bf16[128,2304]{1,0:T(8,128)(2,1)S(1)}, u32[]{:S(2)}, u32[]{:S(2)}) %collective-permute-start.15) | collective-permute-done | bytes 589856 | tf_op jit(solution)/shard_map/ppermute | solution.py:38
  96.1 0.8 copy-done.5
  96.9 3.0 %shard_map.121.refs_0_ = bf16[128,2304]{1,0:T(8,128)(2,1)} custom-call(f32[128,2304]{1,0:T(8,128)} %get-tuple-element.56.own, bf16[128,2304]{1,0:T(8,128)(2,1)} %copy-done.3, bf16[128,2304]{1,0:T(8,128)(2,1)} %copy-done.4, bf16[128,2304]{1,0:T(8,128)(2,1)} %copy-done.5), custom_call_target="tpu_custom_call" | custom-call | bytes 3538944 | tf_op jit(solution)/shard_map/pallas_call | solution.py:63
  101.4 7.8 %collective-permute-done.18.refs_3_ = bf16[128,2304]{1,0:T(8,128)(2,1)S(1)} collective-permute-done((bf16[128,2304]{1,0:T(8,128)(2,1)}, bf16[128,2304]{1,0:T(8,128)(2,1)S(1)}, u32[]{:S(2)}, u32[]{:S(2)}) %collective-permute-start.18) | collective-permute-done | bytes 589856 | tf_op jit(solution)/shard_map/ppermute | solution.py:38
  109.1 1.9 collective-permute-done.17.refs_2_
  111.0 6.3 %collective-permute-done.16.refs_1_ = bf16[128,2304]{1,0:T(8,128)(2,1)S(1)} collective-permute-done((bf16[128,2304]{1,0:T(8,128)(2,1)}, bf16[128,2304]{1,0:T(8,128)(2,1)S(1)}, u32[]{:S(2)}, u32[]{:S(2)}) %collective-permute-start.16) | collective-permute-done | bytes 589856 | tf_op jit(solution)/shard_map/ppermute | solution.py:38
  117.3 0.8 copy-done.32
  118.1 6.9 %shard_map.122 = (bf16[2,128,1024]{2,1,0:T(8,128)(2,1)}, bf16[2,128,1024]{2,1,0:T(8,128)(2,1)}, bf16[2,128,1024]{2,1,0:T(8,128)(2,1)}, bf16[2,128,1024]{2,1,0:T(8,128)(2,1)}) custom-call(bf16[128,2304]{1,0:T(8,128)(2,1)} %shard_map.121.refs_0_, bf16[128,2304]{1,0:T(8,128)(2,1)} %copy-done.32, bf16[128,2304]{1,0:T(8,128)(2,1)} %copy-done.31, ...), custom_call_target="tpu_custom_call" | custom-call | flops 2415919104 | bytes 9175040 | tf_op jit(solution)/shard_map/pallas_call | solution.py:63
  125.0 1.1 collective-permute-start.19
  126.7 5.9 %shard_map.125 = (f32[3,256,768]{2,1,0:T(8,128)}, bf16[3,256,768]{2,1,0:T(8,128)(2,1)}, bf16[3,256,768]{2,1,0:T(8,128)(2,1)}, bf16[3,256,768]{2,1,0:T(8,128)(2,1)}) custom-call(bf16[128,2304]{1,0:T(8,128)(2,1)} %shard_map.121.refs_0_, bf16[128,2304]{1,0:T(8,128)(2,1)} %copy-done.32, bf16[128,2304]{1,0:T(8,128)(2,1)} %copy-done.31, ...), custom_call_target="tpu_custom_call" | custom-call | flops 2415919104 | bytes 10354688 | tf_op jit(solution)/shard_map/pallas_call | solution.py:63
  132.5 1.7 collective-permute-start.29
  134.9 1.3 collective-permute-done.20.refs_2_
  136.2 5.4 %collective-permute-done.21.refs_3_ = bf16[2,128,1024]{2,1,0:T(8,128)(2,1)S(1)} collective-permute-done((bf16[2,128,1024]{2,1,0:T(8,128)(2,1)}, bf16[2,128,1024]{2,1,0:T(8,128)(2,1)S(1)}, u32[]{:S(2)}, u32[]{:S(2)}) %collective-permute-start.21) | collective-permute-done | bytes 524320 | tf_op jit(solution)/shard_map/ppermute | solution.py:38
  141.6 0.8 copy-done.8
  142.3 2.9 %shard_map.123 = (bf16[2,4,16,1024]{3,2,1,0:T(8,128)(2,1)}, bf16[2,4,16,1024]{3,2,1,0:T(8,128)(2,1)}, bf16[2,4,16,1024]{3,2,1,0:T(8,128)(2,1)}, bf16[2,4,16,1024...) custom-call(bf16[2,128,1024]{2,1,0:T(8,128)(2,1)} %get-tuple-element, ...), custom_call_target="tpu_custom_call" | custom-call | bytes 4194304 | tf_op jit(solution)/shard_map/pallas_call | solution.py:63
  145.2 1.0 collective-permute-start.22
  146.2 2.1 collective-permute-start.23
  148.4 2.6 %collective-permute-done.22.refs_1_ = bf16[2,4,16,1024]{3,2,1,0:T(8,128)(2,1)S(1)} collective-permute-done((bf16[2,4,16,1024]{3,2,1,0:T(8,128)(2,1)}, bf16[2,4,16,1024]{3,2,1,0:T(8,128)(2,1)S(1)}, u32[]{:S(2)}, u32[]{:S(2)}) %collective-permute-start.22) | collective-permute-done | bytes 262176 | tf_op jit(solution)/shard_map/ppermute | solution.py:44
  150.9 4.2 %collective-permute-start.24 = (bf16[2,4,16,1024]{3,2,1,0:T(8,128)(2,1)}, bf16[2,4,16,1024]{3,2,1,0:T(8,128)(2,1)S(1)}, u32[]{:S(2)}, u32[]{:S(2)}) collective-permute-start(bf16[2,4,16,1024]{3,2,1,0:T(8,128)(2,1)} %get-tuple-element.67), channel_id=1, source_target_pairs={{0,2},{1,3},{2,4},{3,5},{4,6},{5,7},{6,0},{7,1},{8,10},{9,11},{10,... | collective-permute-start | bytes 786440 | tf_op jit(solution)/shard_map/ppermute | solution.py:44
  155.1 24.4 %collective-permute-start.25 = (bf16[2,4,16,1024]{3,2,1,0:T(8,128)(2,1)}, bf16[2,4,16,1024]{3,2,1,0:T(8,128)(2,1)S(1)}, u32[]{:S(2)}, u32[]{:S(2)}) collective-permute-start(bf16[2,4,16,1024]{3,2,1,0:T(8,128)(2,1)} %get-tuple-element.68), channel_id=1, source_target_pairs={{0,1},{1,0},{2,3},{3,2},{4,5},{5,4},{6,7},{7,6},{8,9},{9,8},{10,11... | collective-permute-start | bytes 786440 | tf_op jit(solution)/shard_map/ppermute | solution.py:44
  179.5 7.2 %collective-permute-start.26 = (bf16[2,4,16,1024]{3,2,1,0:T(8,128)(2,1)}, bf16[2,4,16,1024]{3,2,1,0:T(8,128)(2,1)S(1)}, u32[]{:S(2)}, u32[]{:S(2)}) collective-permute-start(bf16[2,4,16,1024]{3,2,1,0:T(8,128)(2,1)} %get-tuple-element.69), channel_id=1, source_target_pairs={{0,7},{1,6},{2,1},{3,0},{4,3},{5,2},{6,5},{7,4},{8,15},{9,14},{10,... | collective-permute-start | bytes 786440 | tf_op jit(solution)/shard_map/ppermute | solution.py:44
  186.7 6.0 %collective-permute-done.26.refs_5_ = bf16[2,4,16,1024]{3,2,1,0:T(8,128)(2,1)S(1)} collective-permute-done((bf16[2,4,16,1024]{3,2,1,0:T(8,128)(2,1)}, bf16[2,4,16,1024]{3,2,1,0:T(8,128)(2,1)S(1)}, u32[]{:S(2)}, u32[]{:S(2)}) %collective-permute-start.26) | collective-permute-done | bytes 262176 | tf_op jit(solution)/shard_map/ppermute | solution.py:44
  193.1 1.7 collective-permute-done.27.refs_6_
  194.8 8.0 %collective-permute-done.28.refs_7_ = bf16[2,4,16,1024]{3,2,1,0:T(8,128)(2,1)S(1)} collective-permute-done((bf16[2,4,16,1024]{3,2,1,0:T(8,128)(2,1)}, bf16[2,4,16,1024]{3,2,1,0:T(8,128)(2,1)S(1)}, u32[]{:S(2)}, u32[]{:S(2)}) %collective-permute-start.28) | collective-permute-done | bytes 262176 | tf_op jit(solution)/shard_map/ppermute | solution.py:44
  202.8 0.7 copy-done.25
  203.5 4.7 %shard_map.124 = (bf16[128,4096]{1,0:T(8,128)(2,1)}, bf16[128,4096]{1,0:T(8,128)(2,1)}, f32[8,128]{1,0:T(8,128)}) custom-call(s32[4]{0:T(128)} %pad_add_fusion.place, s32[8,128]{1,0:T(8,128)} %bitcast.8, f32[8,128]{1,0:T(8,128)} %bitcast.10, bf16[128,4096]{1,0:T(8,128)(2,1)} %cotangent.3, bf16[2,4,16,1024]{3,2,1,0:T(8,128)(2,1)} %get-tuple-element.64.refs_0_, ...), custom_call_target="tpu_custom_call" | custom-call | flops 536870912 | bytes 5255168 | tf_op jit(solution)/shard_map/pallas_call | solution.py:63
  208.2 1.0 copy-done
  210.0 4.2 %shard_map.126 = (f32[1,256,768]{2,1,0:T(8,128)}, f32[1,256,768]{2,1,0:T(8,128)}, f32[1,256,768]{2,1,0:T(8,128)}) custom-call(f32[3,256,768]{2,1,0:T(8,128)} %get-tuple-element.75.own, bf16[3,256,768]{2,1,0:T(8,128)(2,1)} %copy-done, bf16[3,256,768]{2,1,0:T(8,128)(2,1)} %copy-done.1, bf16[3,256,768]{2,1,0:T(8,128)(2,1)} %copy-done.2), custom_call_target="tpu_custom_call" | custom-call | bytes 8257536 | tf_op jit(solution)/shard_map/pallas_call | solution.py:63
  (101 shorter events, 8.5 us)
Async XLA Ops:
  0.6 13.0 %copy-start.9 = (bf16[1,256,768]{2,1,0:T(8,128)(2,1)S(1)}, bf16[1,256,768]{2,1,0:T(8,128)(2,1)}, u32[]{:S(2)}) copy-start(bf16[1,256,768]{2,1,0:T(8,128)(2,1)} %param.11) | copy-start | bytes 1179652
  1.3 23.8 %copy-start.10 = (bf16[1,256,768]{2,1,0:T(8,128)(2,1)S(1)}, bf16[1,256,768]{2,1,0:T(8,128)(2,1)}, u32[]{:S(2)}) copy-start(bf16[1,256,768]{2,1,0:T(8,128)(2,1)} %param.12) | copy-start | bytes 1179652
  5.0 20.1 %copy-start.11 = (bf16[1,256,768]{2,1,0:T(8,128)(2,1)S(1)}, bf16[1,256,768]{2,1,0:T(8,128)(2,1)}, u32[]{:S(2)}) copy-start(bf16[1,256,768]{2,1,0:T(8,128)(2,1)} %param.13) | copy-start | bytes 1179652
  5.0 10.9 %collective-permute-start = (bf16[2,4,16,1024]{3,2,1,0:T(8,128)(2,1)}, bf16[2,4,16,1024]{3,2,1,0:T(8,128)(2,1)S(1)}, u32[]{:S(2)}, u32[]{:S(2)}) collective-permute-start(bf16[2,4,16,1024]{3,2,1,0:T(8,128)(2,1)} %get-tuple-element.45), channel_id=1, source_target_pairs={{0,2},{1,3},{2,4},{3,5},{4,6},{5,7},{6,0},{7,1},{8,10},{9,11},{10,... | collective-permute-start | bytes 786440 | tf_op jit(solution)/shard_map/ppermute | solution.py:44
  7.5 17.5 %collective-permute-start.1 = (bf16[2,4,16,1024]{3,2,1,0:T(8,128)(2,1)}, bf16[2,4,16,1024]{3,2,1,0:T(8,128)(2,1)S(1)}, u32[]{:S(2)}, u32[]{:S(2)}) collective-permute-start(bf16[2,4,16,1024]{3,2,1,0:T(8,128)(2,1)} %get-tuple-element.46), channel_id=1, source_target_pairs={{0,4},{1,5},{2,6},{3,7},{4,0},{5,1},{6,2},{7,3},{8,12},{9,13},{10,... | collective-permute-start | bytes 786440 | tf_op jit(solution)/shard_map/ppermute | solution.py:44
  10.8 14.3 %collective-permute-start.2 = (bf16[2,4,16,1024]{3,2,1,0:T(8,128)(2,1)}, bf16[2,4,16,1024]{3,2,1,0:T(8,128)(2,1)S(1)}, u32[]{:S(2)}, u32[]{:S(2)}) collective-permute-start(bf16[2,4,16,1024]{3,2,1,0:T(8,128)(2,1)} %get-tuple-element.47), channel_id=1, source_target_pairs={{0,6},{1,7},{2,0},{3,1},{4,2},{5,3},{6,4},{7,5},{8,14},{9,15},{10,... | collective-permute-start | bytes 786440 | tf_op jit(solution)/shard_map/ppermute | solution.py:44
  11.5 16.5 %collective-permute-start.3 = (bf16[2,4,16,1024]{3,2,1,0:T(8,128)(2,1)}, bf16[2,4,16,1024]{3,2,1,0:T(8,128)(2,1)S(1)}, u32[]{:S(2)}, u32[]{:S(2)}) collective-permute-start(bf16[2,4,16,1024]{3,2,1,0:T(8,128)(2,1)} %get-tuple-element.48), channel_id=1, source_target_pairs={{0,1},{1,0},{2,3},{3,2},{4,5},{5,4},{6,7},{7,6},{8,9},{9,8},{10,11... | collective-permute-start | bytes 786440 | tf_op jit(solution)/shard_map/ppermute | solution.py:44
  13.0 15.3 %collective-permute-start.4 = (bf16[2,4,16,1024]{3,2,1,0:T(8,128)(2,1)}, bf16[2,4,16,1024]{3,2,1,0:T(8,128)(2,1)S(1)}, u32[]{:S(2)}, u32[]{:S(2)}) collective-permute-start(bf16[2,4,16,1024]{3,2,1,0:T(8,128)(2,1)} %get-tuple-element.49), channel_id=1, source_target_pairs={{0,3},{1,2},{2,5},{3,4},{4,7},{5,6},{6,1},{7,0},{8,11},{9,10},{10,... | collective-permute-start | bytes 786440 | tf_op jit(solution)/shard_map/ppermute | solution.py:44
  15.9 18.9 %copy-start.12 = (bf16[2,4,16,1024]{3,2,1,0:T(8,128)(2,1)}, bf16[2,4,16,1024]{3,2,1,0:T(8,128)(2,1)S(1)}, u32[]{:S(2)}) copy-start(bf16[2,4,16,1024]{3,2,1,0:T(8,128)(2,1)S(1)} %collective-permute-done.refs_1_) | copy-start | bytes 786436
  15.9 18.9 %collective-permute-start.5 = (bf16[2,4,16,1024]{3,2,1,0:T(8,128)(2,1)}, bf16[2,4,16,1024]{3,2,1,0:T(8,128)(2,1)S(1)}, u32[]{:S(2)}, u32[]{:S(2)}) collective-permute-start(bf16[2,4,16,1024]{3,2,1,0:T(8,128)(2,1)} %get-tuple-element.50), channel_id=1, source_target_pairs={{0,5},{1,4},{2,7},{3,6},{4,1},{5,0},{6,3},{7,2},{8,13},{9,12},{10,... | collective-permute-start | bytes 786440 | tf_op jit(solution)/shard_map/ppermute | solution.py:44
  25.0 9.8 %copy-start.13 = (bf16[2,4,16,1024]{3,2,1,0:T(8,128)(2,1)}, bf16[2,4,16,1024]{3,2,1,0:T(8,128)(2,1)S(1)}, u32[]{:S(2)}) copy-start(bf16[2,4,16,1024]{3,2,1,0:T(8,128)(2,1)S(1)} %collective-permute-done.1.refs_2_) | copy-start | bytes 786436
  25.0 9.7 %collective-permute-start.6 = (bf16[2,4,16,1024]{3,2,1,0:T(8,128)(2,1)}, bf16[2,4,16,1024]{3,2,1,0:T(8,128)(2,1)S(1)}, u32[]{:S(2)}, u32[]{:S(2)}) collective-permute-start(bf16[2,4,16,1024]{3,2,1,0:T(8,128)(2,1)} %get-tuple-element.51), channel_id=1, source_target_pairs={{0,7},{1,6},{2,1},{3,0},{4,3},{5,2},{6,5},{7,4},{8,15},{9,14},{10,... | collective-permute-start | bytes 786440 | tf_op jit(solution)/shard_map/ppermute | solution.py:44
  25.1 43.6 %copy-start.26 = (bf16[3,256,768]{2,1,0:T(8,128)(2,1)}, bf16[3,256,768]{2,1,0:T(8,128)(2,1)S(1)}, u32[]{:S(2)}) copy-start(bf16[3,256,768]{2,1,0:T(8,128)(2,1)S(1)} %constant_dynamic-update-slice_fusion.refs_4_) | copy-start | bytes 3538948
  25.2 9.6 %copy-start.14 = (bf16[2,4,16,1024]{3,2,1,0:T(8,128)(2,1)}, bf16[2,4,16,1024]{3,2,1,0:T(8,128)(2,1)S(1)}, u32[]{:S(2)}) copy-start(bf16[2,4,16,1024]{3,2,1,0:T(8,128)(2,1)S(1)} %collective-permute-done.2.refs_3_) | copy-start | bytes 786436
  25.2 42.5 %collective-permute-start.12 = (bf16[3,256,768]{2,1,0:T(8,128)(2,1)S(1)}, bf16[3,256,768]{2,1,0:T(8,128)(2,1)S(1)}, u32[]{:S(2)}, u32[]{:S(2)}) collective-permute-start(bf16[3,256,768]{2,1,0:T(8,128)(2,1)S(1)} %constant_dynamic-update-slice_fusion.refs_4_), channel_id=1, source_target_pairs={{0,24},{1,97},{2,26},{3,99},{4,28},{5,101},{6,30},{7,103},{8,0},{9... | collective-permute-start | bytes 3538952 | tf_op jit(solution)/shard_map/ppermute | solution.py:32
  28.0 39.7 %collective-permute-start.11 = (bf16[3,256,768]{2,1,0:T(8,128)(2,1)S(1)}, bf16[3,256,768]{2,1,0:T(8,128)(2,1)S(1)}, u32[]{:S(2)}, u32[]{:S(2)}) collective-permute-start(bf16[3,256,768]{2,1,0:T(8,128)(2,1)S(1)} %constant_dynamic-update-slice_fusion.refs_4_), channel_id=1, source_target_pairs={{0,16},{1,65},{2,18},{3,67},{4,20},{5,69},{6,22},{7,71},{8,24},{9,... | collective-permute-start | bytes 3538952 | tf_op jit(solution)/shard_map/ppermute | solution.py:32
  28.3 40.4 %collective-permute-start.10 = (bf16[3,256,768]{2,1,0:T(8,128)(2,1)S(1)}, bf16[3,256,768]{2,1,0:T(8,128)(2,1)S(1)}, u32[]{:S(2)}, u32[]{:S(2)}) collective-permute-start(bf16[3,256,768]{2,1,0:T(8,128)(2,1)S(1)} %constant_dynamic-update-slice_fusion.refs_4_), channel_id=1, source_target_pairs={{0,8},{1,33},{2,10},{3,35},{4,12},{5,37},{6,14},{7,39},{8,16},{9,4... | collective-permute-start | bytes 3538952 | tf_op jit(solution)/shard_map/ppermute | solution.py:32
  38.4 20.7 %collective-permute-start.7 = (bf16[2,128,1024]{2,1,0:T(8,128)(2,1)}, bf16[2,128,1024]{2,1,0:T(8,128)(2,1)S(1)}, u32[]{:S(2)}, u32[]{:S(2)}) collective-permute-start(bf16[2,128,1024]{2,1,0:T(8,128)(2,1)} %get-tuple-element.53), channel_id=1, source_target_pairs={{0,32},{1,9},{2,34},{3,11},{4,36},{5,13},{6,38},{7,15},{8,40},{9,1... | collective-permute-start | bytes 1572872 | tf_op jit(solution)/shard_map/ppermute | solution.py:38
  39.3 26.4 %collective-permute-start.8 = (bf16[2,128,1024]{2,1,0:T(8,128)(2,1)}, bf16[2,128,1024]{2,1,0:T(8,128)(2,1)S(1)}, u32[]{:S(2)}, u32[]{:S(2)}) collective-permute-start(bf16[2,128,1024]{2,1,0:T(8,128)(2,1)} %get-tuple-element.54), channel_id=1, source_target_pairs={{0,64},{1,17},{2,66},{3,19},{4,68},{5,21},{6,70},{7,23},{8,72},{9,... | collective-permute-start | bytes 1572872 | tf_op jit(solution)/shard_map/ppermute | solution.py:38
  59.2 9.5 %copy-start.33 = (bf16[2,128,1024]{2,1,0:T(8,128)(2,1)}, bf16[2,128,1024]{2,1,0:T(8,128)(2,1)S(1)}, u32[]{:S(2)}) copy-start(bf16[2,128,1024]{2,1,0:T(8,128)(2,1)S(1)} %collective-permute-done.7.refs_1_.refs_5_) | copy-start | bytes 1572868
  59.2 8.5 %collective-permute-start.9 = (bf16[2,128,1024]{2,1,0:T(8,128)(2,1)}, bf16[2,128,1024]{2,1,0:T(8,128)(2,1)S(1)}, u32[]{:S(2)}, u32[]{:S(2)}) collective-permute-start(bf16[2,128,1024]{2,1,0:T(8,128)(2,1)} %get-tuple-element.55), channel_id=1, source_target_pairs={{0,96},{1,25},{2,98},{3,27},{4,100},{5,29},{6,102},{7,31},{8,104},... | collective-permute-start | bytes 1572872 | tf_op jit(solution)/shard_map/ppermute | solution.py:38
  76.8 15.7 %collective-permute-start.13 = (bf16[128,2304]{1,0:T(8,128)(2,1)}, bf16[128,2304]{1,0:T(8,128)(2,1)S(1)}, u32[]{:S(2)}, u32[]{:S(2)}) collective-permute-start(bf16[128,2304]{1,0:T(8,128)(2,1)} %get-tuple-element.57), channel_id=1, source_target_pairs={{0,96},{1,25},{2,98},{3,27},{4,100},{5,29},{6,102},{7,31},{8,104},... | collective-permute-start | bytes 1769480 | tf_op jit(solution)/shard_map/ppermute | solution.py:38
  79.0 13.5 %collective-permute-start.14 = (bf16[128,2304]{1,0:T(8,128)(2,1)}, bf16[128,2304]{1,0:T(8,128)(2,1)S(1)}, u32[]{:S(2)}, u32[]{:S(2)}) collective-permute-start(bf16[128,2304]{1,0:T(8,128)(2,1)} %get-tuple-element.58), channel_id=1, source_target_pairs={{0,64},{1,17},{2,66},{3,19},{4,68},{5,21},{6,70},{7,23},{8,72},{9,... | collective-permute-start | bytes 1769480 | tf_op jit(solution)/shard_map/ppermute | solution.py:38
  79.5 16.5 %collective-permute-start.15 = (bf16[128,2304]{1,0:T(8,128)(2,1)}, bf16[128,2304]{1,0:T(8,128)(2,1)S(1)}, u32[]{:S(2)}, u32[]{:S(2)}) collective-permute-start(bf16[128,2304]{1,0:T(8,128)(2,1)} %get-tuple-element.59), channel_id=1, source_target_pairs={{0,32},{1,9},{2,34},{3,11},{4,36},{5,13},{6,38},{7,15},{8,40},{9,1... | collective-permute-start | bytes 1769480 | tf_op jit(solution)/shard_map/ppermute | solution.py:38
  99.9 9.2 %collective-permute-start.18 = (bf16[128,2304]{1,0:T(8,128)(2,1)}, bf16[128,2304]{1,0:T(8,128)(2,1)S(1)}, u32[]{:S(2)}, u32[]{:S(2)}) collective-permute-start(bf16[128,2304]{1,0:T(8,128)(2,1)} %shard_map.121.refs_0_), channel_id=1, source_target_pairs={{0,96},{1,25},{2,98},{3,27},{4,100},{5,29},{6,102},{7,31},{8,104},... | collective-permute-start | bytes 1769480 | tf_op jit(solution)/shard_map/ppermute | solution.py:38
  100.2 10.8 %collective-permute-start.17 = (bf16[128,2304]{1,0:T(8,128)(2,1)}, bf16[128,2304]{1,0:T(8,128)(2,1)S(1)}, u32[]{:S(2)}, u32[]{:S(2)}) collective-permute-start(bf16[128,2304]{1,0:T(8,128)(2,1)} %shard_map.121.refs_0_), channel_id=1, source_target_pairs={{0,64},{1,17},{2,66},{3,19},{4,68},{5,21},{6,70},{7,23},{8,72},{9,... | collective-permute-start | bytes 1769480 | tf_op jit(solution)/shard_map/ppermute | solution.py:38
  100.7 16.5 %collective-permute-start.16 = (bf16[128,2304]{1,0:T(8,128)(2,1)}, bf16[128,2304]{1,0:T(8,128)(2,1)S(1)}, u32[]{:S(2)}, u32[]{:S(2)}) collective-permute-start(bf16[128,2304]{1,0:T(8,128)(2,1)} %shard_map.121.refs_0_), channel_id=1, source_target_pairs={{0,32},{1,9},{2,34},{3,11},{4,36},{5,13},{6,38},{7,15},{8,40},{9,1... | collective-permute-start | bytes 1769480 | tf_op jit(solution)/shard_map/ppermute | solution.py:38
  109.1 8.2 %copy-start.30 = (bf16[128,2304]{1,0:T(8,128)(2,1)}, bf16[128,2304]{1,0:T(8,128)(2,1)S(1)}, u32[]{:S(2)}) copy-start(bf16[128,2304]{1,0:T(8,128)(2,1)S(1)} %collective-permute-done.18.refs_3_) | copy-start | bytes 1769476
  125.0 9.3 %collective-permute-start.19 = (bf16[2,128,1024]{2,1,0:T(8,128)(2,1)}, bf16[2,128,1024]{2,1,0:T(8,128)(2,1)S(1)}, u32[]{:S(2)}, u32[]{:S(2)}) collective-permute-start(bf16[2,128,1024]{2,1,0:T(8,128)(2,1)} %get-tuple-element.61), channel_id=1, source_target_pairs={{0,96},{1,25},{2,98},{3,27},{4,100},{5,29},{6,102},{7,31},{8,104},... | collective-permute-start | bytes 1572872 | tf_op jit(solution)/shard_map/ppermute | solution.py:38
  126.1 10.1 %collective-permute-start.20 = (bf16[2,128,1024]{2,1,0:T(8,128)(2,1)}, bf16[2,128,1024]{2,1,0:T(8,128)(2,1)S(1)}, u32[]{:S(2)}, u32[]{:S(2)}) collective-permute-start(bf16[2,128,1024]{2,1,0:T(8,128)(2,1)} %get-tuple-element.62), channel_id=1, source_target_pairs={{0,64},{1,17},{2,66},{3,19},{4,68},{5,21},{6,70},{7,23},{8,72},{9,... | collective-permute-start | bytes 1572872 | tf_op jit(solution)/shard_map/ppermute | solution.py:38
  126.1 15.5 %collective-permute-start.21 = (bf16[2,128,1024]{2,1,0:T(8,128)(2,1)}, bf16[2,128,1024]{2,1,0:T(8,128)(2,1)S(1)}, u32[]{:S(2)}, u32[]{:S(2)}) collective-permute-start(bf16[2,128,1024]{2,1,0:T(8,128)(2,1)} %get-tuple-element.63), channel_id=1, source_target_pairs={{0,32},{1,9},{2,34},{3,11},{4,36},{5,13},{6,38},{7,15},{8,40},{9,1... | collective-permute-start | bytes 1572872 | tf_op jit(solution)/shard_map/ppermute | solution.py:38
  132.5 75.7 %collective-permute-start.29 = (bf16[3,256,768]{2,1,0:T(8,128)(2,1)}, bf16[3,256,768]{2,1,0:T(8,128)(2,1)S(1)}, u32[]{:S(2)}, u32[]{:S(2)}) collective-permute-start(bf16[3,256,768]{2,1,0:T(8,128)(2,1)} %get-tuple-element.76), channel_id=1, source_target_pairs={{0,24},{1,97},{2,26},{3,99},{4,28},{5,101},{6,30},{7,103},{8,0},{9... | collective-permute-start | bytes 3538952 | tf_op jit(solution)/shard_map/ppermute | solution.py:32
  134.3 73.9 %collective-permute-start.30 = (bf16[3,256,768]{2,1,0:T(8,128)(2,1)}, bf16[3,256,768]{2,1,0:T(8,128)(2,1)S(1)}, u32[]{:S(2)}, u32[]{:S(2)}) collective-permute-start(bf16[3,256,768]{2,1,0:T(8,128)(2,1)} %get-tuple-element.77), channel_id=1, source_target_pairs={{0,16},{1,65},{2,18},{3,67},{4,20},{5,69},{6,22},{7,71},{8,24},{9,... | collective-permute-start | bytes 3538952 | tf_op jit(solution)/shard_map/ppermute | solution.py:32
  134.3 7.3 %copy-start.6 = (bf16[2,128,1024]{2,1,0:T(8,128)(2,1)}, bf16[2,128,1024]{2,1,0:T(8,128)(2,1)S(1)}, u32[]{:S(2)}) copy-start(bf16[2,128,1024]{2,1,0:T(8,128)(2,1)S(1)} %collective-permute-done.19.refs_1_) | copy-start | bytes 1572868
  134.3 73.9 %collective-permute-start.31 = (bf16[3,256,768]{2,1,0:T(8,128)(2,1)}, bf16[3,256,768]{2,1,0:T(8,128)(2,1)S(1)}, u32[]{:S(2)}, u32[]{:S(2)}) collective-permute-start(bf16[3,256,768]{2,1,0:T(8,128)(2,1)} %get-tuple-element.78), channel_id=1, source_target_pairs={{0,8},{1,33},{2,10},{3,35},{4,12},{5,37},{6,14},{7,39},{8,16},{9,4... | collective-permute-start | bytes 3538952 | tf_op jit(solution)/shard_map/ppermute | solution.py:32
  145.2 5.7 %collective-permute-start.22 = (bf16[2,4,16,1024]{3,2,1,0:T(8,128)(2,1)}, bf16[2,4,16,1024]{3,2,1,0:T(8,128)(2,1)S(1)}, u32[]{:S(2)}, u32[]{:S(2)}) collective-permute-start(bf16[2,4,16,1024]{3,2,1,0:T(8,128)(2,1)} %get-tuple-element.65), channel_id=1, source_target_pairs={{0,6},{1,7},{2,0},{3,1},{4,2},{5,3},{6,4},{7,5},{8,14},{9,15},{10,... | collective-permute-start | bytes 786440 | tf_op jit(solution)/shard_map/ppermute | solution.py:44
  146.2 8.9 %collective-permute-start.23 = (bf16[2,4,16,1024]{3,2,1,0:T(8,128)(2,1)}, bf16[2,4,16,1024]{3,2,1,0:T(8,128)(2,1)S(1)}, u32[]{:S(2)}, u32[]{:S(2)}) collective-permute-start(bf16[2,4,16,1024]{3,2,1,0:T(8,128)(2,1)} %get-tuple-element.66), channel_id=1, source_target_pairs={{0,4},{1,5},{2,6},{3,7},{4,0},{5,1},{6,2},{7,3},{8,12},{9,13},{10,... | collective-permute-start | bytes 786440 | tf_op jit(solution)/shard_map/ppermute | solution.py:44
  150.9 51.9 %copy-start.17 = (bf16[2,4,16,1024]{3,2,1,0:T(8,128)(2,1)}, bf16[2,4,16,1024]{3,2,1,0:T(8,128)(2,1)S(1)}, u32[]{:S(2)}) copy-start(bf16[2,4,16,1024]{3,2,1,0:T(8,128)(2,1)S(1)} %collective-permute-done.22.refs_1_) | copy-start | bytes 786436
  150.9 28.6 %collective-permute-start.24 = (bf16[2,4,16,1024]{3,2,1,0:T(8,128)(2,1)}, bf16[2,4,16,1024]{3,2,1,0:T(8,128)(2,1)S(1)}, u32[]{:S(2)}, u32[]{:S(2)}) collective-permute-start(bf16[2,4,16,1024]{3,2,1,0:T(8,128)(2,1)} %get-tuple-element.67), channel_id=1, source_target_pairs={{0,2},{1,3},{2,4},{3,5},{4,6},{5,7},{6,0},{7,1},{8,10},{9,11},{10,... | collective-permute-start | bytes 786440 | tf_op jit(solution)/shard_map/ppermute | solution.py:44
  155.1 47.7 %copy-start.19 = (bf16[2,4,16,1024]{3,2,1,0:T(8,128)(2,1)}, bf16[2,4,16,1024]{3,2,1,0:T(8,128)(2,1)S(1)}, u32[]{:S(2)}) copy-start(bf16[2,4,16,1024]{3,2,1,0:T(8,128)(2,1)S(1)} %collective-permute-done.23.refs_2_) | copy-start | bytes 786436
  155.1 31.6 %collective-permute-start.25 = (bf16[2,4,16,1024]{3,2,1,0:T(8,128)(2,1)}, bf16[2,4,16,1024]{3,2,1,0:T(8,128)(2,1)S(1)}, u32[]{:S(2)}, u32[]{:S(2)}) collective-permute-start(bf16[2,4,16,1024]{3,2,1,0:T(8,128)(2,1)} %get-tuple-element.68), channel_id=1, source_target_pairs={{0,1},{1,0},{2,3},{3,2},{4,5},{5,4},{6,7},{7,6},{8,9},{9,8},{10,11... | collective-permute-start | bytes 786440 | tf_op jit(solution)/shard_map/ppermute | solution.py:44
  179.5 23.3 %copy-start.21 = (bf16[2,4,16,1024]{3,2,1,0:T(8,128)(2,1)}, bf16[2,4,16,1024]{3,2,1,0:T(8,128)(2,1)S(1)}, u32[]{:S(2)}) copy-start(bf16[2,4,16,1024]{3,2,1,0:T(8,128)(2,1)S(1)} %collective-permute-done.24.refs_3_) | copy-start | bytes 786436
  179.5 13.2 %collective-permute-start.26 = (bf16[2,4,16,1024]{3,2,1,0:T(8,128)(2,1)}, bf16[2,4,16,1024]{3,2,1,0:T(8,128)(2,1)S(1)}, u32[]{:S(2)}, u32[]{:S(2)}) collective-permute-start(bf16[2,4,16,1024]{3,2,1,0:T(8,128)(2,1)} %get-tuple-element.69), channel_id=1, source_target_pairs={{0,7},{1,6},{2,1},{3,0},{4,3},{5,2},{6,5},{7,4},{8,15},{9,14},{10,... | collective-permute-start | bytes 786440 | tf_op jit(solution)/shard_map/ppermute | solution.py:44
  186.7 16.1 %copy-start.22 = (bf16[2,4,16,1024]{3,2,1,0:T(8,128)(2,1)}, bf16[2,4,16,1024]{3,2,1,0:T(8,128)(2,1)S(1)}, u32[]{:S(2)}) copy-start(bf16[2,4,16,1024]{3,2,1,0:T(8,128)(2,1)S(1)} %collective-permute-done.25.refs_4_) | copy-start | bytes 786436
  186.7 8.1 %collective-permute-start.27 = (bf16[2,4,16,1024]{3,2,1,0:T(8,128)(2,1)}, bf16[2,4,16,1024]{3,2,1,0:T(8,128)(2,1)S(1)}, u32[]{:S(2)}, u32[]{:S(2)}) collective-permute-start(bf16[2,4,16,1024]{3,2,1,0:T(8,128)(2,1)} %get-tuple-element.70), channel_id=1, source_target_pairs={{0,5},{1,4},{2,7},{3,6},{4,1},{5,0},{6,3},{7,2},{8,13},{9,12},{10,... | collective-permute-start | bytes 786440 | tf_op jit(solution)/shard_map/ppermute | solution.py:44
  192.7 10.1 %copy-start.23 = (bf16[2,4,16,1024]{3,2,1,0:T(8,128)(2,1)}, bf16[2,4,16,1024]{3,2,1,0:T(8,128)(2,1)S(1)}, u32[]{:S(2)}) copy-start(bf16[2,4,16,1024]{3,2,1,0:T(8,128)(2,1)S(1)} %collective-permute-done.26.refs_5_) | copy-start | bytes 786436
  192.7 10.0 %collective-permute-start.28 = (bf16[2,4,16,1024]{3,2,1,0:T(8,128)(2,1)}, bf16[2,4,16,1024]{3,2,1,0:T(8,128)(2,1)S(1)}, u32[]{:S(2)}, u32[]{:S(2)}) collective-permute-start(bf16[2,4,16,1024]{3,2,1,0:T(8,128)(2,1)} %get-tuple-element.71), channel_id=1, source_target_pairs={{0,3},{1,2},{2,5},{3,4},{4,7},{5,6},{6,1},{7,0},{8,11},{9,10},{10,... | collective-permute-start | bytes 786440 | tf_op jit(solution)/shard_map/ppermute | solution.py:44
  194.8 8.0 %copy-start.24 = (bf16[2,4,16,1024]{3,2,1,0:T(8,128)(2,1)}, bf16[2,4,16,1024]{3,2,1,0:T(8,128)(2,1)S(1)}, u32[]{:S(2)}) copy-start(bf16[2,4,16,1024]{3,2,1,0:T(8,128)(2,1)S(1)} %collective-permute-done.27.refs_6_) | copy-start | bytes 786436
  (20 other events, 48.9 us)

commit v2 on v1

--- a/solution.py
+++ b/solution.py
@@ -28,10 +28,9 @@
     return pairs
 
 
-def shift_a(v, s):
-    return lax.ppermute(
-        v, AXES, _perm(lambda y, x, z, c: (y, x + s, z, c) if c == 0 else (y + s, x, z, c))
-    )
+def groups_a():
+    groups = [[_dev(y, x, z, 0) for x in range(4)] for y in range(4) for z in range(4)]
+    return groups + [[_dev(y, x, z, 1) for y in range(4)] for x in range(4) for z in range(4)]
 
 
 def shift_b(v, s):
@@ -102,9 +101,7 @@
     y, x, c = place[0], place[1], place[3]
     dy, dx = (yb - y + 4) & 3, (xb - x + 4) & 3
     flip = c ^ dc
-    sb = jnp.where(flip == 0, dy, dx)
-    sa = (4 - jnp.where(flip == 0, dx, dy)) & 3
-    return sb, sa
+    return jnp.where(flip == 0, dy, dx), jnp.where(flip == 0, xb, yb)
 
 
 def dispatch_kernel(place, ids, gates, tokens, cotangent, *outs):
@@ -124,9 +121,9 @@
 
 
 def to_b_kernel(*refs):
-    ins, outs = refs[:REL], refs[REL:]
+    ins, outs = refs[:SIDE], refs[SIDE:]
     for s in range(SIDE):
-        for r in range(REL):
+        for r in range(SIDE):
             for kind in range(2):
                 outs[s][kind, r * CAP : r * CAP + CAP, :] = ins[r][kind, s]
 
@@ -134,7 +131,7 @@
 def to_z_kernel(*refs):
     ins, outs = refs[:SIDE], refs[SIDE:]
     for s in range(SIDE):
-        for r in range(REL):
+        for r in range(SIDE):
             for kind in range(2):
                 outs[r][kind, s] = ins[s][kind, r * CAP : r * CAP + CAP, :]
 
@@ -143,15 +140,20 @@
     return jnp.concatenate([p[kind, :, cols] for p in pieces], axis=0)
 
 
+def thirds(pieces):
+    return [jnp.concatenate([p[:, k * FW : k * FW + FW] for p in pieces], axis=0) for k in range(3)]
+
+
 def partial_kernel(*refs):
-    xs, ws, own, outs = refs[:4], refs[4:8], refs[8], refs[9:]
+    xs, ws, own, outs = refs[:4], refs[4], refs[5], refs[6:]
     rows = xs[0].shape[1]
     for which in range(3):
         left = stacked(xs, 0 if which < 2 else 1)
         for n in range(FW // COLS):
             cols = slice(n * COLS, n * COLS + COLS)
             at = slice(which * FW + n * COLS, which * FW + n * COLS + COLS)
-            got = dot(left, stacked(ws, which, cols))
+            right = jnp.concatenate([ws[a, which, :, cols] for a in range(SIDE)], axis=0)
+            got = dot(left, right)
             own[:, at] = got[:rows]
             for p in range(1, SIDE):
                 outs[p - 1][:, at] = got[p * rows : p * rows + rows].astype(BF)
@@ -173,39 +175,26 @@
 
 
 def rows_kernel(*refs):
-    hs, ws, outs = refs[:4], refs[4:8], refs[8:]
+    hs, ws, outs = refs[:4], refs[4], refs[5:]
     rows = hs[0].shape[0]
-    hidden, ggate, gup = (
-        jnp.concatenate([h[:, k * FW : k * FW + FW] for h in hs], axis=0) for k in range(3)
-    )
+    hidden, ggate, gup = thirds(hs)
     for a in range(SIDE):
         cols = slice(a * COLS, a * COLS + COLS)
-        made = dot_last(hidden, ws[a][2]).astype(BF)
-        back = (dot_last(ggate, ws[a][0]) + dot_last(gup, ws[a][1])).astype(BF)
+        made = dot_last(hidden, ws[a, 2]).astype(BF)
+        back = (dot_last(ggate, ws[a, 0]) + dot_last(gup, ws[a, 1])).astype(BF)
         for p in range(SIDE):
             outs[p][0, :, cols] = made[p * rows : p * rows + rows]
             outs[p][1, :, cols] = back[p * rows : p * rows + rows]
 
 
 def weights_kernel(*refs):
-    hs, xs, own, outs = refs[:4], refs[4:8], refs[8], refs[9:]
-    hidden, ggate, gup = (
-        jnp.concatenate([h[:, k * FW : k * FW + FW] for h in hs], axis=0) for k in range(3)
-    )
+    hs, xs, out = refs[:8], refs[8:16], refs[16]
+    hidden, ggate, gup = thirds(hs)
     for a in range(SIDE):
         cols = slice(a * COLS, a * COLS + COLS)
         x, g = stacked(xs, 0, cols), stacked(xs, 1, cols)
         for k, (left, right) in enumerate(((x, ggate), (x, gup), (g, hidden))):
-            got = dot_first(left, right)
-            if a == 0:
-                own[k] = got
-            else:
-                outs[a - 1][k] = got.astype(BF)
-
-
-def total_kernel(own, p1, p2, p3, *outs):
-    for k in range(3):
-        outs[k][0] = (own[k] + p1[k].astype(F32)) + (p2[k].astype(F32) + p3[k].astype(F32))
+            out[a, k] = dot_first(left, right).astype(BF)
 
 
 def combine_kernel(place, ids, gates, cotangent, *refs):
@@ -243,9 +232,11 @@
     place = jnp.stack([dp // 4, dp % 4, ex // 2, ex % 2]).astype(jnp.int32)
     ids_t, gates_t = expert_ids.T, gates.T
     chunk = width // SIDE
+    rows = SIDE * CAP
+    work = 2 * SIDE * rows * chunk * 3 * FW
 
     held = jnp.concatenate([w_gate, w_up, w_down], axis=0)
-    ws = [held] + [shift_a(held, s) for s in (1, 2, 3)]
+    ws = lax.all_gather(held, AXES, axis_index_groups=groups_a())
 
     sends = call(
         dispatch_kernel,
@@ -255,37 +246,36 @@
         smem=1,
     )
     came = [sends[0]] + [shift_z(sends[r], r % 4, r // 4) for r in range(1, REL)]
-    turned = call(to_b_kernel, [shape((2, REL * CAP, chunk))] * SIDE, came, 0)
-    xs = [turned[0]] + [shift_b(turned[s], s) for s in (1, 2, 3)]
-
-    rows = REL * CAP
-    parts = call(
-        partial_kernel,
-        [shape((rows, 3 * FW), F32)] + [shape((rows, 3 * FW))] * 3,
-        (*xs, *ws),
-        2 * SIDE * rows * chunk * 3 * FW,
-    )
-    others = [shift_b(parts[s], -s) for s in (1, 2, 3)]
-    (mid,) = call(hidden_kernel, [shape((rows, 3 * FW))], (parts[0], *others), 0)
-    hs = [mid] + [shift_b(mid, s) for s in (1, 2, 3)]
-
-    outs = call(
-        rows_kernel,
-        [shape((2, rows, chunk))] * SIDE,
-        (*hs, *ws),
-        2 * SIDE * rows * chunk * 3 * FW,
-    )
-    home = [outs[0]] + [shift_b(outs[s], -s) for s in (1, 2, 3)]
-    grads = call(
-        weights_kernel,
-        [shape((3, COLS, FW), F32)] + [shape((3, COLS, FW))] * 3,
-        (*hs, *xs),
-        2 * SIDE * rows * chunk * 3 * FW,
-    )
-    others_w = [shift_a(grads[s], -s) for s in (1, 2, 3)]
-    split = call(to_z_kernel, [shape((2, SIDE, CAP, chunk))] * REL, home, 0)
-    backs = [split[0]] + [shift_z(split[r], -(r % 4), r // 4) for r in range(1, REL)]
-    gw = call(total_kernel, [shape((1, COLS, FW), F32)] * 3, (grads[0], *others_w), 0)
+    xs, hs, backs = [], [], []
+    for half in range(2):
+        turned = call(
+            to_b_kernel,
+            [shape((2, rows, chunk))] * SIDE,
+            came[half * SIDE : half * SIDE + SIDE],
+            0,
+        )
+        xs.append([turned[0]] + [shift_b(turned[s], s) for s in (1, 2, 3)])
+    for half in range(2):
+        parts = call(
+            partial_kernel,
+            [shape((rows, 3 * FW), F32)] + [shape((rows, 3 * FW))] * 3,
+            (*xs[half], ws),
+            work,
+        )
+        others = [shift_b(parts[s], -s) for s in (1, 2, 3)]
+        (mid,) = call(hidden_kernel, [shape((rows, 3 * FW))], (parts[0], *others), 0)
+        hs.append([mid] + [shift_b(mid, s) for s in (1, 2, 3)])
+    (grads,) = call(
+        weights_kernel, [shape((SIDE, 3, COLS, FW))], (*hs[0], *hs[1], *xs[0], *xs[1]), 2 * work
+    )
+    total = lax.psum_scatter(grads, AXES, axis_index_groups=groups_a()).astype(F32)
+    for half in range(2):
+        outs = call(rows_kernel, [shape((2, rows, chunk))] * SIDE, (*hs[half], ws), work)
+        home = [outs[0]] + [shift_b(outs[s], -s) for s in (1, 2, 3)]
+        split = call(to_z_kernel, [shape((2, SIDE, CAP, chunk))] * SIDE, home, 0)
+        backs += [
+            split[dz] if dz + half == 0 else shift_z(split[dz], -dz, half) for dz in range(SIDE)
+        ]
     mixed, gtok, gg_t = call(
         combine_kernel,
         [shape((tok, width)), shape((tok, width)), shape(ids_t.shape, F32)],
@@ -293,7 +283,7 @@
         8 * tok * tok * width,
         smem=1,
     )
-    return mixed, gtok, gg_t.T, *gw
+    return mixed, gtok, gg_t.T, total[:1], total[1:2], total[2:]
 
 
 def solution(mesh):

time: 215 us -> 175 us (0.81)
  waiting for transfers between devices: 91.1 us -> 42.4 us
  starting transfers between devices: 73.6 us -> 55 us
  between operations: 0.93 us -> 14.3 us
  Pallas kernels: 41.3 us -> 49 us
  other arithmetic: 0.59 us -> 4.53 us
  local copies, waits for them, and re-layouts: 6.81 us -> 9.5 us
    ppermute x12 -> x24, waiting for transfers between devices: 64.4 us -> 14.3 us  [shift_b(): lax.ppermute(v, AXES, _perm(lambda y, x, z, c: (y + s, x, z, c) if c == 0...]
    ppermute x14, starting transfers between devices: 57.1 us -> 28.8 us  [shift_z(): lax.ppermute(v, AXES, _perm(lambda y, x, z, c: (y, x, z + dz, c + dc)))]
    ppermute x12 -> x24, starting transfers between devices: 9.79 us -> 26.1 us  [shift_b(): lax.ppermute(v, AXES, _perm(lambda y, x, z, c: (y + s, x, z, c) if c == 0...]
    pallas_call x9 -> x13, Pallas kernels: 41.3 us -> 49 us  [call(): pl.pallas_call(kernel, out_shape=tuple(outs), in_specs=[sm] * smem + [vm]...]
    ppermute x6 -> x0, starting transfers between devices: 6.69 us -> none  [shift_a(): lax.ppermute(v, AXES, _perm(lambda y, x, z, c: (y, x + s, z, c) if c == 0...]
    concatenate x0 -> x1, other arithmetic: none -> 2.4 us  [per_device(): held = jnp.concatenate([w_gate, w_up, w_down], axis=0)]
    ppermute x14, waiting for transfers between devices: 25.7 us -> 28 us  [shift_z(): lax.ppermute(v, AXES, _perm(lambda y, x, z, c: (y, x, z + dz, c + dc)))]
    unnamed x74 -> x76, local copies, waits for them, and re-layouts: 6.78 us -> 8.05 us
  transfers between devices with their start and end apart: 32 -> 40, of which waited for: 17 -> 15; matrix products, arithmetic and copies ran while one was open for 0% -> 0% of each run, Pallas kernels for 8% -> 24%
where the time goes in v2:
time: 175 us
  starting transfers between devices  55 us (31%)
  Pallas kernels  49 us (28%)
  waiting for transfers between devices  42.4 us (24%)
  between operations  14.3 us (8%)
  local copies, waits for them, and re-layouts  9.5 us (5%)
  other arithmetic  4.53 us (3%)
    pallas_call x13, Pallas kernels, call(): pl.pallas_call(kernel, out_shape=tuple(outs), in_specs=[sm] * smem + [vm]...  49 us
    ppermute x14, starting transfers between devices, shift_z(): lax.ppermute(v, AXES, _perm(lambda y, x, z, c: (y, x, z + dz, c + dc)))  28.8 us
    ppermute x14, waiting for transfers between devices, shift_z(): lax.ppermute(v, AXES, _perm(lambda y, x, z, c: (y, x, z + dz, c + dc)))  28 us
    ppermute x24, starting transfers between devices, shift_b(): lax.ppermute(v, AXES, _perm(lambda y, x, z, c: (y + s, x, z, c) if c == 0...  26.1 us
    ppermute x24, waiting for transfers between devices, shift_b(): lax.ppermute(v, AXES, _perm(lambda y, x, z, c: (y + s, x, z, c) if c == 0...  14.3 us
    unnamed x76, local copies, waits for them, and re-layouts  8.05 us
  transfers between devices with their start and end apart: 40, of which 15 were waited for; matrix products, arithmetic and copies ran while one was open for 0% of the time, Pallas kernels for 24%

profile of v2, /device:TPU:1, one launch (start us, length us, event | category | flops | bytes accessed | tf_op | source)
XLA Modules:
  0.0 174.8 jit_solution(9697006898136697419)
XLA Ops:
  7.2 2.4 %pad_maximum_fusion = bf16[3,256,768]{2,1,0:T(8,128)(2,1)} fusion(bf16[1,256,768]{2,1,0:T(8,128)(2,1)} %param.13, bf16[1,256,768]{2,1,0:T(8,128)(2,1)} %param.12, bf16[1,256,768]{2,1,0:T(8,128)(2,1)} %param.11), kind=kLoop, calls=%fused_computation | loop fusion | flops 1179648 | bytes 2359296 | tf_op jit(solution)/shard_map/concatenate | solution.py:238
  10.4 3.7 %shard_map.118 = (bf16[2,4,16,1024]{3,2,1,0:T(8,128)(2,1)}, bf16[2,4,16,1024]{3,2,1,0:T(8,128)(2,1)}, bf16[2,4,16,1024]{3,2,1,0:T(8,128)(2,1)}, bf16[2,4,16,1024...) custom-call(s32[4]{0:T(128)} %pad_add_fusion.place, ...), custom_call_target="tpu_custom_call" | custom-call | flops 268435456 | bytes 4202496 | tf_op jit(solution)/shard_map/pallas_call | solution.py:62
  14.1 1.4 collective-permute-start.18
  15.5 1.6 collective-permute-start.19
  17.1 3.7 %collective-permute-start.20 = (bf16[2,4,16,1024]{3,2,1,0:T(8,128)(2,1)}, bf16[2,4,16,1024]{3,2,1,0:T(8,128)(2,1)S(1)}, u32[]{:S(2)}, u32[]{:S(2)}) collective-permute-start(bf16[2,4,16,1024]{3,2,1,0:T(8,128)(2,1)} %get-tuple-element.71), channel_id=1, source_target_pairs={{0,5},{1,4},{2,7},{3,6},{4,1},{5,0},{6,3},{7,2},{8,13},{9,12},{10,... | collective-permute-start | bytes 786440 | tf_op jit(solution)/shard_map/ppermute | solution.py:43
  22.7 3.6 %collective-permute-done.19.refs_1_ = bf16[2,4,16,1024]{3,2,1,0:T(8,128)(2,1)S(1)} collective-permute-done((bf16[2,4,16,1024]{3,2,1,0:T(8,128)(2,1)}, bf16[2,4,16,1024]{3,2,1,0:T(8,128)(2,1)S(1)}, u32[]{:S(2)}, u32[]{:S(2)}) %collective-permute-start.19) | collective-permute-done | bytes 262176 | tf_op jit(solution)/shard_map/ppermute | solution.py:43
  26.3 2.1 %collective-permute-start.2 = (bf16[2,4,16,1024]{3,2,1,0:T(8,128)(2,1)}, bf16[2,4,16,1024]{3,2,1,0:T(8,128)(2,1)S(1)}, u32[]{:S(2)}, u32[]{:S(2)}) collective-permute-start(bf16[2,4,16,1024]{3,2,1,0:T(8,128)(2,1)} %get-tuple-element.52), channel_id=1, source_target_pairs={{0,6},{1,7},{2,0},{3,1},{4,2},{5,3},{6,4},{7,5},{8,14},{9,15},{10,... | collective-permute-start | bytes 786440 | tf_op jit(solution)/shard_map/ppermute | solution.py:43
  28.4 5.1 %collective-permute-done.20.refs_2_ = bf16[2,4,16,1024]{3,2,1,0:T(8,128)(2,1)S(1)} collective-permute-done((bf16[2,4,16,1024]{3,2,1,0:T(8,128)(2,1)}, bf16[2,4,16,1024]{3,2,1,0:T(8,128)(2,1)S(1)}, u32[]{:S(2)}, u32[]{:S(2)}) %collective-permute-start.20) | collective-permute-done | bytes 262176 | tf_op jit(solution)/shard_map/ppermute | solution.py:43
  34.9 2.2 %shard_map.124 = (bf16[2,64,1024]{2,1,0:T(8,128)(2,1)}, bf16[2,64,1024]{2,1,0:T(8,128)(2,1)}, bf16[2,64,1024]{2,1,0:T(8,128)(2,1)}, bf16[2,64,1024]{2,1,0:T(8,128)(2,1)}) custom-call(bf16[2,4,16,1024]{3,2,1,0:T(8,128)(2,1)} %copy-done.26, bf16[2,4,16,1024]{3,2,1,0:T(8,128)(2,1)} %copy-done.28, bf16[2,4,16,1024]{3,2,1,0:T(8,128)(2,1)} %copy-done.29, ...), custom_call_target="tpu_custom_call" | custom-call | bytes 2097152 | tf_op jit(solution)/shard_map/pallas_call | solution.py:62
  37.2 1.2 collective-permute-start.22
  38.3 2.5 %collective-permute-start.23 = (bf16[2,64,1024]{2,1,0:T(8,128)(2,1)}, bf16[2,64,1024]{2,1,0:T(8,128)(2,1)S(1)}, u32[]{:S(2)}, u32[]{:S(2)}) collective-permute-start(bf16[2,64,1024]{2,1,0:T(8,128)(2,1)} %get-tuple-element.75), channel_id=1, source_target_pairs={{0,64},{1,17},{2,66},{3,19},{4,68},{5,21},{6,70},{7,23},{8,72},{9,... | collective-permute-start | bytes 786440 | tf_op jit(solution)/shard_map/ppermute | solution.py:37
  40.8 1.1 collective-permute-start.24
  41.9 1.9 %collective-permute-done.1.refs_2_ = bf16[2,4,16,1024]{3,2,1,0:T(8,128)(2,1)S(1)} collective-permute-done((bf16[2,4,16,1024]{3,2,1,0:T(8,128)(2,1)}, bf16[2,4,16,1024]{3,2,1,0:T(8,128)(2,1)S(1)}, u32[]{:S(2)}, u32[]{:S(2)}) %collective-permute-start.1) | collective-permute-done | bytes 262176 | tf_op jit(solution)/shard_map/ppermute | solution.py:43
  44.6 2.2 %shard_map.119 = (bf16[2,64,1024]{2,1,0:T(8,128)(2,1)}, bf16[2,64,1024]{2,1,0:T(8,128)(2,1)}, bf16[2,64,1024]{2,1,0:T(8,128)(2,1)}, bf16[2,64,1024]{2,1,0:T(8,128)(2,1)}) custom-call(bf16[2,4,16,1024]{3,2,1,0:T(8,128)(2,1)} %get-tuple-element.49.refs_0_, bf16[2,4,16,1024]{3,2,1,0:T(8,128)(2,1)} %copy-done.19, bf16[2,4,16,1024]{3,2,1,0:T(8,128)(2,1)} %copy-done.21, ...), custom_call_target="tpu_custom_call" | custom-call | bytes 2097152 | tf_op jit(solution)/shard_map/pallas_call | solution.py:62
  46.8 1.2 collective-permute-start.3
  48.0 2.4 %collective-permute-start.4 = (bf16[2,64,1024]{2,1,0:T(8,128)(2,1)}, bf16[2,64,1024]{2,1,0:T(8,128)(2,1)S(1)}, u32[]{:S(2)}, u32[]{:S(2)}) collective-permute-start(bf16[2,64,1024]{2,1,0:T(8,128)(2,1)} %get-tuple-element.55), channel_id=1, source_target_pairs={{0,64},{1,17},{2,66},{3,19},{4,68},{5,21},{6,70},{7,23},{8,72},{9,... | collective-permute-start | bytes 786440 | tf_op jit(solution)/shard_map/ppermute | solution.py:37
  50.4 1.2 collective-permute-start.5
  51.6 1.1 collective-permute-done.23.refs_2_.refs_14_
  53.5 5.1 %shard_map.125 = (f32[64,2304]{1,0:T(8,128)}, bf16[64,2304]{1,0:T(8,128)(2,1)}, bf16[64,2304]{1,0:T(8,128)(2,1)}, bf16[64,2304]{1,0:T(8,128)(2,1)}) custom-call(bf16[2,64,1024]{2,1,0:T(8,128)(2,1)} %get-tuple-element.73.refs_0_.refs_12_, bf16[2,64,1024]{2,1,0:T(8,128)(2,1)} %copy-done.6, bf16[2,64,1024]{2,1,0:T(8,128)(2,1)} %copy-done.7, ...), custom_call_target="tpu_custom_call" | custom-call | flops 1207959552 | bytes 7241728 | tf_op jit(solution)/shard_map/pallas_call | solution.py:62
  61.9 5.1 %shard_map.120 = (f32[64,2304]{1,0:T(8,128)}, bf16[64,2304]{1,0:T(8,128)(2,1)}, bf16[64,2304]{1,0:T(8,128)(2,1)}, bf16[64,2304]{1,0:T(8,128)(2,1)}) custom-call(bf16[2,64,1024]{2,1,0:T(8,128)(2,1)} %get-tuple-element.53.refs_0_.refs_8_, bf16[2,64,1024]{2,1,0:T(8,128)(2,1)} %copy-done.9, bf16[2,64,1024]{2,1,0:T(8,128)(2,1)} %copy-done.10, ...), custom_call_target="tpu_custom_call" | custom-call | flops 1207959552 | bytes 7241728 | tf_op jit(solution)/shard_map/pallas_call | solution.py:62
  67.0 1.8 %collective-permute-start.6 = (bf16[64,2304]{1,0:T(8,128)(2,1)}, bf16[64,2304]{1,0:T(8,128)(2,1)S(1)}, u32[]{:S(2)}, u32[]{:S(2)}) collective-permute-start(bf16[64,2304]{1,0:T(8,128)(2,1)} %get-tuple-element.58), channel_id=1, source_target_pairs={{0,96},{1,25},{2,98},{3,27},{4,100},{5,29},{6,102},{7,31},{8,104},... | collective-permute-start | bytes 884744 | tf_op jit(solution)/shard_map/ppermute | solution.py:37
  71.2 2.2 %shard_map.126.refs_0_.refs_4_ = bf16[64,2304]{1,0:T(8,128)(2,1)} custom-call(f32[64,2304]{1,0:T(8,128)} %get-tuple-element.77.own, bf16[64,2304]{1,0:T(8,128)(2,1)} %copy-done.12, bf16[64,2304]{1,0:T(8,128)(2,1)} %copy-done.14, bf16[64,2304]{1,0:T(8,128)(2,1)} %copy-done.16), custom_call_target="tpu_custom_call" | custom-call | bytes 1769472 | tf_op jit(solution)/shard_map/pallas_call | solution.py:62
  73.5 1.9 %collective-permute-start.30 = (bf16[64,2304]{1,0:T(8,128)(2,1)}, bf16[64,2304]{1,0:T(8,128)(2,1)S(1)}, u32[]{:S(2)}, u32[]{:S(2)}) collective-permute-start(bf16[64,2304]{1,0:T(8,128)(2,1)} %shard_map.126.refs_0_.refs_4_), channel_id=1, source_target_pairs={{0,96},{1,25},{2,98},{3,27},{4,100},{5,29},{6,102},{7,31},{8,104},... | collective-permute-start | bytes 884744 | tf_op jit(solution)/shard_map/ppermute | solution.py:37
  76.5 3.1 %collective-permute-done.8.p3 = bf16[64,2304]{1,0:T(8,128)(2,1)S(1)} collective-permute-done((bf16[64,2304]{1,0:T(8,128)(2,1)}, bf16[64,2304]{1,0:T(8,128)(2,1)S(1)}, u32[]{:S(2)}, u32[]{:S(2)}) %collective-permute-start.8) | collective-permute-done | bytes 294944 | tf_op jit(solution)/shard_map/ppermute | solution.py:37
  80.3 2.2 %shard_map.121.refs_0_ = bf16[64,2304]{1,0:T(8,128)(2,1)} custom-call(f32[64,2304]{1,0:T(8,128)} %get-tuple-element.57.own, bf16[64,2304]{1,0:T(8,128)(2,1)} %copy-done.13, bf16[64,2304]{1,0:T(8,128)(2,1)} %copy-done.15, bf16[64,2304]{1,0:T(8,128)(2,1)} %copy-done.17), custom_call_target="tpu_custom_call" | custom-call | bytes 1769472 | tf_op jit(solution)/shard_map/pallas_call | solution.py:62
  84.4 1.7 collective-permute-done.28.refs_1_.refs_5_
  86.1 2.5 %collective-permute-done.11.refs_3_ = bf16[64,2304]{1,0:T(8,128)(2,1)S(1)} collective-permute-done((bf16[64,2304]{1,0:T(8,128)(2,1)}, bf16[64,2304]{1,0:T(8,128)(2,1)S(1)}, u32[]{:S(2)}, u32[]{:S(2)}) %collective-permute-start.11) | collective-permute-done | bytes 294944 | tf_op jit(solution)/shard_map/ppermute | solution.py:37
  88.6 1.6 collective-permute-done.10.refs_2_
  90.3 3.3 %collective-permute-done.9.refs_1_ = bf16[64,2304]{1,0:T(8,128)(2,1)S(1)} collective-permute-done((bf16[64,2304]{1,0:T(8,128)(2,1)}, bf16[64,2304]{1,0:T(8,128)(2,1)S(1)}, u32[]{:S(2)}, u32[]{:S(2)}) %collective-permute-start.9) | collective-permute-done | bytes 294944 | tf_op jit(solution)/shard_map/ppermute | solution.py:37
  94.4 7.1 %shard_map.130 = bf16[4,3,256,768]{3,2,1,0:T(8,128)(2,1)} custom-call(bf16[64,2304]{1,0:T(8,128)(2,1)} %shard_map.121.refs_0_, bf16[64,2304]{1,0:T(8,128)(2,1)} %copy-done.5, bf16[64,2304]{1,0:T(8,128)(2,1)} %copy-done.4, bf16[64,2304]{1,0:T(8,128)(2,1)} %copy-done.2, bf16[64,2304]{1,0:T(8,128)(2,1)} %shard_map.126.refs_0_.refs_4_, ...), custom_call_target="tpu_custom_call" | custom-call | flops 2415919104 | bytes 9175040 | tf_op jit(solution)/shard_map/pallas_call | solution.py:62
  101.5 5.1 %shard_map.127 = (bf16[2,64,1024]{2,1,0:T(8,128)(2,1)}, bf16[2,64,1024]{2,1,0:T(8,128)(2,1)}, bf16[2,64,1024]{2,1,0:T(8,128)(2,1)}, bf16[2,64,1024]{2,1,0:T(8,128)(2,1)}) custom-call(bf16[64,2304]{1,0:T(8,128)(2,1)} %shard_map.126.refs_0_.refs_4_, bf16[64,2304]{1,0:T(8,128)(2,1)} %copy-done.3, bf16[64,2304]{1,0:T(8,128)(2,1)} %copy-done.1, ...), custom_call_target="tpu_custom_call" | custom-call | flops 1207959552 | bytes 6946816 | tf_op jit(solution)/shard_map/pallas_call | solution.py:62
  106.5 1.2 collective-permute-start.31
  108.4 5.0 %shard_map.122 = (bf16[2,64,1024]{2,1,0:T(8,128)(2,1)}, bf16[2,64,1024]{2,1,0:T(8,128)(2,1)}, bf16[2,64,1024]{2,1,0:T(8,128)(2,1)}, bf16[2,64,1024]{2,1,0:T(8,128)(2,1)}) custom-call(bf16[64,2304]{1,0:T(8,128)(2,1)} %shard_map.121.refs_0_, bf16[64,2304]{1,0:T(8,128)(2,1)} %copy-done.5, bf16[64,2304]{1,0:T(8,128)(2,1)} %copy-done.4, ...), custom_call_target="tpu_custom_call" | custom-call | flops 1207959552 | bytes 6946816 | tf_op jit(solution)/shard_map/pallas_call | solution.py:62
  113.4 2.1 %collective-permute-start.12 = (bf16[2,64,1024]{2,1,0:T(8,128)(2,1)}, bf16[2,64,1024]{2,1,0:T(8,128)(2,1)S(1)}, u32[]{:S(2)}, u32[]{:S(2)}) collective-permute-start(bf16[2,64,1024]{2,1,0:T(8,128)(2,1)} %get-tuple-element.62), channel_id=1, source_target_pairs={{0,96},{1,25},{2,98},{3,27},{4,100},{5,29},{6,102},{7,31},{8,104},... | collective-permute-start | bytes 786440 | tf_op jit(solution)/shard_map/ppermute | solution.py:37
  115.5 1.8 %collective-permute-start.13 = (bf16[2,64,1024]{2,1,0:T(8,128)(2,1)}, bf16[2,64,1024]{2,1,0:T(8,128)(2,1)S(1)}, u32[]{:S(2)}, u32[]{:S(2)}) collective-permute-start(bf16[2,64,1024]{2,1,0:T(8,128)(2,1)} %get-tuple-element.63), channel_id=1, source_target_pairs={{0,64},{1,17},{2,66},{3,19},{4,68},{5,21},{6,70},{7,23},{8,72},{9,... | collective-permute-start | bytes 786440 | tf_op jit(solution)/shard_map/ppermute | solution.py:37
  119.0 2.2 %shard_map.128 = (bf16[2,4,16,1024]{3,2,1,0:T(8,128)(2,1)}, bf16[2,4,16,1024]{3,2,1,0:T(8,128)(2,1)}, bf16[2,4,16,1024]{3,2,1,0:T(8,128)(2,1)}, bf16[2,4,16,1024]{3,2,1,0:T(8,128)(2,1)}) custom-call(bf16[2,64,1024]{2,1,0:T(8,128)(2,1)} %get-tuple-element.81.refs_0_, bf16[2,64,1024]{2,1,0:T(8,128)(2,1)} %copy-done.24, bf16[2,64,1024]{2,1,0:T(8,128)(2,1)} %copy-done.25, ...), custom_call_target="tpu_custom_call" | custom-call | bytes 2097152 | tf_op jit(solution)/shard_map/pallas_call | solution.py:62
  121.2 7.5 %collective-permute-start.34 = (bf16[2,4,16,1024]{3,2,1,0:T(8,128)(2,1)}, bf16[2,4,16,1024]{3,2,1,0:T(8,128)(2,1)S(1)}, u32[]{:S(2)}, u32[]{:S(2)}) collective-permute-start(bf16[2,4,16,1024]{3,2,1,0:T(8,128)(2,1)} %get-tuple-element.85), channel_id=1, source_target_pairs={{0,1},{1,0},{2,3},{3,2},{4,5},{5,4},{6,7},{7,6},{8,9},{9,8},{10,11... | collective-permute-start | bytes 786440 | tf_op jit(solution)/shard_map/ppermute | solution.py:43
  128.7 3.7 %collective-permute-start.35 = (bf16[2,4,16,1024]{3,2,1,0:T(8,128)(2,1)}, bf16[2,4,16,1024]{3,2,1,0:T(8,128)(2,1)S(1)}, u32[]{:S(2)}, u32[]{:S(2)}) collective-permute-start(bf16[2,4,16,1024]{3,2,1,0:T(8,128)(2,1)} %get-tuple-element.86), channel_id=1, source_target_pairs={{0,7},{1,6},{2,1},{3,0},{4,3},{5,2},{6,5},{7,4},{8,15},{9,14},{10,... | collective-permute-start | bytes 786440 | tf_op jit(solution)/shard_map/ppermute | solution.py:43
  132.4 2.8 %collective-permute-start.36 = (bf16[2,4,16,1024]{3,2,1,0:T(8,128)(2,1)}, bf16[2,4,16,1024]{3,2,1,0:T(8,128)(2,1)S(1)}, u32[]{:S(2)}, u32[]{:S(2)}) collective-permute-start(bf16[2,4,16,1024]{3,2,1,0:T(8,128)(2,1)} %get-tuple-element.87), channel_id=1, source_target_pairs={{0,5},{1,4},{2,7},{3,6},{4,1},{5,0},{6,3},{7,2},{8,13},{9,12},{10,... | collective-permute-start | bytes 786440 | tf_op jit(solution)/shard_map/ppermute | solution.py:43
  136.5 2.2 %shard_map.123 = (bf16[2,4,16,1024]{3,2,1,0:T(8,128)(2,1)}, bf16[2,4,16,1024]{3,2,1,0:T(8,128)(2,1)}, bf16[2,4,16,1024]{3,2,1,0:T(8,128)(2,1)}, bf16[2,4,16,1024]{3,2,1,0:T(8,128)(2,1)}) custom-call(bf16[2,64,1024]{2,1,0:T(8,128)(2,1)} %get-tuple-element.61.refs_0_, bf16[2,64,1024]{2,1,0:T(8,128)(2,1)} %copy-done.18, bf16[2,64,1024]{2,1,0:T(8,128)(2,1)} %copy-done.20, ...), custom_call_target="tpu_custom_call" | custom-call | bytes 2097152 | tf_op jit(solution)/shard_map/pallas_call | solution.py:62
  139.7 2.6 %collective-permute-start.16 = (bf16[2,4,16,1024]{3,2,1,0:T(8,128)(2,1)}, bf16[2,4,16,1024]{3,2,1,0:T(8,128)(2,1)S(1)}, u32[]{:S(2)}, u32[]{:S(2)}) collective-permute-start(bf16[2,4,16,1024]{3,2,1,0:T(8,128)(2,1)} %get-tuple-element.67), channel_id=1, source_target_pairs={{0,4},{1,5},{2,6},{3,7},{4,0},{5,1},{6,2},{7,3},{8,12},{9,13},{10,... | collective-permute-start | bytes 786440 | tf_op jit(solution)/shard_map/ppermute | solution.py:43
  142.2 1.4 collective-permute-done.35.refs_5_
  143.7 4.7 %collective-permute-done.37.refs_7_ = bf16[2,4,16,1024]{3,2,1,0:T(8,128)(2,1)S(1)} collective-permute-done((bf16[2,4,16,1024]{3,2,1,0:T(8,128)(2,1)}, bf16[2,4,16,1024]{3,2,1,0:T(8,128)(2,1)S(1)}, u32[]{:S(2)}, u32[]{:S(2)}) %collective-permute-start.37) | collective-permute-done | bytes 262176 | tf_op jit(solution)/shard_map/ppermute | solution.py:43
  148.4 6.6 %collective-permute-done.15.refs_1_ = bf16[2,4,16,1024]{3,2,1,0:T(8,128)(2,1)S(1)} collective-permute-done((bf16[2,4,16,1024]{3,2,1,0:T(8,128)(2,1)}, bf16[2,4,16,1024]{3,2,1,0:T(8,128)(2,1)S(1)}, u32[]{:S(2)}, u32[]{:S(2)}) %collective-permute-start.15) | collective-permute-done | bytes 262176 | tf_op jit(solution)/shard_map/ppermute | solution.py:43
  155.0 4.6 %collective-permute-done.17.refs_3_ = bf16[2,4,16,1024]{3,2,1,0:T(8,128)(2,1)S(1)} collective-permute-done((bf16[2,4,16,1024]{3,2,1,0:T(8,128)(2,1)}, bf16[2,4,16,1024]{3,2,1,0:T(8,128)(2,1)S(1)}, u32[]{:S(2)}, u32[]{:S(2)}) %collective-permute-start.17) | collective-permute-done | bytes 262176 | tf_op jit(solution)/shard_map/ppermute | solution.py:43
  160.4 4.7 %shard_map.129 = (bf16[128,4096]{1,0:T(8,128)(2,1)}, bf16[128,4096]{1,0:T(8,128)(2,1)}, f32[8,128]{1,0:T(8,128)}) custom-call(s32[4]{0:T(128)} %pad_add_fusion.place, s32[8,128]{1,0:T(8,128)} %bitcast.19, f32[8,128]{1,0:T(8,128)} %bitcast.21, bf16[128,4096]{1,0:T(8,128)(2,1)} %cotangent.3, bf16[2,4,16,1024]{3,2,1,0:T(8,128)(2,1)} %get-tuple-element.65.refs_0_, ...), custom_call_target="tpu_custom_call" | custom-call | flops 536870912 | bytes 5255168 | tf_op jit(solution)/shard_map/pallas_call | solution.py:62
  165.1 1.5 convert_element_type.4
  166.5 1.4 slice_bitcast_fusion
  (127 shorter events, 21.1 us)
Async XLA Ops:
  7.2 45.5 %all-gather.3.cloned.1.call-start = ((), (), s32[]{:S(2)}) async-start(), calls=%async_computation.2 | async-start | bytes 5898240 | tf_op jit(solution)/shard_map/all_gather | solution.py:239
  9.6 155.4 %reduce-scatter.2.cloned.1.call-start = ((), (), s32[]{:S(2)}) async-start(), calls=%async_computation.1 | async-start | bytes 5898240 | tf_op jit(solution)/shard_map/reduce_scatter | solution.py:271
  14.1 8.1 %collective-permute-start.18 = (bf16[2,4,16,1024]{3,2,1,0:T(8,128)(2,1)}, bf16[2,4,16,1024]{3,2,1,0:T(8,128)(2,1)S(1)}, u32[]{:S(2)}, u32[]{:S(2)}) collective-permute-start(bf16[2,4,16,1024]{3,2,1,0:T(8,128)(2,1)} %get-tuple-element.69), channel_id=1, source_target_pairs={{0,1},{1,0},{2,3},{3,2},{4,5},{5,4},{6,7},{7,6},{8,9},{9,8},{10,11... | collective-permute-start | bytes 786440 | tf_op jit(solution)/shard_map/ppermute | solution.py:43
  15.5 10.8 %collective-permute-start.19 = (bf16[2,4,16,1024]{3,2,1,0:T(8,128)(2,1)}, bf16[2,4,16,1024]{3,2,1,0:T(8,128)(2,1)S(1)}, u32[]{:S(2)}, u32[]{:S(2)}) collective-permute-start(bf16[2,4,16,1024]{3,2,1,0:T(8,128)(2,1)} %get-tuple-element.70), channel_id=1, source_target_pairs={{0,3},{1,2},{2,5},{3,4},{4,7},{5,6},{6,1},{7,0},{8,11},{9,10},{10,... | collective-permute-start | bytes 786440 | tf_op jit(solution)/shard_map/ppermute | solution.py:43
  17.1 16.4 %collective-permute-start.20 = (bf16[2,4,16,1024]{3,2,1,0:T(8,128)(2,1)}, bf16[2,4,16,1024]{3,2,1,0:T(8,128)(2,1)S(1)}, u32[]{:S(2)}, u32[]{:S(2)}) collective-permute-start(bf16[2,4,16,1024]{3,2,1,0:T(8,128)(2,1)} %get-tuple-element.71), channel_id=1, source_target_pairs={{0,5},{1,4},{2,7},{3,6},{4,1},{5,0},{6,3},{7,2},{8,13},{9,12},{10,... | collective-permute-start | bytes 786440 | tf_op jit(solution)/shard_map/ppermute | solution.py:43
  20.8 12.7 %collective-permute-start.21 = (bf16[2,4,16,1024]{3,2,1,0:T(8,128)(2,1)}, bf16[2,4,16,1024]{3,2,1,0:T(8,128)(2,1)S(1)}, u32[]{:S(2)}, u32[]{:S(2)}) collective-permute-start(bf16[2,4,16,1024]{3,2,1,0:T(8,128)(2,1)} %get-tuple-element.72), channel_id=1, source_target_pairs={{0,7},{1,6},{2,1},{3,0},{4,3},{5,2},{6,5},{7,4},{8,15},{9,14},{10,... | collective-permute-start | bytes 786440 | tf_op jit(solution)/shard_map/ppermute | solution.py:43
  21.5 19.4 %collective-permute-start = (bf16[2,4,16,1024]{3,2,1,0:T(8,128)(2,1)}, bf16[2,4,16,1024]{3,2,1,0:T(8,128)(2,1)S(1)}, u32[]{:S(2)}, u32[]{:S(2)}) collective-permute-start(bf16[2,4,16,1024]{3,2,1,0:T(8,128)(2,1)} %get-tuple-element.50), channel_id=1, source_target_pairs={{0,2},{1,3},{2,4},{3,5},{4,6},{5,7},{6,0},{7,1},{8,10},{9,11},{10,... | collective-permute-start | bytes 786440 | tf_op jit(solution)/shard_map/ppermute | solution.py:43
  22.2 11.3 %copy-start.26 = (bf16[2,4,16,1024]{3,2,1,0:T(8,128)(2,1)}, bf16[2,4,16,1024]{3,2,1,0:T(8,128)(2,1)S(1)}, u32[]{:S(2)}) copy-start(bf16[2,4,16,1024]{3,2,1,0:T(8,128)(2,1)S(1)} %collective-permute-done.18.refs_0_) | copy-start | bytes 786436
  22.2 21.6 %collective-permute-start.1 = (bf16[2,4,16,1024]{3,2,1,0:T(8,128)(2,1)}, bf16[2,4,16,1024]{3,2,1,0:T(8,128)(2,1)S(1)}, u32[]{:S(2)}, u32[]{:S(2)}) collective-permute-start(bf16[2,4,16,1024]{3,2,1,0:T(8,128)(2,1)} %get-tuple-element.51), channel_id=1, source_target_pairs={{0,4},{1,5},{2,6},{3,7},{4,0},{5,1},{6,2},{7,3},{8,12},{9,13},{10,... | collective-permute-start | bytes 786440 | tf_op jit(solution)/shard_map/ppermute | solution.py:43
  26.3 17.5 %collective-permute-start.2 = (bf16[2,4,16,1024]{3,2,1,0:T(8,128)(2,1)}, bf16[2,4,16,1024]{3,2,1,0:T(8,128)(2,1)S(1)}, u32[]{:S(2)}, u32[]{:S(2)}) collective-permute-start(bf16[2,4,16,1024]{3,2,1,0:T(8,128)(2,1)} %get-tuple-element.52), channel_id=1, source_target_pairs={{0,6},{1,7},{2,0},{3,1},{4,2},{5,3},{6,4},{7,5},{8,14},{9,15},{10,... | collective-permute-start | bytes 786440 | tf_op jit(solution)/shard_map/ppermute | solution.py:43
  37.2 13.3 %collective-permute-start.22 = (bf16[2,64,1024]{2,1,0:T(8,128)(2,1)}, bf16[2,64,1024]{2,1,0:T(8,128)(2,1)S(1)}, u32[]{:S(2)}, u32[]{:S(2)}) collective-permute-start(bf16[2,64,1024]{2,1,0:T(8,128)(2,1)} %get-tuple-element.74), channel_id=1, source_target_pairs={{0,32},{1,9},{2,34},{3,11},{4,36},{5,13},{6,38},{7,15},{8,40},{9,1... | collective-permute-start | bytes 786440 | tf_op jit(solution)/shard_map/ppermute | solution.py:37
  38.3 14.3 %collective-permute-start.23 = (bf16[2,64,1024]{2,1,0:T(8,128)(2,1)}, bf16[2,64,1024]{2,1,0:T(8,128)(2,1)S(1)}, u32[]{:S(2)}, u32[]{:S(2)}) collective-permute-start(bf16[2,64,1024]{2,1,0:T(8,128)(2,1)} %get-tuple-element.75), channel_id=1, source_target_pairs={{0,64},{1,17},{2,66},{3,19},{4,68},{5,21},{6,70},{7,23},{8,72},{9,... | collective-permute-start | bytes 786440 | tf_op jit(solution)/shard_map/ppermute | solution.py:37
  40.8 11.8 %collective-permute-start.24 = (bf16[2,64,1024]{2,1,0:T(8,128)(2,1)}, bf16[2,64,1024]{2,1,0:T(8,128)(2,1)S(1)}, u32[]{:S(2)}, u32[]{:S(2)}) collective-permute-start(bf16[2,64,1024]{2,1,0:T(8,128)(2,1)} %get-tuple-element.76), channel_id=1, source_target_pairs={{0,96},{1,25},{2,98},{3,27},{4,100},{5,29},{6,102},{7,31},{8,104},... | collective-permute-start | bytes 786440 | tf_op jit(solution)/shard_map/ppermute | solution.py:37
  46.8 13.5 %collective-permute-start.3 = (bf16[2,64,1024]{2,1,0:T(8,128)(2,1)}, bf16[2,64,1024]{2,1,0:T(8,128)(2,1)S(1)}, u32[]{:S(2)}, u32[]{:S(2)}) collective-permute-start(bf16[2,64,1024]{2,1,0:T(8,128)(2,1)} %get-tuple-element.54), channel_id=1, source_target_pairs={{0,32},{1,9},{2,34},{3,11},{4,36},{5,13},{6,38},{7,15},{8,40},{9,1... | collective-permute-start | bytes 786440 | tf_op jit(solution)/shard_map/ppermute | solution.py:37
  48.0 13.1 %collective-permute-start.4 = (bf16[2,64,1024]{2,1,0:T(8,128)(2,1)}, bf16[2,64,1024]{2,1,0:T(8,128)(2,1)S(1)}, u32[]{:S(2)}, u32[]{:S(2)}) collective-permute-start(bf16[2,64,1024]{2,1,0:T(8,128)(2,1)} %get-tuple-element.55), channel_id=1, source_target_pairs={{0,64},{1,17},{2,66},{3,19},{4,68},{5,21},{6,70},{7,23},{8,72},{9,... | collective-permute-start | bytes 786440 | tf_op jit(solution)/shard_map/ppermute | solution.py:37
  50.4 10.7 %collective-permute-start.5 = (bf16[2,64,1024]{2,1,0:T(8,128)(2,1)}, bf16[2,64,1024]{2,1,0:T(8,128)(2,1)S(1)}, u32[]{:S(2)}, u32[]{:S(2)}) collective-permute-start(bf16[2,64,1024]{2,1,0:T(8,128)(2,1)} %get-tuple-element.56), channel_id=1, source_target_pairs={{0,96},{1,25},{2,98},{3,27},{4,100},{5,29},{6,102},{7,31},{8,104},... | collective-permute-start | bytes 786440 | tf_op jit(solution)/shard_map/ppermute | solution.py:37
  58.6 11.0 %collective-permute-start.25 = (bf16[64,2304]{1,0:T(8,128)(2,1)}, bf16[64,2304]{1,0:T(8,128)(2,1)S(1)}, u32[]{:S(2)}, u32[]{:S(2)}) collective-permute-start(bf16[64,2304]{1,0:T(8,128)(2,1)} %get-tuple-element.78), channel_id=1, source_target_pairs={{0,96},{1,25},{2,98},{3,27},{4,100},{5,29},{6,102},{7,31},{8,104},... | collective-permute-start | bytes 884744 | tf_op jit(solution)/shard_map/ppermute | solution.py:37
  59.3 11.1 %collective-permute-start.26 = (bf16[64,2304]{1,0:T(8,128)(2,1)}, bf16[64,2304]{1,0:T(8,128)(2,1)S(1)}, u32[]{:S(2)}, u32[]{:S(2)}) collective-permute-start(bf16[64,2304]{1,0:T(8,128)(2,1)} %get-tuple-element.79), channel_id=1, source_target_pairs={{0,64},{1,17},{2,66},{3,19},{4,68},{5,21},{6,70},{7,23},{8,72},{9,... | collective-permute-start | bytes 884744 | tf_op jit(solution)/shard_map/ppermute | solution.py:37
  60.3 10.1 %collective-permute-start.27 = (bf16[64,2304]{1,0:T(8,128)(2,1)}, bf16[64,2304]{1,0:T(8,128)(2,1)S(1)}, u32[]{:S(2)}, u32[]{:S(2)}) collective-permute-start(bf16[64,2304]{1,0:T(8,128)(2,1)} %get-tuple-element.80), channel_id=1, source_target_pairs={{0,32},{1,9},{2,34},{3,11},{4,36},{5,13},{6,38},{7,15},{8,40},{9,1... | collective-permute-start | bytes 884744 | tf_op jit(solution)/shard_map/ppermute | solution.py:37
  67.0 9.3 %collective-permute-start.6 = (bf16[64,2304]{1,0:T(8,128)(2,1)}, bf16[64,2304]{1,0:T(8,128)(2,1)S(1)}, u32[]{:S(2)}, u32[]{:S(2)}) collective-permute-start(bf16[64,2304]{1,0:T(8,128)(2,1)} %get-tuple-element.58), channel_id=1, source_target_pairs={{0,96},{1,25},{2,98},{3,27},{4,100},{5,29},{6,102},{7,31},{8,104},... | collective-permute-start | bytes 884744 | tf_op jit(solution)/shard_map/ppermute | solution.py:37
  68.8 7.6 %collective-permute-start.7 = (bf16[64,2304]{1,0:T(8,128)(2,1)}, bf16[64,2304]{1,0:T(8,128)(2,1)S(1)}, u32[]{:S(2)}, u32[]{:S(2)}) collective-permute-start(bf16[64,2304]{1,0:T(8,128)(2,1)} %get-tuple-element.59), channel_id=1, source_target_pairs={{0,64},{1,17},{2,66},{3,19},{4,68},{5,21},{6,70},{7,23},{8,72},{9,... | collective-permute-start | bytes 884744 | tf_op jit(solution)/shard_map/ppermute | solution.py:37
  69.6 10.0 %collective-permute-start.8 = (bf16[64,2304]{1,0:T(8,128)(2,1)}, bf16[64,2304]{1,0:T(8,128)(2,1)S(1)}, u32[]{:S(2)}, u32[]{:S(2)}) collective-permute-start(bf16[64,2304]{1,0:T(8,128)(2,1)} %get-tuple-element.60), channel_id=1, source_target_pairs={{0,32},{1,9},{2,34},{3,11},{4,36},{5,13},{6,38},{7,15},{8,40},{9,1... | collective-permute-start | bytes 884744 | tf_op jit(solution)/shard_map/ppermute | solution.py:37
  73.5 10.2 %collective-permute-start.30 = (bf16[64,2304]{1,0:T(8,128)(2,1)}, bf16[64,2304]{1,0:T(8,128)(2,1)S(1)}, u32[]{:S(2)}, u32[]{:S(2)}) collective-permute-start(bf16[64,2304]{1,0:T(8,128)(2,1)} %shard_map.126.refs_0_.refs_4_), channel_id=1, source_target_pairs={{0,96},{1,25},{2,98},{3,27},{4,100},{5,29},{6,102},{7,31},{8,104},... | collective-permute-start | bytes 884744 | tf_op jit(solution)/shard_map/ppermute | solution.py:37
  75.4 9.0 %collective-permute-start.29 = (bf16[64,2304]{1,0:T(8,128)(2,1)}, bf16[64,2304]{1,0:T(8,128)(2,1)S(1)}, u32[]{:S(2)}, u32[]{:S(2)}) collective-permute-start(bf16[64,2304]{1,0:T(8,128)(2,1)} %shard_map.126.refs_0_.refs_4_), channel_id=1, source_target_pairs={{0,64},{1,17},{2,66},{3,19},{4,68},{5,21},{6,70},{7,23},{8,72},{9,... | collective-permute-start | bytes 884744 | tf_op jit(solution)/shard_map/ppermute | solution.py:37
  76.4 9.7 %collective-permute-start.28 = (bf16[64,2304]{1,0:T(8,128)(2,1)}, bf16[64,2304]{1,0:T(8,128)(2,1)S(1)}, u32[]{:S(2)}, u32[]{:S(2)}) collective-permute-start(bf16[64,2304]{1,0:T(8,128)(2,1)} %shard_map.126.refs_0_.refs_4_), channel_id=1, source_target_pairs={{0,32},{1,9},{2,34},{3,11},{4,36},{5,13},{6,38},{7,15},{8,40},{9,1... | collective-permute-start | bytes 884744 | tf_op jit(solution)/shard_map/ppermute | solution.py:37
  82.5 6.1 %collective-permute-start.11 = (bf16[64,2304]{1,0:T(8,128)(2,1)}, bf16[64,2304]{1,0:T(8,128)(2,1)S(1)}, u32[]{:S(2)}, u32[]{:S(2)}) collective-permute-start(bf16[64,2304]{1,0:T(8,128)(2,1)} %shard_map.121.refs_0_), channel_id=1, source_target_pairs={{0,96},{1,25},{2,98},{3,27},{4,100},{5,29},{6,102},{7,31},{8,104},... | collective-permute-start | bytes 884744 | tf_op jit(solution)/shard_map/ppermute | solution.py:37
  82.9 7.4 %collective-permute-start.10 = (bf16[64,2304]{1,0:T(8,128)(2,1)}, bf16[64,2304]{1,0:T(8,128)(2,1)S(1)}, u32[]{:S(2)}, u32[]{:S(2)}) collective-permute-start(bf16[64,2304]{1,0:T(8,128)(2,1)} %shard_map.121.refs_0_), channel_id=1, source_target_pairs={{0,64},{1,17},{2,66},{3,19},{4,68},{5,21},{6,70},{7,23},{8,72},{9,... | collective-permute-start | bytes 884744 | tf_op jit(solution)/shard_map/ppermute | solution.py:37
  83.6 10.0 %copy-start = (bf16[64,2304]{1,0:T(8,128)(2,1)}, bf16[64,2304]{1,0:T(8,128)(2,1)S(1)}, u32[]{:S(2)}) copy-start(bf16[64,2304]{1,0:T(8,128)(2,1)S(1)} %collective-permute-done.30.refs_3_.refs_7_) | copy-start | bytes 884740
  83.6 10.0 %collective-permute-start.9 = (bf16[64,2304]{1,0:T(8,128)(2,1)}, bf16[64,2304]{1,0:T(8,128)(2,1)S(1)}, u32[]{:S(2)}, u32[]{:S(2)}) collective-permute-start(bf16[64,2304]{1,0:T(8,128)(2,1)} %shard_map.121.refs_0_), channel_id=1, source_target_pairs={{0,32},{1,9},{2,34},{3,11},{4,36},{5,13},{6,38},{7,15},{8,40},{9,1... | collective-permute-start | bytes 884744 | tf_op jit(solution)/shard_map/ppermute | solution.py:37
  84.4 9.2 %copy-start.1 = (bf16[64,2304]{1,0:T(8,128)(2,1)}, bf16[64,2304]{1,0:T(8,128)(2,1)S(1)}, u32[]{:S(2)}) copy-start(bf16[64,2304]{1,0:T(8,128)(2,1)S(1)} %collective-permute-done.29.refs_2_.refs_6_) | copy-start | bytes 884740
  86.1 7.5 %copy-start.3 = (bf16[64,2304]{1,0:T(8,128)(2,1)}, bf16[64,2304]{1,0:T(8,128)(2,1)S(1)}, u32[]{:S(2)}) copy-start(bf16[64,2304]{1,0:T(8,128)(2,1)S(1)} %collective-permute-done.28.refs_1_.refs_5_) | copy-start | bytes 884740
  106.5 10.7 %collective-permute-start.31 = (bf16[2,64,1024]{2,1,0:T(8,128)(2,1)}, bf16[2,64,1024]{2,1,0:T(8,128)(2,1)S(1)}, u32[]{:S(2)}, u32[]{:S(2)}) collective-permute-start(bf16[2,64,1024]{2,1,0:T(8,128)(2,1)} %get-tuple-element.82), channel_id=1, source_target_pairs={{0,96},{1,25},{2,98},{3,27},{4,100},{5,29},{6,102},{7,31},{8,104},... | collective-permute-start | bytes 786440 | tf_op jit(solution)/shard_map/ppermute | solution.py:37
  107.8 9.7 %collective-permute-start.32 = (bf16[2,64,1024]{2,1,0:T(8,128)(2,1)}, bf16[2,64,1024]{2,1,0:T(8,128)(2,1)S(1)}, u32[]{:S(2)}, u32[]{:S(2)}) collective-permute-start(bf16[2,64,1024]{2,1,0:T(8,128)(2,1)} %get-tuple-element.83), channel_id=1, source_target_pairs={{0,64},{1,17},{2,66},{3,19},{4,68},{5,21},{6,70},{7,23},{8,72},{9,... | collective-permute-start | bytes 786440 | tf_op jit(solution)/shard_map/ppermute | solution.py:37
  107.8 10.5 %collective-permute-start.33 = (bf16[2,64,1024]{2,1,0:T(8,128)(2,1)}, bf16[2,64,1024]{2,1,0:T(8,128)(2,1)S(1)}, u32[]{:S(2)}, u32[]{:S(2)}) collective-permute-start(bf16[2,64,1024]{2,1,0:T(8,128)(2,1)} %get-tuple-element.84), channel_id=1, source_target_pairs={{0,32},{1,9},{2,34},{3,11},{4,36},{5,13},{6,38},{7,15},{8,40},{9,1... | collective-permute-start | bytes 786440 | tf_op jit(solution)/shard_map/ppermute | solution.py:37
  113.4 19.0 %collective-permute-start.12 = (bf16[2,64,1024]{2,1,0:T(8,128)(2,1)}, bf16[2,64,1024]{2,1,0:T(8,128)(2,1)S(1)}, u32[]{:S(2)}, u32[]{:S(2)}) collective-permute-start(bf16[2,64,1024]{2,1,0:T(8,128)(2,1)} %get-tuple-element.62), channel_id=1, source_target_pairs={{0,96},{1,25},{2,98},{3,27},{4,100},{5,29},{6,102},{7,31},{8,104},... | collective-permute-start | bytes 786440 | tf_op jit(solution)/shard_map/ppermute | solution.py:37
  115.5 19.7 %collective-permute-start.13 = (bf16[2,64,1024]{2,1,0:T(8,128)(2,1)}, bf16[2,64,1024]{2,1,0:T(8,128)(2,1)S(1)}, u32[]{:S(2)}, u32[]{:S(2)}) collective-permute-start(bf16[2,64,1024]{2,1,0:T(8,128)(2,1)} %get-tuple-element.63), channel_id=1, source_target_pairs={{0,64},{1,17},{2,66},{3,19},{4,68},{5,21},{6,70},{7,23},{8,72},{9,... | collective-permute-start | bytes 786440 | tf_op jit(solution)/shard_map/ppermute | solution.py:37
  117.3 18.5 %collective-permute-start.14 = (bf16[2,64,1024]{2,1,0:T(8,128)(2,1)}, bf16[2,64,1024]{2,1,0:T(8,128)(2,1)S(1)}, u32[]{:S(2)}, u32[]{:S(2)}) collective-permute-start(bf16[2,64,1024]{2,1,0:T(8,128)(2,1)} %get-tuple-element.64), channel_id=1, source_target_pairs={{0,32},{1,9},{2,34},{3,11},{4,36},{5,13},{6,38},{7,15},{8,40},{9,1... | collective-permute-start | bytes 786440 | tf_op jit(solution)/shard_map/ppermute | solution.py:37
  121.2 18.4 %collective-permute-start.34 = (bf16[2,4,16,1024]{3,2,1,0:T(8,128)(2,1)}, bf16[2,4,16,1024]{3,2,1,0:T(8,128)(2,1)S(1)}, u32[]{:S(2)}, u32[]{:S(2)}) collective-permute-start(bf16[2,4,16,1024]{3,2,1,0:T(8,128)(2,1)} %get-tuple-element.85), channel_id=1, source_target_pairs={{0,1},{1,0},{2,3},{3,2},{4,5},{5,4},{6,7},{7,6},{8,9},{9,8},{10,11... | collective-permute-start | bytes 786440 | tf_op jit(solution)/shard_map/ppermute | solution.py:43
  128.7 14.9 %collective-permute-start.35 = (bf16[2,4,16,1024]{3,2,1,0:T(8,128)(2,1)}, bf16[2,4,16,1024]{3,2,1,0:T(8,128)(2,1)S(1)}, u32[]{:S(2)}, u32[]{:S(2)}) collective-permute-start(bf16[2,4,16,1024]{3,2,1,0:T(8,128)(2,1)} %get-tuple-element.86), channel_id=1, source_target_pairs={{0,7},{1,6},{2,1},{3,0},{4,3},{5,2},{6,5},{7,4},{8,15},{9,14},{10,... | collective-permute-start | bytes 786440 | tf_op jit(solution)/shard_map/ppermute | solution.py:43
  132.4 11.3 %collective-permute-start.36 = (bf16[2,4,16,1024]{3,2,1,0:T(8,128)(2,1)}, bf16[2,4,16,1024]{3,2,1,0:T(8,128)(2,1)S(1)}, u32[]{:S(2)}, u32[]{:S(2)}) collective-permute-start(bf16[2,4,16,1024]{3,2,1,0:T(8,128)(2,1)} %get-tuple-element.87), channel_id=1, source_target_pairs={{0,5},{1,4},{2,7},{3,6},{4,1},{5,0},{6,3},{7,2},{8,13},{9,12},{10,... | collective-permute-start | bytes 786440 | tf_op jit(solution)/shard_map/ppermute | solution.py:43
  135.2 13.2 %collective-permute-start.37 = (bf16[2,4,16,1024]{3,2,1,0:T(8,128)(2,1)}, bf16[2,4,16,1024]{3,2,1,0:T(8,128)(2,1)S(1)}, u32[]{:S(2)}, u32[]{:S(2)}) collective-permute-start(bf16[2,4,16,1024]{3,2,1,0:T(8,128)(2,1)} %get-tuple-element.88), channel_id=1, source_target_pairs={{0,3},{1,2},{2,5},{3,4},{4,7},{5,6},{6,1},{7,0},{8,11},{9,10},{10,... | collective-permute-start | bytes 786440 | tf_op jit(solution)/shard_map/ppermute | solution.py:43
  138.7 16.3 %collective-permute-start.15 = (bf16[2,4,16,1024]{3,2,1,0:T(8,128)(2,1)}, bf16[2,4,16,1024]{3,2,1,0:T(8,128)(2,1)S(1)}, u32[]{:S(2)}, u32[]{:S(2)}) collective-permute-start(bf16[2,4,16,1024]{3,2,1,0:T(8,128)(2,1)} %get-tuple-element.66), channel_id=1, source_target_pairs={{0,6},{1,7},{2,0},{3,1},{4,2},{5,3},{6,4},{7,5},{8,14},{9,15},{10,... | collective-permute-start | bytes 786440 | tf_op jit(solution)/shard_map/ppermute | solution.py:43
  139.7 20.0 %copy-start.31 = (bf16[2,4,16,1024]{3,2,1,0:T(8,128)(2,1)}, bf16[2,4,16,1024]{3,2,1,0:T(8,128)(2,1)S(1)}, u32[]{:S(2)}) copy-start(bf16[2,4,16,1024]{3,2,1,0:T(8,128)(2,1)S(1)} %collective-permute-done.34.refs_4_) | copy-start | bytes 786436
  139.7 15.4 %collective-permute-start.16 = (bf16[2,4,16,1024]{3,2,1,0:T(8,128)(2,1)}, bf16[2,4,16,1024]{3,2,1,0:T(8,128)(2,1)S(1)}, u32[]{:S(2)}, u32[]{:S(2)}) collective-permute-start(bf16[2,4,16,1024]{3,2,1,0:T(8,128)(2,1)} %get-tuple-element.67), channel_id=1, source_target_pairs={{0,4},{1,5},{2,6},{3,7},{4,0},{5,1},{6,2},{7,3},{8,12},{9,13},{10,... | collective-permute-start | bytes 786440 | tf_op jit(solution)/shard_map/ppermute | solution.py:43
  143.6 16.0 %copy-start.32 = (bf16[2,4,16,1024]{3,2,1,0:T(8,128)(2,1)}, bf16[2,4,16,1024]{3,2,1,0:T(8,128)(2,1)S(1)}, u32[]{:S(2)}) copy-start(bf16[2,4,16,1024]{3,2,1,0:T(8,128)(2,1)S(1)} %collective-permute-done.35.refs_5_) | copy-start | bytes 786436
  143.7 16.0 %collective-permute-start.17 = (bf16[2,4,16,1024]{3,2,1,0:T(8,128)(2,1)}, bf16[2,4,16,1024]{3,2,1,0:T(8,128)(2,1)S(1)}, u32[]{:S(2)}, u32[]{:S(2)}) collective-permute-start(bf16[2,4,16,1024]{3,2,1,0:T(8,128)(2,1)} %get-tuple-element.68), channel_id=1, source_target_pairs={{0,2},{1,3},{2,4},{3,5},{4,6},{5,7},{6,0},{7,1},{8,10},{9,11},{10,... | collective-permute-start | bytes 786440 | tf_op jit(solution)/shard_map/ppermute | solution.py:43
  143.7 16.0 %copy-start.33 = (bf16[2,4,16,1024]{3,2,1,0:T(8,128)(2,1)}, bf16[2,4,16,1024]{3,2,1,0:T(8,128)(2,1)S(1)}, u32[]{:S(2)}) copy-start(bf16[2,4,16,1024]{3,2,1,0:T(8,128)(2,1)S(1)} %collective-permute-done.36.refs_6_) | copy-start | bytes 786436
  148.4 11.3 %copy-start.34 = (bf16[2,4,16,1024]{3,2,1,0:T(8,128)(2,1)}, bf16[2,4,16,1024]{3,2,1,0:T(8,128)(2,1)S(1)}, u32[]{:S(2)}) copy-start(bf16[2,4,16,1024]{3,2,1,0:T(8,128)(2,1)S(1)} %collective-permute-done.37.refs_7_) | copy-start | bytes 786436
  (30 other events, 55.2 us)
Sparse Core Ops, SparseCore 0:
  9.8 41.1 all-gather.2
  101.6 46.3 reduce-scatter.1

commit v3 on v2

--- a/solution.py
+++ b/solution.py
@@ -13,7 +13,7 @@
 REL = 8
 COLS = 256
 FW = 768
-VMEM = 56 * 2**20
+VMEM = 12 * 2**20
 
 
 def _dev(y, x, z, c):
@@ -55,17 +55,16 @@
     return lax.dot_general(left, right, (((0,), (0,)), ((), ())), preferred_element_type=F32)
 
 
-def call(kernel, outs, ins, flops, smem=0):
-    vm = pl.BlockSpec(memory_space=pltpu.VMEM)
-    sm = pl.BlockSpec(memory_space=pltpu.SMEM)
-    moved = sum(v.size * v.dtype.itemsize for v in list(ins[smem:]) + list(outs))
+def call(kernel, outs, ins, flops, smem=0, hbm=0, scratch=(), vmem=VMEM):
+    spaces = [pltpu.SMEM] * smem + [pltpu.HBM] * hbm + [pltpu.VMEM] * (len(ins) - smem - hbm)
     return pl.pallas_call(
         kernel,
         out_shape=tuple(outs),
-        in_specs=[sm] * smem + [vm] * (len(ins) - smem),
-        out_specs=tuple([vm] * len(outs)),
-        compiler_params=pltpu.CompilerParams(vmem_limit_bytes=VMEM),
-        cost_estimate=pl.CostEstimate(flops=flops, bytes_accessed=moved, transcendentals=0),
+        in_specs=[pl.BlockSpec(memory_space=space) for space in spaces],
+        out_specs=tuple(pl.BlockSpec(memory_space=pltpu.VMEM) for _ in outs),
+        scratch_shapes=list(scratch),
+        compiler_params=pltpu.CompilerParams(vmem_limit_bytes=vmem),
+        cost_estimate=pl.CostEstimate(flops=flops // 100, bytes_accessed=1024, transcendentals=0),
     )(*ins)
 
 
@@ -104,13 +103,34 @@
     return jnp.where(flip == 0, dy, dx), jnp.where(flip == 0, xb, yb)
 
 
-def dispatch_kernel(place, ids, gates, tokens, cotangent, *outs):
-    _, chosen, scale = routing(place, ids[...], gates[...])
+def dispatch_kernel(place, ids, gates, tokens, cotangent, *refs):
+    outs, (ids_v, gates_v, tok_v, cot_v, sem) = refs[:REL], refs[REL:]
+    small = [
+        pltpu.make_async_copy(ids, ids_v, sem.at[0]),
+        pltpu.make_async_copy(gates, gates_v, sem.at[1]),
+    ]
+    wide, quarter = [], tokens.shape[1] // SIDE
+    for q in range(SIDE):
+        cols = slice(q * quarter, q * quarter + quarter)
+        wide.append(
+            (
+                pltpu.make_async_copy(tokens.at[:, cols], tok_v.at[q], sem.at[2 + 2 * q]),
+                pltpu.make_async_copy(cotangent.at[:, cols], cot_v.at[q], sem.at[3 + 2 * q]),
+            )
+        )
+    for copy in small + [c for pair in wide for c in pair]:
+        copy.start()
+    for copy in small:
+        copy.wait()
+    _, chosen, scale = routing(place, ids_v[...], gates_v[...])
     chosen = chosen.astype(BF)
     for blk in range(16):
-        cols = slice(blk * COLS, blk * COLS + COLS)
-        rows = dot(chosen, tokens[:, cols]).astype(BF)
-        grads = (scale * dot(chosen, cotangent[:, cols])).astype(BF)
+        q, cols = blk // 4, slice(blk % 4 * COLS, blk % 4 * COLS + COLS)
+        if blk % 4 == 0:
+            for copy in wide[q]:
+                copy.wait()
+        rows = dot(chosen, tok_v[q, :, cols]).astype(BF)
+        grads = (scale * dot(chosen, cot_v[q, :, cols])).astype(BF)
         for dc in range(2):
             sb, sa = block_place(place, dc, blk // 4, blk % 4)
             lanes = pl.ds(pl.multiple_of(sa * COLS, COLS), COLS)
@@ -144,8 +164,18 @@
     return [jnp.concatenate([p[:, k * FW : k * FW + FW] for p in pieces], axis=0) for k in range(3)]
 
 
+def held_kernel(gate, up, down, out, sem):
+    copies = [
+        pltpu.make_async_copy(w.at[0], out.at[k], sem.at[k]) for k, w in enumerate((gate, up, down))
+    ]
+    for copy in copies:
+        copy.start()
+    for copy in copies:
+        copy.wait()
+
+
 def partial_kernel(*refs):
-    xs, ws, own, outs = refs[:4], refs[4], refs[5], refs[6:]
+    xs, ws, outs = refs[:8], refs[8], refs[9:]
     rows = xs[0].shape[1]
     for which in range(3):
         left = stacked(xs, 0 if which < 2 else 1)
@@ -154,9 +184,8 @@
             at = slice(which * FW + n * COLS, which * FW + n * COLS + COLS)
             right = jnp.concatenate([ws[a, which, :, cols] for a in range(SIDE)], axis=0)
             got = dot(left, right)
-            own[:, at] = got[:rows]
-            for p in range(1, SIDE):
-                outs[p - 1][:, at] = got[p * rows : p * rows + rows].astype(BF)
+            for p in range(2 * SIDE):
+                outs[p][:, at] = got[p * rows : p * rows + rows].astype(outs[p].dtype)
 
 
 def hidden_kernel(own, p1, p2, p3, out):
@@ -195,6 +224,11 @@
         x, g = stacked(xs, 0, cols), stacked(xs, 1, cols)
         for k, (left, right) in enumerate(((x, ggate), (x, gup), (g, hidden))):
             out[a, k] = dot_first(left, right).astype(BF)
+
+
+def total_kernel(summed, *outs):
+    for k in range(3):
+        outs[k][0] = summed[k].astype(F32)
 
 
 def combine_kernel(place, ids, gates, cotangent, *refs):
@@ -235,7 +269,15 @@
     rows = SIDE * CAP
     work = 2 * SIDE * rows * chunk * 3 * FW
 
-    held = jnp.concatenate([w_gate, w_up, w_down], axis=0)
+    (held,) = call(
+        held_kernel,
+        [shape((3, COLS, FW))],
+        (w_gate, w_up, w_down),
+        0,
+        hbm=3,
+        vmem=60 * 2**20,
+        scratch=[pltpu.SemaphoreType.DMA((3,))],
+    )
     ws = lax.all_gather(held, AXES, axis_index_groups=groups_a())
 
     sends = call(
@@ -244,6 +286,15 @@
         (place, ids_t, gates_t, tokens, cotangent),
         4 * tok * tok * width,
         smem=1,
+        hbm=4,
+        vmem=60 * 2**20,
+        scratch=[
+            pltpu.VMEM(ids_t.shape, jnp.int32),
+            pltpu.VMEM(ids_t.shape, F32),
+            pltpu.VMEM((SIDE, tok, chunk), BF),
+            pltpu.VMEM((SIDE, tok, chunk), BF),
+            pltpu.SemaphoreType.DMA((10,)),
+        ],
     )
     came = [sends[0]] + [shift_z(sends[r], r % 4, r // 4) for r in range(1, REL)]
     xs, hs, backs = [], [], []
@@ -255,27 +306,37 @@
             0,
         )
         xs.append([turned[0]] + [shift_b(turned[s], s) for s in (1, 2, 3)])
+    blocks = [shape((rows, 3 * FW), F32)] + [shape((rows, 3 * FW))] * 3
+    parts = call(partial_kernel, blocks * 2, (*xs[0], *xs[1], ws), 2 * work)
     for half in range(2):
-        parts = call(
-            partial_kernel,
-            [shape((rows, 3 * FW), F32)] + [shape((rows, 3 * FW))] * 3,
-            (*xs[half], ws),
-            work,
+        own, *sent = parts[half * SIDE : half * SIDE + SIDE]
+        others = [shift_b(sent[s - 1], -s) for s in (1, 2, 3)]
+        (mid,) = call(hidden_kernel, [shape((rows, 3 * FW))], (own, *others), 0)
+        hs.append([mid] + [shift_b(mid, s) for s in (1, 2, 3)])
+
+    def send_back(half, hs):
+        outs = call(
+            rows_kernel, [shape((2, rows, chunk))] * SIDE, (*hs, ws), work
         )
-        others = [shift_b(parts[s], -s) for s in (1, 2, 3)]
-        (mid,) = call(hidden_kernel, [shape((rows, 3 * FW))], (parts[0], *others), 0)
-        hs.append([mid] + [shift_b(mid, s) for s in (1, 2, 3)])
+        return [outs[0]] + [shift_b(outs[s], -s) for s in (1, 2, 3)], outs
+
+    def to_source(half, home):
+        split = call(to_z_kernel, [shape((2, SIDE, CAP, chunk))] * SIDE, home, 0)
+        return [split[dz] if dz + half == 0 else shift_z(split[dz], -dz, half) for dz in range(SIDE)]
+
+    home_a, _ = send_back(0, hs[0])
+    hs_b, _ = lax.optimization_barrier((hs[1], (home_a[1], home_a[3])))
     (grads,) = call(
-        weights_kernel, [shape((SIDE, 3, COLS, FW))], (*hs[0], *hs[1], *xs[0], *xs[1]), 2 * work
-    )
-    total = lax.psum_scatter(grads, AXES, axis_index_groups=groups_a()).astype(F32)
-    for half in range(2):
-        outs = call(rows_kernel, [shape((2, rows, chunk))] * SIDE, (*hs[half], ws), work)
-        home = [outs[0]] + [shift_b(outs[s], -s) for s in (1, 2, 3)]
-        split = call(to_z_kernel, [shape((2, SIDE, CAP, chunk))] * SIDE, home, 0)
-        backs += [
-            split[dz] if dz + half == 0 else shift_z(split[dz], -dz, half) for dz in range(SIDE)
-        ]
+        weights_kernel,
+        [shape((SIDE, 3, COLS, FW))],
+        (*hs[0], *hs_b, *xs[0], *xs[1]),
+        2 * work,
+    )
+    home_b, _ = send_back(1, lax.optimization_barrier((hs[1], grads))[0])
+    total = lax.psum_scatter(grads, AXES, axis_index_groups=groups_a())
+    backs = to_source(0, home_a) + to_source(1, home_b)
+    gw = call(total_kernel, [shape((1, COLS, FW), F32)] * 3, (total,), 0)
+    backs, gw = lax.optimization_barrier((backs, gw))
     mixed, gtok, gg_t = call(
         combine_kernel,
         [shape((tok, width)), shape((tok, width)), shape(ids_t.shape, F32)],
@@ -283,7 +344,7 @@
         8 * tok * tok * width,
         smem=1,
     )
-    return mixed, gtok, gg_t.T, total[:1], total[1:2], total[2:]
+    return mixed, gtok, gg_t.T, *gw
 
 
 def solution(mesh):

time: 175 us -> 156 us (0.89)
  Pallas kernels: 49 us -> 21.2 us
  waiting for transfers between devices: 42.4 us -> 51.3 us
  other arithmetic: 4.53 us -> 0.65 us
  starting transfers between devices: 55 us -> 56.9 us
    pallas_call x13 -> x14, Pallas kernels: 49 us -> 21.2 us  [call(): pl.pallas_call(kernel, out_shape=tuple(outs), in_specs=[pl.BlockSpec(memo...]
    ppermute x14, waiting for transfers between devices: 28 us -> 6.75 us  [shift_z(): lax.ppermute(v, AXES, _perm(lambda y, x, z, c: (y, x, z + dz, c + dc)))]
    ppermute x24, waiting for transfers between devices: 14.3 us -> 33.4 us  [shift_b(): lax.ppermute(v, AXES, _perm(lambda y, x, z, c: (y + s, x, z, c) if c == 0...]
    reduce_scatter x1, waiting for transfers between devices: 0.01 us -> 11.1 us  [per_device(): total = lax.psum_scatter(grads, AXES, axis_index_groups=groups_a())]
    unnamed x76 -> x30, local copies, waits for them, and re-layouts: 8.05 us -> 11.2 us
    concatenate x1 -> x0, other arithmetic: 2.4 us -> none  [per_device(): held = jnp.concatenate([w_gate, w_up, w_down], axis=0)]
    ppermute x14, starting transfers between devices: 28.8 us -> 30.9 us  [shift_z(): lax.ppermute(v, AXES, _perm(lambda y, x, z, c: (y, x, z + dz, c + dc)))]
  transfers between devices with their start and end apart: 40 -> 40, of which waited for: 15 -> 19; matrix products, arithmetic and copies ran while one was open for 0% -> 0% of each run, Pallas kernels for 24% -> 7%
where the time goes in v3:
time: 156 us; the launch traced here: 155 us
  starting transfers between devices  56.9 us (36%)
  waiting for transfers between devices  51.3 us (33%)
  Pallas kernels  21.2 us (14%)
  between operations  14.3 us (9%)
  local copies, waits for them, and re-layouts  11.2 us (7%)
    ppermute x24, waiting for transfers between devices, shift_b(): lax.ppermute(v, AXES, _perm(lambda y, x, z, c: (y + s, x, z, c) if c == 0...  33.4 us
    ppermute x14, starting transfers between devices, shift_z(): lax.ppermute(v, AXES, _perm(lambda y, x, z, c: (y, x, z + dz, c + dc)))  30.9 us
    ppermute x24, starting transfers between devices, shift_b(): lax.ppermute(v, AXES, _perm(lambda y, x, z, c: (y + s, x, z, c) if c == 0...  26 us
    pallas_call x14, Pallas kernels, call(): pl.pallas_call(kernel, out_shape=tuple(outs), in_specs=[pl.BlockSpec(memo...  21.2 us
    unnamed x30, local copies, waits for them, and re-layouts  11.2 us
    reduce_scatter x1, waiting for transfers between devices, per_device(): total = lax.psum_scatter(grads, AXES, axis_index_groups=groups_a())  11.1 us
    ppermute x14, waiting for transfers between devices, shift_z(): lax.ppermute(v, AXES, _perm(lambda y, x, z, c: (y, x, z + dz, c + dc)))  6.75 us
  transfers between devices with their start and end apart: 40, of which 19 were waited for; matrix products, arithmetic and copies ran while one was open for 0% of the time, Pallas kernels for 7%

profile of v3, /device:TPU:1, one launch (start us, length us, event | category | flops | bytes accessed | tf_op | source)
XLA Modules:
  0.0 155.5 jit_solution(3131473465702325019)
XLA Ops:
  7.2 2.3 %shard_map.121 = bf16[3,256,768]{2,1,0:T(8,128)(2,1)} custom-call(bf16[1,256,768]{2,1,0:T(8,128)(2,1)} %gate.1, bf16[1,256,768]{2,1,0:T(8,128)(2,1)} %up.1, bf16[1,256,768]{2,1,0:T(8,128)(2,1)} %down.1), custom_call_target="tpu_custom_call" | custom-call | bytes 1024 | tf_op jit(solution)/shard_map/pallas_call | solution.py:60
  10.3 4.2 %shard_map.118 = (bf16[2,4,16,1024]{3,2,1,0:T(8,128)(2,1)}, bf16[2,4,16,1024]{3,2,1,0:T(8,128)(2,1)}, bf16[2,4,16,1024]{3,2,1,0:T(8,128)(2,1)}, bf16[2,4,16,1024...) custom-call(s32[4]{0:T(128)} %pad_add_fusion.place, ...), custom_call_target="tpu_custom_call" | custom-call | flops 2684354 | bytes 1024 | tf_op jit(solution)/shard_map/pallas_call | solution.py:60
  14.5 2.5 %collective-permute-start = (bf16[2,4,16,1024]{3,2,1,0:T(8,128)(2,1)}, bf16[2,4,16,1024]{3,2,1,0:T(8,128)(2,1)S(1)}, u32[]{:S(2)}, u32[]{:S(2)}) collective-permute-start(bf16[2,4,16,1024]{3,2,1,0:T(8,128)(2,1)} %get-tuple-element.72), channel_id=1, source_target_pairs={{0,2},{1,3},{2,4},{3,5},{4,6},{5,7},{6,0},{7,1},{8,10},{9,11},{10,... | collective-permute-start | bytes 786440 | tf_op jit(solution)/shard_map/ppermute | solution.py:43
  17.1 3.3 %collective-permute-start.1 = (bf16[2,4,16,1024]{3,2,1,0:T(8,128)(2,1)}, bf16[2,4,16,1024]{3,2,1,0:T(8,128)(2,1)S(1)}, u32[]{:S(2)}, u32[]{:S(2)}) collective-permute-start(bf16[2,4,16,1024]{3,2,1,0:T(8,128)(2,1)} %get-tuple-element.73), channel_id=1, source_target_pairs={{0,4},{1,5},{2,6},{3,7},{4,0},{5,1},{6,2},{7,3},{8,12},{9,13},{10,... | collective-permute-start | bytes 786440 | tf_op jit(solution)/shard_map/ppermute | solution.py:43
  21.1 1.5 collective-permute-start.6
  23.2 2.2 %collective-permute-done.refs_1_ = bf16[2,4,16,1024]{3,2,1,0:T(8,128)(2,1)S(1)} collective-permute-done((bf16[2,4,16,1024]{3,2,1,0:T(8,128)(2,1)}, bf16[2,4,16,1024]{3,2,1,0:T(8,128)(2,1)S(1)}, u32[]{:S(2)}, u32[]{:S(2)}) %collective-permute-start) | collective-permute-done | bytes 262176 | tf_op jit(solution)/shard_map/ppermute | solution.py:43
  25.4 9.2 %collective-permute-start.8 = (bf16[2,4,16,1024]{3,2,1,0:T(8,128)(2,1)}, bf16[2,4,16,1024]{3,2,1,0:T(8,128)(2,1)S(1)}, u32[]{:S(2)}, u32[]{:S(2)}) collective-permute-start(bf16[2,4,16,1024]{3,2,1,0:T(8,128)(2,1)} %get-tuple-element.81), channel_id=1, source_target_pairs={{0,5},{1,4},{2,7},{3,6},{4,1},{5,0},{6,3},{7,2},{8,13},{9,12},{10,... | collective-permute-start | bytes 786440 | tf_op jit(solution)/shard_map/ppermute | solution.py:43
  35.6 1.3 collective-permute-start.3
  36.9 2.5 %collective-permute-start.4 = (bf16[2,64,1024]{2,1,0:T(8,128)(2,1)S(1)}, bf16[2,64,1024]{2,1,0:T(8,128)(2,1)S(1)}, u32[]{:S(2)}, u32[]{:S(2)}) collective-permute-start(bf16[2,64,1024]{2,1,0:T(8,128)(2,1)S(1)} %get-tuple-element.77), channel_id=1, source_target_pairs={{0,64},{1,17},{2,66},{3,19},{4,68},{5,21},{6,70},{7,23},{8,72},{9,... | collective-permute-start | bytes 786440 | tf_op jit(solution)/shard_map/ppermute | solution.py:37
  39.4 1.1 collective-permute-start.5
  40.5 3.5 %collective-permute-done.8.refs_2_ = bf16[2,4,16,1024]{3,2,1,0:T(8,128)(2,1)S(1)} collective-permute-done((bf16[2,4,16,1024]{3,2,1,0:T(8,128)(2,1)}, bf16[2,4,16,1024]{3,2,1,0:T(8,128)(2,1)S(1)}, u32[]{:S(2)}, u32[]{:S(2)}) %collective-permute-start.8) | collective-permute-done | bytes 262176 | tf_op jit(solution)/shard_map/ppermute | solution.py:43
  44.2 1.2 collective-permute-start.10
  45.4 2.5 %collective-permute-start.11 = (bf16[2,64,1024]{2,1,0:T(8,128)(2,1)S(1)}, bf16[2,64,1024]{2,1,0:T(8,128)(2,1)S(1)}, u32[]{:S(2)}, u32[]{:S(2)}) collective-permute-start(bf16[2,64,1024]{2,1,0:T(8,128)(2,1)S(1)} %get-tuple-element.85), channel_id=1, source_target_pairs={{0,64},{1,17},{2,66},{3,19},{4,68},{5,21},{6,70},{7,23},{8,72},{9,... | collective-permute-start | bytes 786440 | tf_op jit(solution)/shard_map/ppermute | solution.py:37
  47.9 1.1 collective-permute-start.12
  49.0 2.8 %collective-permute-done.4.refs_2_.refs_10_ = bf16[2,64,1024]{2,1,0:T(8,128)(2,1)S(1)} collective-permute-done((bf16[2,64,1024]{2,1,0:T(8,128)(2,1)S(1)}, bf16[2,64,1024]{2,1,0:T(8,128)(2,1)S(1)}, u32[]{:S(2)}, u32[]{:S(2)}) %collective-permute-start.4) | collective-permute-done | bytes 262176 | tf_op jit(solution)/shard_map/ppermute | solution.py:37
  51.8 3.4 %collective-permute-done.10.refs_5_.refs_13_ = bf16[2,64,1024]{2,1,0:T(8,128)(2,1)S(1)} collective-permute-done((bf16[2,64,1024]{2,1,0:T(8,128)(2,1)S(1)}, bf16[2,64,1024]{2,1,0:T(8,128)(2,1)S(1)}, u32[]{:S(2)}, u32[]{:S(2)}) %collective-permute-start.10) | collective-permute-done | bytes 262176 | tf_op jit(solution)/shard_map/ppermute | solution.py:37
  55.3 2.8 %collective-permute-done.11.refs_6_.refs_14_ = bf16[2,64,1024]{2,1,0:T(8,128)(2,1)S(1)} collective-permute-done((bf16[2,64,1024]{2,1,0:T(8,128)(2,1)S(1)}, bf16[2,64,1024]{2,1,0:T(8,128)(2,1)S(1)}, u32[]{:S(2)}, u32[]{:S(2)}) %collective-permute-start.11) | collective-permute-done | bytes 262176 | tf_op jit(solution)/shard_map/ppermute | solution.py:37
  58.1 2.3 %copy-done = bf16[12,256,768]{2,1,0:T(8,128)(2,1)S(1)} copy-done((bf16[12,256,768]{2,1,0:T(8,128)(2,1)S(1)}, bf16[12,256,768]{2,1,0:T(8,128)(2,1)}, u32[]{:S(2)}) %copy-start) | copy-done | bytes 4718616
  60.4 2.6 %shard_map.122 = (f32[64,2304]{1,0:T(8,128)S(1)}, bf16[64,2304]{1,0:T(8,128)(2,1)S(1)}, bf16[64,2304]{1,0:T(8,128)(2,1)S(1)}, bf16[64,2304]{1,0:T(8,128)(2,1)S(1...) custom-call(bf16[2,64,1024]{2,1,0:T(8,128)(2,1)S(1)} %get-tuple-elem, ...), custom_call_target="tpu_custom_call" | custom-call | flops 24159192 | bytes 1024 | tf_op jit(solution)/shard_map/pallas_call | solution.py:60
  63.9 1.6 %collective-permute-start.14 = (bf16[64,2304]{1,0:T(8,128)(2,1)S(1)}, bf16[64,2304]{1,0:T(8,128)(2,1)S(1)}, u32[]{:S(2)}, u32[]{:S(2)}) collective-permute-start(bf16[64,2304]{1,0:T(8,128)(2,1)S(1)} %get-tuple-element.89), channel_id=1, source_target_pairs={{0,64},{1,17},{2,66},{3,19},{4,68},{5,21},{6,70},{7,23},{8,72},{9,... | collective-permute-start | bytes 884744 | tf_op jit(solution)/shard_map/ppermute | solution.py:37
  65.9 2.3 %collective-permute-start.25 = (bf16[64,2304]{1,0:T(8,128)(2,1)S(1)}, bf16[64,2304]{1,0:T(8,128)(2,1)S(1)}, u32[]{:S(2)}, u32[]{:S(2)}) collective-permute-start(bf16[64,2304]{1,0:T(8,128)(2,1)S(1)} %get-tuple-element.100), channel_id=1, source_target_pairs={{0,96},{1,25},{2,98},{3,27},{4,100},{5,29},{6,102},{7,31},{8,104},... | collective-permute-start | bytes 884744 | tf_op jit(solution)/shard_map/ppermute | solution.py:37
  69.6 1.8 %collective-permute-done.14.p2 = bf16[64,2304]{1,0:T(8,128)(2,1)S(1)} collective-permute-done((bf16[64,2304]{1,0:T(8,128)(2,1)S(1)}, bf16[64,2304]{1,0:T(8,128)(2,1)S(1)}, u32[]{:S(2)}, u32[]{:S(2)}) %collective-permute-start.14) | collective-permute-done | bytes 294944 | tf_op jit(solution)/shard_map/ppermute | solution.py:37
  71.4 3.1 %collective-permute-done.15.p3 = bf16[64,2304]{1,0:T(8,128)(2,1)S(1)} collective-permute-done((bf16[64,2304]{1,0:T(8,128)(2,1)S(1)}, bf16[64,2304]{1,0:T(8,128)(2,1)S(1)}, u32[]{:S(2)}, u32[]{:S(2)}) %collective-permute-start.15) | collective-permute-done | bytes 294944 | tf_op jit(solution)/shard_map/ppermute | solution.py:37
  75.1 1.6 %collective-permute-start.17 = (bf16[64,2304]{1,0:T(8,128)(2,1)S(1)}, bf16[64,2304]{1,0:T(8,128)(2,1)S(1)}, u32[]{:S(2)}, u32[]{:S(2)}) collective-permute-start(bf16[64,2304]{1,0:T(8,128)(2,1)S(1)} %shard_map.123.refs_0_), channel_id=1, source_target_pairs={{0,64},{1,17},{2,66},{3,19},{4,68},{5,21},{6,70},{7,23},{8,72},{9,... | collective-permute-start | bytes 884744 | tf_op jit(solution)/shard_map/ppermute | solution.py:37
  77.7 3.1 %collective-permute-done.27.p3 = bf16[64,2304]{1,0:T(8,128)(2,1)S(1)} collective-permute-done((bf16[64,2304]{1,0:T(8,128)(2,1)S(1)}, bf16[64,2304]{1,0:T(8,128)(2,1)S(1)}, u32[]{:S(2)}, u32[]{:S(2)}) %collective-permute-start.27) | collective-permute-done | bytes 294944 | tf_op jit(solution)/shard_map/ppermute | solution.py:37
  81.5 1.6 %collective-permute-start.29 = (bf16[64,2304]{1,0:T(8,128)(2,1)S(1)}, bf16[64,2304]{1,0:T(8,128)(2,1)S(1)}, u32[]{:S(2)}, u32[]{:S(2)}) collective-permute-start(bf16[64,2304]{1,0:T(8,128)(2,1)S(1)} %shard_map.126.refs_4_.refs_0_), channel_id=1, source_target_pairs={{0,64},{1,17},{2,66},{3,19},{4,68},{5,21},{6,70},{7,23},{8,72},{9,... | collective-permute-start | bytes 884744 | tf_op jit(solution)/shard_map/ppermute | solution.py:37
  84.1 3.0 %collective-permute-done.16.refs_1_ = bf16[64,2304]{1,0:T(8,128)(2,1)S(1)} collective-permute-done((bf16[64,2304]{1,0:T(8,128)(2,1)S(1)}, bf16[64,2304]{1,0:T(8,128)(2,1)S(1)}, u32[]{:S(2)}, u32[]{:S(2)}) %collective-permute-start.16) | collective-permute-done | bytes 294944 | tf_op jit(solution)/shard_map/ppermute | solution.py:37
  87.1 1.4 shard_map.124
  89.7 1.1 collective-permute-start.21
  90.7 2.7 %collective-permute-done.28.refs_5_.refs_1_ = bf16[64,2304]{1,0:T(8,128)(2,1)S(1)} collective-permute-done((bf16[64,2304]{1,0:T(8,128)(2,1)S(1)}, bf16[64,2304]{1,0:T(8,128)(2,1)S(1)}, u32[]{:S(2)}, u32[]{:S(2)}) %collective-permute-start.28) | collective-permute-done | bytes 294944 | tf_op jit(solution)/shard_map/ppermute | solution.py:37
  93.4 1.3 collective-permute-done.19.refs_1_
  97.1 2.6 %shard_map.127 = bf16[4,3,256,768]{3,2,1,0:T(8,128)(2,1)S(1)} custom-call(bf16[64,2304]{1,0:T(8,128)(2,1)S(1)} %shard_map.123.refs_0_, bf16[64,2304]{1,0:T(8,128)(2,1)S(1)} %collective-permute-done.16.refs_1_, bf16[64,2304]{1,0:T(8,128)(2,1)S(1)} %collective-permute-done.17.refs_2_, bf16[64,2304]{1,0:T(8,128)(2,1)S(1)} %collective-permute-done.18.refs_3_, ...), custom_call_target="tpu_custom_call" | custom-call | flops 24159192 | bytes 1024 | tf_op jit(solution)/shard_map/pallas_call | solution.py:60
  99.8 2.2 %copy-done.3 = bf16[4,3,256,768]{3,2,1,0:T(8,128)(2,1)} copy-done((bf16[4,3,256,768]{3,2,1,0:T(8,128)(2,1)}, bf16[4,3,256,768]{3,2,1,0:T(8,128)(2,1)S(1)}, u32[]{:S(2)}) %copy-start.3) | copy-done | bytes 4718616
  102.0 1.4 collective-permute-start.20
  103.4 2.3 %copy-done.2 = bf16[12,256,768]{2,1,0:T(8,128)(2,1)S(1)} copy-done((bf16[12,256,768]{2,1,0:T(8,128)(2,1)S(1)}, bf16[12,256,768]{2,1,0:T(8,128)(2,1)}, u32[]{:S(2)}) %copy-start.2) | copy-done | bytes 4718616
  105.7 1.4 shard_map.128
  107.1 1.2 collective-permute-start.31
  109.8 2.8 %collective-permute-start.22 = (bf16[2,4,16,1024]{3,2,1,0:T(8,128)(2,1)S(1)}, bf16[2,4,16,1024]{3,2,1,0:T(8,128)(2,1)S(1)}, u32[]{:S(2)}, u32[]{:S(2)}) collective-permute-start(bf16[2,4,16,1024]{3,2,1,0:T(8,128)(2,1)S(1)} %get-tuple-element.96), channel_id=1, source_target_pairs={{0,6},{1,7},{2,0},{3,1},{4,2},{5,3},{6,4},{7,5},{8,14},{9,15},{10,... | collective-permute-start | bytes 786440 | tf_op jit(solution)/shard_map/ppermute | solution.py:43
  113.1 1.1 collective-permute-start.24
  114.1 1.1 collective-permute-done.32.refs_2_
  115.2 5.4 %collective-permute-done.33.refs_3_ = bf16[2,64,1024]{2,1,0:T(8,128)(2,1)S(1)} collective-permute-done((bf16[2,64,1024]{2,1,0:T(8,128)(2,1)S(1)}, bf16[2,64,1024]{2,1,0:T(8,128)(2,1)S(1)}, u32[]{:S(2)}, u32[]{:S(2)}) %collective-permute-start.33) | collective-permute-done | bytes 262176 | tf_op jit(solution)/shard_map/ppermute | solution.py:37
  120.6 1.0 shard_map.129
  121.7 4.8 %collective-permute-start.34 = (bf16[2,4,16,1024]{3,2,1,0:T(8,128)(2,1)}, bf16[2,4,16,1024]{3,2,1,0:T(8,128)(2,1)S(1)}, u32[]{:S(2)}, u32[]{:S(2)}) collective-permute-start(bf16[2,4,16,1024]{3,2,1,0:T(8,128)(2,1)} %get-tuple-element.115), channel_id=1, source_target_pairs={{0,1},{1,0},{2,3},{3,2},{4,5},{5,4},{6,7},{7,6},{8,9},{9,8},{10,11... | collective-permute-start | bytes 786440 | tf_op jit(solution)/shard_map/ppermute | solution.py:43
  126.4 2.8 %collective-permute-start.35 = (bf16[2,4,16,1024]{3,2,1,0:T(8,128)(2,1)}, bf16[2,4,16,1024]{3,2,1,0:T(8,128)(2,1)S(1)}, u32[]{:S(2)}, u32[]{:S(2)}) collective-permute-start(bf16[2,4,16,1024]{3,2,1,0:T(8,128)(2,1)} %get-tuple-element.116), channel_id=1, source_target_pairs={{0,7},{1,6},{2,1},{3,0},{4,3},{5,2},{6,5},{7,4},{8,15},{9,14},{10,... | collective-permute-start | bytes 786440 | tf_op jit(solution)/shard_map/ppermute | solution.py:43
  130.3 11.1 %reduce-scatter.2.cloned.1.call-done = bf16[1,3,256,768]{3,2,1,0:T(8,128)(2,1)} async-done(((bf16[4,3,256,768]{3,2,1,0:T(8,128)(2,1)}), bf16[1,3,256,768]{3,2,1,0:T(8,128)(2,1)}) %reduce-scatter.2.cloned.1.call-update) | async-done | bytes 1179664 | tf_op jit(solution)/shard_map/reduce_scatter | solution.py:336
  141.4 1.3 copy-done.5
  142.7 1.5 shard_map.130
  145.2 3.4 %shard_map.131 = (bf16[128,4096]{1,0:T(8,128)(2,1)}, bf16[128,4096]{1,0:T(8,128)(2,1)}, f32[8,128]{1,0:T(8,128)}) custom-call(s32[4]{0:T(128)S(1)} %copy-done.13, s32[8,128]{1,0:T(8,128)S(1)} %bitcast.14, f32[8,128]{1,0:T(8,128)S(1)} %bitcast.16, bf16[128,4096]{1,0:T(8,128)(2,1)S(1)} %copy-done.4, bf16[2,4,16,1024]{3,2,1,0:T(8,128)(2,1)S(1)} %get-tuple-element.122.refs_0_, ...), custom_call_target="tpu_custom_call" | custom-call | flops 5368709 | bytes 1024 | tf_op jit(solution)/shard_map/pallas_call | solution.py:60
  (79 shorter events, 16.8 us)
Async XLA Ops:
  7.2 50.9 %all-gather.3.cloned.1.call-start = ((), (), s32[]{:S(2)}) async-start(), calls=%async_computation.2 | async-start | bytes 5898240 | tf_op jit(solution)/shard_map/all_gather | solution.py:281
  9.5 131.9 %reduce-scatter.2.cloned.1.call-start = ((), (), s32[]{:S(2)}) async-start(), calls=%async_computation.1 | async-start | bytes 5898240 | tf_op jit(solution)/shard_map/reduce_scatter | solution.py:336
  14.5 10.9 %collective-permute-start = (bf16[2,4,16,1024]{3,2,1,0:T(8,128)(2,1)}, bf16[2,4,16,1024]{3,2,1,0:T(8,128)(2,1)S(1)}, u32[]{:S(2)}, u32[]{:S(2)}) collective-permute-start(bf16[2,4,16,1024]{3,2,1,0:T(8,128)(2,1)} %get-tuple-element.72), channel_id=1, source_target_pairs={{0,2},{1,3},{2,4},{3,5},{4,6},{5,7},{6,0},{7,1},{8,10},{9,11},{10,... | collective-permute-start | bytes 786440 | tf_op jit(solution)/shard_map/ppermute | solution.py:43
  17.1 17.5 %collective-permute-start.1 = (bf16[2,4,16,1024]{3,2,1,0:T(8,128)(2,1)}, bf16[2,4,16,1024]{3,2,1,0:T(8,128)(2,1)S(1)}, u32[]{:S(2)}, u32[]{:S(2)}) collective-permute-start(bf16[2,4,16,1024]{3,2,1,0:T(8,128)(2,1)} %get-tuple-element.73), channel_id=1, source_target_pairs={{0,4},{1,5},{2,6},{3,7},{4,0},{5,1},{6,2},{7,3},{8,12},{9,13},{10,... | collective-permute-start | bytes 786440 | tf_op jit(solution)/shard_map/ppermute | solution.py:43
  20.4 14.2 %collective-permute-start.2 = (bf16[2,4,16,1024]{3,2,1,0:T(8,128)(2,1)}, bf16[2,4,16,1024]{3,2,1,0:T(8,128)(2,1)S(1)}, u32[]{:S(2)}, u32[]{:S(2)}) collective-permute-start(bf16[2,4,16,1024]{3,2,1,0:T(8,128)(2,1)} %get-tuple-element.74), channel_id=1, source_target_pairs={{0,6},{1,7},{2,0},{3,1},{4,2},{5,3},{6,4},{7,5},{8,14},{9,15},{10,... | collective-permute-start | bytes 786440 | tf_op jit(solution)/shard_map/ppermute | solution.py:43
  21.1 15.8 %collective-permute-start.6 = (bf16[2,4,16,1024]{3,2,1,0:T(8,128)(2,1)}, bf16[2,4,16,1024]{3,2,1,0:T(8,128)(2,1)S(1)}, u32[]{:S(2)}, u32[]{:S(2)}) collective-permute-start(bf16[2,4,16,1024]{3,2,1,0:T(8,128)(2,1)} %get-tuple-element.79), channel_id=1, source_target_pairs={{0,1},{1,0},{2,3},{3,2},{4,5},{5,4},{6,7},{7,6},{8,9},{9,8},{10,11... | collective-permute-start | bytes 786440 | tf_op jit(solution)/shard_map/ppermute | solution.py:43
  22.6 16.8 %collective-permute-start.7 = (bf16[2,4,16,1024]{3,2,1,0:T(8,128)(2,1)}, bf16[2,4,16,1024]{3,2,1,0:T(8,128)(2,1)S(1)}, u32[]{:S(2)}, u32[]{:S(2)}) collective-permute-start(bf16[2,4,16,1024]{3,2,1,0:T(8,128)(2,1)} %get-tuple-element.80), channel_id=1, source_target_pairs={{0,3},{1,2},{2,5},{3,4},{4,7},{5,6},{6,1},{7,0},{8,11},{9,10},{10,... | collective-permute-start | bytes 786440 | tf_op jit(solution)/shard_map/ppermute | solution.py:43
  25.4 18.7 %collective-permute-start.8 = (bf16[2,4,16,1024]{3,2,1,0:T(8,128)(2,1)}, bf16[2,4,16,1024]{3,2,1,0:T(8,128)(2,1)S(1)}, u32[]{:S(2)}, u32[]{:S(2)}) collective-permute-start(bf16[2,4,16,1024]{3,2,1,0:T(8,128)(2,1)} %get-tuple-element.81), channel_id=1, source_target_pairs={{0,5},{1,4},{2,7},{3,6},{4,1},{5,0},{6,3},{7,2},{8,13},{9,12},{10,... | collective-permute-start | bytes 786440 | tf_op jit(solution)/shard_map/ppermute | solution.py:43
  34.6 9.5 %collective-permute-start.9 = (bf16[2,4,16,1024]{3,2,1,0:T(8,128)(2,1)}, bf16[2,4,16,1024]{3,2,1,0:T(8,128)(2,1)S(1)}, u32[]{:S(2)}, u32[]{:S(2)}) collective-permute-start(bf16[2,4,16,1024]{3,2,1,0:T(8,128)(2,1)} %get-tuple-element.82), channel_id=1, source_target_pairs={{0,7},{1,6},{2,1},{3,0},{4,3},{5,2},{6,5},{7,4},{8,15},{9,14},{10,... | collective-permute-start | bytes 786440 | tf_op jit(solution)/shard_map/ppermute | solution.py:43
  35.6 12.2 %collective-permute-start.3 = (bf16[2,64,1024]{2,1,0:T(8,128)(2,1)S(1)}, bf16[2,64,1024]{2,1,0:T(8,128)(2,1)S(1)}, u32[]{:S(2)}, u32[]{:S(2)}) collective-permute-start(bf16[2,64,1024]{2,1,0:T(8,128)(2,1)S(1)} %get-tuple-element.76), channel_id=1, source_target_pairs={{0,32},{1,9},{2,34},{3,11},{4,36},{5,13},{6,38},{7,15},{8,40},{9,1... | collective-permute-start | bytes 786440 | tf_op jit(solution)/shard_map/ppermute | solution.py:37
  36.9 14.9 %collective-permute-start.4 = (bf16[2,64,1024]{2,1,0:T(8,128)(2,1)S(1)}, bf16[2,64,1024]{2,1,0:T(8,128)(2,1)S(1)}, u32[]{:S(2)}, u32[]{:S(2)}) collective-permute-start(bf16[2,64,1024]{2,1,0:T(8,128)(2,1)S(1)} %get-tuple-element.77), channel_id=1, source_target_pairs={{0,64},{1,17},{2,66},{3,19},{4,68},{5,21},{6,70},{7,23},{8,72},{9,... | collective-permute-start | bytes 786440 | tf_op jit(solution)/shard_map/ppermute | solution.py:37
  39.4 12.5 %collective-permute-start.5 = (bf16[2,64,1024]{2,1,0:T(8,128)(2,1)S(1)}, bf16[2,64,1024]{2,1,0:T(8,128)(2,1)S(1)}, u32[]{:S(2)}, u32[]{:S(2)}) collective-permute-start(bf16[2,64,1024]{2,1,0:T(8,128)(2,1)S(1)} %get-tuple-element.78), channel_id=1, source_target_pairs={{0,96},{1,25},{2,98},{3,27},{4,100},{5,29},{6,102},{7,31},{8,104},... | collective-permute-start | bytes 786440 | tf_op jit(solution)/shard_map/ppermute | solution.py:37
  44.2 11.1 %collective-permute-start.10 = (bf16[2,64,1024]{2,1,0:T(8,128)(2,1)S(1)}, bf16[2,64,1024]{2,1,0:T(8,128)(2,1)S(1)}, u32[]{:S(2)}, u32[]{:S(2)}) collective-permute-start(bf16[2,64,1024]{2,1,0:T(8,128)(2,1)S(1)} %get-tuple-element.84), channel_id=1, source_target_pairs={{0,32},{1,9},{2,34},{3,11},{4,36},{5,13},{6,38},{7,15},{8,40},{9,1... | collective-permute-start | bytes 786440 | tf_op jit(solution)/shard_map/ppermute | solution.py:37
  45.4 12.7 %collective-permute-start.11 = (bf16[2,64,1024]{2,1,0:T(8,128)(2,1)S(1)}, bf16[2,64,1024]{2,1,0:T(8,128)(2,1)S(1)}, u32[]{:S(2)}, u32[]{:S(2)}) collective-permute-start(bf16[2,64,1024]{2,1,0:T(8,128)(2,1)S(1)} %get-tuple-element.85), channel_id=1, source_target_pairs={{0,64},{1,17},{2,66},{3,19},{4,68},{5,21},{6,70},{7,23},{8,72},{9,... | collective-permute-start | bytes 786440 | tf_op jit(solution)/shard_map/ppermute | solution.py:37
  47.9 10.2 %collective-permute-start.12 = (bf16[2,64,1024]{2,1,0:T(8,128)(2,1)S(1)}, bf16[2,64,1024]{2,1,0:T(8,128)(2,1)S(1)}, u32[]{:S(2)}, u32[]{:S(2)}) collective-permute-start(bf16[2,64,1024]{2,1,0:T(8,128)(2,1)S(1)} %get-tuple-element.86), channel_id=1, source_target_pairs={{0,96},{1,25},{2,98},{3,27},{4,100},{5,29},{6,102},{7,31},{8,104},... | collective-permute-start | bytes 786440 | tf_op jit(solution)/shard_map/ppermute | solution.py:37
  58.1 2.3 %copy-start = (bf16[12,256,768]{2,1,0:T(8,128)(2,1)S(1)}, bf16[12,256,768]{2,1,0:T(8,128)(2,1)}, u32[]{:S(2)}) copy-start(bf16[12,256,768]{2,1,0:T(8,128)(2,1)} %all-gather.3.cloned.1.call-done) | copy-start | bytes 14155780
  60.4 26.7 %copy-start.1 = (bf16[12,256,768]{2,1,0:T(8,128)(2,1)S(1)}, bf16[12,256,768]{2,1,0:T(8,128)(2,1)}, u32[]{:S(2)}) copy-start(bf16[12,256,768]{2,1,0:T(8,128)(2,1)} %all-gather.3.cloned.1.call-done) | copy-start | bytes 14155780
  63.0 5.9 %collective-permute-start.13 = (bf16[64,2304]{1,0:T(8,128)(2,1)S(1)}, bf16[64,2304]{1,0:T(8,128)(2,1)S(1)}, u32[]{:S(2)}, u32[]{:S(2)}) collective-permute-start(bf16[64,2304]{1,0:T(8,128)(2,1)S(1)} %get-tuple-element.88), channel_id=1, source_target_pairs={{0,96},{1,25},{2,98},{3,27},{4,100},{5,29},{6,102},{7,31},{8,104},... | collective-permute-start | bytes 884744 | tf_op jit(solution)/shard_map/ppermute | solution.py:37
  63.9 7.4 %collective-permute-start.14 = (bf16[64,2304]{1,0:T(8,128)(2,1)S(1)}, bf16[64,2304]{1,0:T(8,128)(2,1)S(1)}, u32[]{:S(2)}, u32[]{:S(2)}) collective-permute-start(bf16[64,2304]{1,0:T(8,128)(2,1)S(1)} %get-tuple-element.89), channel_id=1, source_target_pairs={{0,64},{1,17},{2,66},{3,19},{4,68},{5,21},{6,70},{7,23},{8,72},{9,... | collective-permute-start | bytes 884744 | tf_op jit(solution)/shard_map/ppermute | solution.py:37
  65.5 9.0 %collective-permute-start.15 = (bf16[64,2304]{1,0:T(8,128)(2,1)S(1)}, bf16[64,2304]{1,0:T(8,128)(2,1)S(1)}, u32[]{:S(2)}, u32[]{:S(2)}) collective-permute-start(bf16[64,2304]{1,0:T(8,128)(2,1)S(1)} %get-tuple-element.90), channel_id=1, source_target_pairs={{0,32},{1,9},{2,34},{3,11},{4,36},{5,13},{6,38},{7,15},{8,40},{9,1... | collective-permute-start | bytes 884744 | tf_op jit(solution)/shard_map/ppermute | solution.py:37
  65.9 10.8 %collective-permute-start.25 = (bf16[64,2304]{1,0:T(8,128)(2,1)S(1)}, bf16[64,2304]{1,0:T(8,128)(2,1)S(1)}, u32[]{:S(2)}, u32[]{:S(2)}) collective-permute-start(bf16[64,2304]{1,0:T(8,128)(2,1)S(1)} %get-tuple-element.100), channel_id=1, source_target_pairs={{0,96},{1,25},{2,98},{3,27},{4,100},{5,29},{6,102},{7,31},{8,104},... | collective-permute-start | bytes 884744 | tf_op jit(solution)/shard_map/ppermute | solution.py:37
  68.2 9.5 %collective-permute-start.26 = (bf16[64,2304]{1,0:T(8,128)(2,1)S(1)}, bf16[64,2304]{1,0:T(8,128)(2,1)S(1)}, u32[]{:S(2)}, u32[]{:S(2)}) collective-permute-start(bf16[64,2304]{1,0:T(8,128)(2,1)S(1)} %get-tuple-element.101), channel_id=1, source_target_pairs={{0,64},{1,17},{2,66},{3,19},{4,68},{5,21},{6,70},{7,23},{8,72},{9,... | collective-permute-start | bytes 884744 | tf_op jit(solution)/shard_map/ppermute | solution.py:37
  69.0 11.8 %collective-permute-start.27 = (bf16[64,2304]{1,0:T(8,128)(2,1)S(1)}, bf16[64,2304]{1,0:T(8,128)(2,1)S(1)}, u32[]{:S(2)}, u32[]{:S(2)}) collective-permute-start(bf16[64,2304]{1,0:T(8,128)(2,1)S(1)} %get-tuple-element.102), channel_id=1, source_target_pairs={{0,32},{1,9},{2,34},{3,11},{4,36},{5,13},{6,38},{7,15},{8,40},{9,1... | collective-permute-start | bytes 884744 | tf_op jit(solution)/shard_map/ppermute | solution.py:37
  74.7 8.3 %collective-permute-start.18 = (bf16[64,2304]{1,0:T(8,128)(2,1)S(1)}, bf16[64,2304]{1,0:T(8,128)(2,1)S(1)}, u32[]{:S(2)}, u32[]{:S(2)}) collective-permute-start(bf16[64,2304]{1,0:T(8,128)(2,1)S(1)} %shard_map.123.refs_0_), channel_id=1, source_target_pairs={{0,96},{1,25},{2,98},{3,27},{4,100},{5,29},{6,102},{7,31},{8,104},... | collective-permute-start | bytes 884744 | tf_op jit(solution)/shard_map/ppermute | solution.py:37
  75.1 9.0 %collective-permute-start.17 = (bf16[64,2304]{1,0:T(8,128)(2,1)S(1)}, bf16[64,2304]{1,0:T(8,128)(2,1)S(1)}, u32[]{:S(2)}, u32[]{:S(2)}) collective-permute-start(bf16[64,2304]{1,0:T(8,128)(2,1)S(1)} %shard_map.123.refs_0_), channel_id=1, source_target_pairs={{0,64},{1,17},{2,66},{3,19},{4,68},{5,21},{6,70},{7,23},{8,72},{9,... | collective-permute-start | bytes 884744 | tf_op jit(solution)/shard_map/ppermute | solution.py:37
  76.7 10.5 %collective-permute-start.16 = (bf16[64,2304]{1,0:T(8,128)(2,1)S(1)}, bf16[64,2304]{1,0:T(8,128)(2,1)S(1)}, u32[]{:S(2)}, u32[]{:S(2)}) collective-permute-start(bf16[64,2304]{1,0:T(8,128)(2,1)S(1)} %shard_map.123.refs_0_), channel_id=1, source_target_pairs={{0,32},{1,9},{2,34},{3,11},{4,36},{5,13},{6,38},{7,15},{8,40},{9,1... | collective-permute-start | bytes 884744 | tf_op jit(solution)/shard_map/ppermute | solution.py:37
  81.0 9.7 %collective-permute-start.30 = (bf16[64,2304]{1,0:T(8,128)(2,1)S(1)}, bf16[64,2304]{1,0:T(8,128)(2,1)S(1)}, u32[]{:S(2)}, u32[]{:S(2)}) collective-permute-start(bf16[64,2304]{1,0:T(8,128)(2,1)S(1)} %shard_map.126.refs_4_.refs_0_), channel_id=1, source_target_pairs={{0,96},{1,25},{2,98},{3,27},{4,100},{5,29},{6,102},{7,31},{8,104},... | collective-permute-start | bytes 884744 | tf_op jit(solution)/shard_map/ppermute | solution.py:37
  81.5 9.3 %collective-permute-start.29 = (bf16[64,2304]{1,0:T(8,128)(2,1)S(1)}, bf16[64,2304]{1,0:T(8,128)(2,1)S(1)}, u32[]{:S(2)}, u32[]{:S(2)}) collective-permute-start(bf16[64,2304]{1,0:T(8,128)(2,1)S(1)} %shard_map.126.refs_4_.refs_0_), channel_id=1, source_target_pairs={{0,64},{1,17},{2,66},{3,19},{4,68},{5,21},{6,70},{7,23},{8,72},{9,... | collective-permute-start | bytes 884744 | tf_op jit(solution)/shard_map/ppermute | solution.py:37
  83.0 10.4 %collective-permute-start.28 = (bf16[64,2304]{1,0:T(8,128)(2,1)S(1)}, bf16[64,2304]{1,0:T(8,128)(2,1)S(1)}, u32[]{:S(2)}, u32[]{:S(2)}) collective-permute-start(bf16[64,2304]{1,0:T(8,128)(2,1)S(1)} %shard_map.126.refs_4_.refs_0_), channel_id=1, source_target_pairs={{0,32},{1,9},{2,34},{3,11},{4,36},{5,13},{6,38},{7,15},{8,40},{9,1... | collective-permute-start | bytes 884744 | tf_op jit(solution)/shard_map/ppermute | solution.py:37
  89.2 5.5 %collective-permute-start.19 = (bf16[2,64,1024]{2,1,0:T(8,128)(2,1)S(1)}, bf16[2,64,1024]{2,1,0:T(8,128)(2,1)S(1)}, u32[]{:S(2)}, u32[]{:S(2)}) collective-permute-start(bf16[2,64,1024]{2,1,0:T(8,128)(2,1)S(1)} %get-tuple-element.92), channel_id=1, source_target_pairs={{0,96},{1,25},{2,98},{3,27},{4,100},{5,29},{6,102},{7,31},{8,104},... | collective-permute-start | bytes 786440 | tf_op jit(solution)/shard_map/ppermute | solution.py:37
  89.7 6.7 %collective-permute-start.21 = (bf16[2,64,1024]{2,1,0:T(8,128)(2,1)S(1)}, bf16[2,64,1024]{2,1,0:T(8,128)(2,1)S(1)}, u32[]{:S(2)}, u32[]{:S(2)}) collective-permute-start(bf16[2,64,1024]{2,1,0:T(8,128)(2,1)S(1)} %get-tuple-element.94), channel_id=1, source_target_pairs={{0,32},{1,9},{2,34},{3,11},{4,36},{5,13},{6,38},{7,15},{8,40},{9,1... | collective-permute-start | bytes 786440 | tf_op jit(solution)/shard_map/ppermute | solution.py:37
  101.9 7.8 %copy-start.7 = (bf16[2,64,1024]{2,1,0:T(8,128)(2,1)S(1)}, bf16[2,64,1024]{2,1,0:T(8,128)(2,1)}, u32[]{:S(2)}) copy-start(bf16[2,64,1024]{2,1,0:T(8,128)(2,1)} %copy-done.6) | copy-start | bytes 786436
  101.9 7.8 %copy-start.9 = (bf16[2,64,1024]{2,1,0:T(8,128)(2,1)S(1)}, bf16[2,64,1024]{2,1,0:T(8,128)(2,1)}, u32[]{:S(2)}) copy-start(bf16[2,64,1024]{2,1,0:T(8,128)(2,1)} %copy-done.8) | copy-start | bytes 786436
  101.9 43.3 %copy-start.4 = (bf16[128,4096]{1,0:T(8,128)(2,1)S(1)}, bf16[128,4096]{1,0:T(8,128)(2,1)}, u32[]{:S(2)}) copy-start(bf16[128,4096]{1,0:T(8,128)(2,1)} %cotangent.3) | copy-start | bytes 3145732
  101.9 43.3 %copy-start.11 = (s32[128,8]{0,1:T(8,128)S(1)}, s32[128,8]{0,1:T(8,128)}, u32[]{:S(2)}) copy-start(s32[128,8]{0,1:T(8,128)} %param.8) | copy-start | bytes 12292
  101.9 43.3 %copy-start.12 = (f32[128,8]{0,1:T(8,128)S(1)}, f32[128,8]{0,1:T(8,128)}, u32[]{:S(2)}) copy-start(f32[128,8]{0,1:T(8,128)} %param.9) | copy-start | bytes 12292
  102.0 43.2 %copy-start.13 = (s32[4]{0:T(128)S(1)}, s32[4]{0:T(128)}, u32[]{:S(2)}) copy-start(s32[4]{0:T(128)} %pad_add_fusion.place) | copy-start | bytes 52
  102.0 7.7 %collective-permute-start.20 = (bf16[2,64,1024]{2,1,0:T(8,128)(2,1)}, bf16[2,64,1024]{2,1,0:T(8,128)(2,1)S(1)}, u32[]{:S(2)}, u32[]{:S(2)}) collective-permute-start(bf16[2,64,1024]{2,1,0:T(8,128)(2,1)} %copy-done.14), channel_id=1, source_target_pairs={{0,64},{1,17},{2,66},{3,19},{4,68},{5,21},{6,70},{7,23},{8,72},{9,... | collective-permute-start | bytes 786440 | tf_op jit(solution)/shard_map/ppermute | solution.py:37
  107.1 5.9 %collective-permute-start.31 = (bf16[2,64,1024]{2,1,0:T(8,128)(2,1)S(1)}, bf16[2,64,1024]{2,1,0:T(8,128)(2,1)S(1)}, u32[]{:S(2)}, u32[]{:S(2)}) collective-permute-start(bf16[2,64,1024]{2,1,0:T(8,128)(2,1)S(1)} %get-tuple-element.112), channel_id=1, source_target_pairs={{0,96},{1,25},{2,98},{3,27},{4,100},{5,29},{6,102},{7,31},{8,104},... | collective-permute-start | bytes 786440 | tf_op jit(solution)/shard_map/ppermute | solution.py:37
  108.4 6.8 %collective-permute-start.32 = (bf16[2,64,1024]{2,1,0:T(8,128)(2,1)S(1)}, bf16[2,64,1024]{2,1,0:T(8,128)(2,1)S(1)}, u32[]{:S(2)}, u32[]{:S(2)}) collective-permute-start(bf16[2,64,1024]{2,1,0:T(8,128)(2,1)S(1)} %get-tuple-element.113), channel_id=1, source_target_pairs={{0,64},{1,17},{2,66},{3,19},{4,68},{5,21},{6,70},{7,23},{8,72},{9,... | collective-permute-start | bytes 786440 | tf_op jit(solution)/shard_map/ppermute | solution.py:37
  109.0 11.7 %collective-permute-start.33 = (bf16[2,64,1024]{2,1,0:T(8,128)(2,1)S(1)}, bf16[2,64,1024]{2,1,0:T(8,128)(2,1)S(1)}, u32[]{:S(2)}, u32[]{:S(2)}) collective-permute-start(bf16[2,64,1024]{2,1,0:T(8,128)(2,1)S(1)} %get-tuple-element.114), channel_id=1, source_target_pairs={{0,32},{1,9},{2,34},{3,11},{4,36},{5,13},{6,38},{7,15},{8,40},{9,1... | collective-permute-start | bytes 786440 | tf_op jit(solution)/shard_map/ppermute | solution.py:37
  109.8 19.4 %collective-permute-start.22 = (bf16[2,4,16,1024]{3,2,1,0:T(8,128)(2,1)S(1)}, bf16[2,4,16,1024]{3,2,1,0:T(8,128)(2,1)S(1)}, u32[]{:S(2)}, u32[]{:S(2)}) collective-permute-start(bf16[2,4,16,1024]{3,2,1,0:T(8,128)(2,1)S(1)} %get-tuple-element.96), channel_id=1, source_target_pairs={{0,6},{1,7},{2,0},{3,1},{4,2},{5,3},{6,4},{7,5},{8,14},{9,15},{10,... | collective-permute-start | bytes 786440 | tf_op jit(solution)/shard_map/ppermute | solution.py:43
  112.6 17.4 %collective-permute-start.23 = (bf16[2,4,16,1024]{3,2,1,0:T(8,128)(2,1)S(1)}, bf16[2,4,16,1024]{3,2,1,0:T(8,128)(2,1)S(1)}, u32[]{:S(2)}, u32[]{:S(2)}) collective-permute-start(bf16[2,4,16,1024]{3,2,1,0:T(8,128)(2,1)S(1)} %get-tuple-element.97), channel_id=1, source_target_pairs={{0,4},{1,5},{2,6},{3,7},{4,0},{5,1},{6,2},{7,3},{8,12},{9,13},{10,... | collective-permute-start | bytes 786440 | tf_op jit(solution)/shard_map/ppermute | solution.py:43
  113.1 31.1 %collective-permute-start.24 = (bf16[2,4,16,1024]{3,2,1,0:T(8,128)(2,1)S(1)}, bf16[2,4,16,1024]{3,2,1,0:T(8,128)(2,1)S(1)}, u32[]{:S(2)}, u32[]{:S(2)}) collective-permute-start(bf16[2,4,16,1024]{3,2,1,0:T(8,128)(2,1)S(1)} %get-tuple-element.98), channel_id=1, source_target_pairs={{0,2},{1,3},{2,4},{3,5},{4,6},{5,7},{6,0},{7,1},{8,10},{9,11},{10,... | collective-permute-start | bytes 786440 | tf_op jit(solution)/shard_map/ppermute | solution.py:43
  121.7 22.5 %collective-permute-start.34 = (bf16[2,4,16,1024]{3,2,1,0:T(8,128)(2,1)}, bf16[2,4,16,1024]{3,2,1,0:T(8,128)(2,1)S(1)}, u32[]{:S(2)}, u32[]{:S(2)}) collective-permute-start(bf16[2,4,16,1024]{3,2,1,0:T(8,128)(2,1)} %get-tuple-element.115), channel_id=1, source_target_pairs={{0,1},{1,0},{2,3},{3,2},{4,5},{5,4},{6,7},{7,6},{8,9},{9,8},{10,11... | collective-permute-start | bytes 786440 | tf_op jit(solution)/shard_map/ppermute | solution.py:43
  126.4 17.8 %collective-permute-start.35 = (bf16[2,4,16,1024]{3,2,1,0:T(8,128)(2,1)}, bf16[2,4,16,1024]{3,2,1,0:T(8,128)(2,1)S(1)}, u32[]{:S(2)}, u32[]{:S(2)}) collective-permute-start(bf16[2,4,16,1024]{3,2,1,0:T(8,128)(2,1)} %get-tuple-element.116), channel_id=1, source_target_pairs={{0,7},{1,6},{2,1},{3,0},{4,3},{5,2},{6,5},{7,4},{8,15},{9,14},{10,... | collective-permute-start | bytes 786440 | tf_op jit(solution)/shard_map/ppermute | solution.py:43
  129.2 15.0 %collective-permute-start.36 = (bf16[2,4,16,1024]{3,2,1,0:T(8,128)(2,1)}, bf16[2,4,16,1024]{3,2,1,0:T(8,128)(2,1)S(1)}, u32[]{:S(2)}, u32[]{:S(2)}) collective-permute-start(bf16[2,4,16,1024]{3,2,1,0:T(8,128)(2,1)} %get-tuple-element.117), channel_id=1, source_target_pairs={{0,5},{1,4},{2,7},{3,6},{4,1},{5,0},{6,3},{7,2},{8,13},{9,12},{10,... | collective-permute-start | bytes 786440 | tf_op jit(solution)/shard_map/ppermute | solution.py:43
  130.1 15.1 %collective-permute-start.37 = (bf16[2,4,16,1024]{3,2,1,0:T(8,128)(2,1)}, bf16[2,4,16,1024]{3,2,1,0:T(8,128)(2,1)S(1)}, u32[]{:S(2)}, u32[]{:S(2)}) collective-permute-start(bf16[2,4,16,1024]{3,2,1,0:T(8,128)(2,1)} %get-tuple-element.118), channel_id=1, source_target_pairs={{0,3},{1,2},{2,5},{3,4},{4,7},{5,6},{6,1},{7,0},{8,11},{9,10},{10,... | collective-permute-start | bytes 786440 | tf_op jit(solution)/shard_map/ppermute | solution.py:43
  (7 other events, 8.9 us)
Sparse Core Ops, SparseCore 0:
  9.7 44.3 all-gather.2
  102.1 39.2 reduce-scatter.1

commit v4 on v3

--- a/solution.py
+++ b/solution.py
@@ -1,3 +1,5 @@
+import functools
+
 import jax
 import jax.numpy as jnp
 from jax import lax
@@ -109,35 +111,30 @@
         pltpu.make_async_copy(ids, ids_v, sem.at[0]),
         pltpu.make_async_copy(gates, gates_v, sem.at[1]),
     ]
-    wide, quarter = [], tokens.shape[1] // SIDE
-    for q in range(SIDE):
-        cols = slice(q * quarter, q * quarter + quarter)
-        wide.append(
-            (
-                pltpu.make_async_copy(tokens.at[:, cols], tok_v.at[q], sem.at[2 + 2 * q]),
-                pltpu.make_async_copy(cotangent.at[:, cols], cot_v.at[q], sem.at[3 + 2 * q]),
-            )
-        )
-    for copy in small + [c for pair in wide for c in pair]:
+    part = tokens.shape[0] // SIDE
+    wide = []
+    for k, (src, dst) in enumerate(((tokens, tok_v), (cotangent, cot_v))):
+        for q in range(SIDE):
+            at = pl.ds(q * part, part)
+            wide.append(pltpu.make_async_copy(src.at[at], dst.at[at], sem.at[2 + SIDE * k + q]))
+    for copy in small + wide:
         copy.start()
     for copy in small:
         copy.wait()
     _, chosen, scale = routing(place, ids_v[...], gates_v[...])
     chosen = chosen.astype(BF)
-    for blk in range(16):
-        q, cols = blk // 4, slice(blk % 4 * COLS, blk % 4 * COLS + COLS)
-        if blk % 4 == 0:
-            for copy in wide[q]:
-                copy.wait()
-        rows = dot(chosen, tok_v[q, :, cols]).astype(BF)
-        grads = (scale * dot(chosen, cot_v[q, :, cols])).astype(BF)
-        for dc in range(2):
-            sb, sa = block_place(place, dc, blk // 4, blk % 4)
-            lanes = pl.ds(pl.multiple_of(sa * COLS, COLS), COLS)
-            for dz in range(4):
-                r = dc * 4 + dz
-                outs[r][0, sb, :, lanes] = rows[r * CAP : r * CAP + CAP]
-                outs[r][1, sb, :, lanes] = grads[r * CAP : r * CAP + CAP]
+    for kind, held in enumerate((tok_v, cot_v)):
+        for copy in wide[SIDE * kind : SIDE * kind + SIDE]:
+            copy.wait()
+        for blk in range(16):
+            rows = dot(chosen, held[:, blk * COLS : blk * COLS + COLS])
+            rows = (scale * rows if kind else rows).astype(BF)
+            for dc in range(2):
+                sb, sa = block_place(place, dc, blk // 4, blk % 4)
+                lanes = pl.ds(pl.multiple_of(sa * COLS, COLS), COLS)
+                for dz in range(4):
+                    r = dc * 4 + dz
+                    outs[r][kind, sb, :, lanes] = rows[r * CAP : r * CAP + CAP]
 
 
 def to_b_kernel(*refs):
@@ -231,30 +228,33 @@
         outs[k][0] = summed[k].astype(F32)
 
 
-def combine_kernel(place, ids, gates, cotangent, *refs):
-    backs, (mixed, gtok, ggates) = refs[:REL], refs[REL:]
+def combine_kernel(half, place, ids, gates, cotangent, *refs):
+    backs, (mixed, gtok, ggates) = refs[:SIDE], refs[-3:]
+    held = refs[SIDE:-3]
     labels, chosen, scale = routing(place, ids[...], gates[...])
+    slots = slice(half * SIDE * CAP, half * SIDE * CAP + SIDE * CAP)
+    labels, chosen, scale = labels[half * SIDE :][:SIDE], chosen[slots], scale[slots]
     spread = chosen.T.astype(BF)
     scores = jnp.zeros(chosen.shape, F32)
     for blk in range(16):
         cols = slice(blk * COLS, blk * COLS + COLS)
-        made, grads = [], []
-        for dc in range(2):
-            sb, sa = block_place(place, dc, blk // 4, blk % 4)
-            lanes = pl.ds(pl.multiple_of(sa * COLS, COLS), COLS)
-            for dz in range(4):
-                made.append(backs[dc * 4 + dz][0, sb, :, lanes])
-                grads.append(backs[dc * 4 + dz][1, sb, :, lanes])
-        made, grads = jnp.concatenate(made, axis=0), jnp.concatenate(grads, axis=0)
+        sb, sa = block_place(place, half, blk // 4, blk % 4)
+        lanes = pl.ds(pl.multiple_of(sa * COLS, COLS), COLS)
+        made, grads = (
+            jnp.concatenate([b[kind, sb, :, lanes] for b in backs], axis=0) for kind in range(2)
+        )
         scaled = scale * made.astype(F32)
         upper = scaled.astype(BF)
         lower = (scaled - upper.astype(F32)).astype(BF)
-        mixed[:, cols] = (dot(spread, upper) + dot(spread, lower)).astype(BF)
-        gtok[:, cols] = dot(spread, grads).astype(BF)
+        mix, gto = dot(spread, upper) + dot(spread, lower), dot(spread, grads)
+        if held:
+            mix, gto = mix + held[0][:, cols], gto + held[1][:, cols]
+        mixed[:, cols] = mix.astype(mixed.dtype)
+        gtok[:, cols] = gto.astype(gtok.dtype)
         scores += dot_last(made, cotangent[:, cols])
     picked = chosen * scores
-    total = jnp.zeros(ids.shape, F32)
-    for r in range(REL):
+    total = held[2][...] if held else jnp.zeros(ids.shape, F32)
+    for r in range(SIDE):
         mine = jnp.sum(picked[r * CAP : r * CAP + CAP], axis=0, keepdims=True)
         total += jnp.where(ids[...] == labels[r], mine, 0.0)
     ggates[...] = total
@@ -291,8 +291,8 @@
         scratch=[
             pltpu.VMEM(ids_t.shape, jnp.int32),
             pltpu.VMEM(ids_t.shape, F32),
-            pltpu.VMEM((SIDE, tok, chunk), BF),
-            pltpu.VMEM((SIDE, tok, chunk), BF),
+            pltpu.VMEM(tokens.shape, BF),
+            pltpu.VMEM(tokens.shape, BF),
             pltpu.SemaphoreType.DMA((10,)),
         ],
     )
@@ -322,28 +322,35 @@
 
     def to_source(half, home):
         split = call(to_z_kernel, [shape((2, SIDE, CAP, chunk))] * SIDE, home, 0)
-        return [split[dz] if dz + half == 0 else shift_z(split[dz], -dz, half) for dz in range(SIDE)]
-
-    home_a, _ = send_back(0, hs[0])
-    hs_b, _ = lax.optimization_barrier((hs[1], (home_a[1], home_a[3])))
+        sent = [split[dz] if dz + half == 0 else shift_z(split[dz], -dz, half) for dz in range(SIDE)]
+        return sent, split
+
+    home_a, outs = send_back(0, hs[0])
+    home_b, outs = send_back(1, lax.optimization_barrier((hs[1], outs[0]))[0])
+    backs, split = to_source(0, lax.optimization_barrier((home_a, outs[0]))[0])
+    hs_b, _ = lax.optimization_barrier((hs[1], (outs[0], split[0])))
     (grads,) = call(
         weights_kernel,
         [shape((SIDE, 3, COLS, FW))],
         (*hs[0], *hs_b, *xs[0], *xs[1]),
         2 * work,
     )
-    home_b, _ = send_back(1, lax.optimization_barrier((hs[1], grads))[0])
     total = lax.psum_scatter(grads, AXES, axis_index_groups=groups_a())
-    backs = to_source(0, home_a) + to_source(1, home_b)
+    late, _ = to_source(1, lax.optimization_barrier((home_b, (grads, split[0])))[0])
+
+    def combine(half, dtype, ins):
+        return call(
+            functools.partial(combine_kernel, half),
+            [shape((tok, width), dtype), shape((tok, width), dtype), shape(ids_t.shape, F32)],
+            (place, ids_t, gates_t, cotangent, *ins),
+            4 * tok * tok * width,
+            smem=1,
+        )
+
+    sums = combine(0, F32, backs)
+    mixed, gtok, gg_t = combine(1, BF, (*late, *sums))
+    total, _ = lax.optimization_barrier((total, gg_t))
     gw = call(total_kernel, [shape((1, COLS, FW), F32)] * 3, (total,), 0)
-    backs, gw = lax.optimization_barrier((backs, gw))
-    mixed, gtok, gg_t = call(
-        combine_kernel,
-        [shape((tok, width)), shape((tok, width)), shape(ids_t.shape, F32)],
-        (place, ids_t, gates_t, cotangent, *backs),
-        8 * tok * tok * width,
-        smem=1,
-    )
     return mixed, gtok, gg_t.T, *gw
 
 

time: 156 us -> 152 us (0.974)
  local copies, waits for them, and re-layouts: 11.2 us -> 7.26 us
  starting transfers between devices: 56.9 us -> 54.4 us
    reduce_scatter x1, waiting for transfers between devices: 11.1 us -> 0.01 us  [per_device(): total = lax.psum_scatter(grads, AXES, axis_index_groups=groups_a())]
    ppermute x14, waiting for transfers between devices: 6.75 us -> 17.7 us  [shift_z(): lax.ppermute(v, AXES, _perm(lambda y, x, z, c: (y, x, z + dz, c + dc)))]
    unnamed x30 -> x26, local copies, waits for them, and re-layouts: 11.2 us -> 7.26 us
    ppermute x24, starting transfers between devices: 26 us -> 24.2 us  [shift_b(): lax.ppermute(v, AXES, _perm(lambda y, x, z, c: (y + s, x, z, c) if c == 0...]
    pallas_call x14 -> x15, Pallas kernels: 21.2 us -> 22.6 us  [call(): pl.pallas_call(kernel, out_shape=tuple(outs), in_specs=[pl.BlockSpec(memo...]
  transfers between devices with their start and end apart: 40 -> 40, of which waited for: 19 -> 21; matrix products, arithmetic and copies ran while one was open for 0% -> 0% of each run, Pallas kernels for 7% -> 9%
where the time goes in v4:
time: 152 us; the launch traced here: 151 us
  starting transfers between devices  54.4 us (36%)
  waiting for transfers between devices  51.8 us (34%)
  Pallas kernels  22.6 us (15%)
  between operations  14.3 us (9%)
  local copies, waits for them, and re-layouts  7.26 us (5%)
    ppermute x24, waiting for transfers between devices, shift_b(): lax.ppermute(v, AXES, _perm(lambda y, x, z, c: (y + s, x, z, c) if c == 0...  34 us
    ppermute x14, starting transfers between devices, shift_z(): lax.ppermute(v, AXES, _perm(lambda y, x, z, c: (y, x, z + dz, c + dc)))  30.2 us
    ppermute x24, starting transfers between devices, shift_b(): lax.ppermute(v, AXES, _perm(lambda y, x, z, c: (y + s, x, z, c) if c == 0...  24.2 us
    pallas_call x15, Pallas kernels, call(): pl.pallas_call(kernel, out_shape=tuple(outs), in_specs=[pl.BlockSpec(memo...  22.6 us
    ppermute x14, waiting for transfers between devices, shift_z(): lax.ppermute(v, AXES, _perm(lambda y, x, z, c: (y, x, z + dz, c + dc)))  17.7 us
    unnamed x26, local copies, waits for them, and re-layouts  7.26 us
  transfers between devices with their start and end apart: 40, of which 21 were waited for; matrix products, arithmetic and copies ran while one was open for 0% of the time, Pallas kernels for 9%

profile of v4, /device:TPU:1, one launch (start us, length us, event | category | flops | bytes accessed | tf_op | source)
XLA Modules:
  0.0 151.0 jit_solution(8261355782400907274)
XLA Ops:
  7.2 2.3 %shard_map.121 = bf16[3,256,768]{2,1,0:T(8,128)(2,1)} custom-call(bf16[1,256,768]{2,1,0:T(8,128)(2,1)} %gate.1, bf16[1,256,768]{2,1,0:T(8,128)(2,1)} %up.1, bf16[1,256,768]{2,1,0:T(8,128)(2,1)} %down.1), custom_call_target="tpu_custom_call" | custom-call | bytes 1024 | tf_op jit(solution)/shard_map/pallas_call | solution.py:62
  10.2 4.1 %shard_map.118 = (bf16[2,4,16,1024]{3,2,1,0:T(8,128)(2,1)}, bf16[2,4,16,1024]{3,2,1,0:T(8,128)(2,1)}, bf16[2,4,16,1024]{3,2,1,0:T(8,128)(2,1)}, bf16[2,4,16,1024...) custom-call(s32[4]{0:T(128)} %pad_add_fusion.place, ...), custom_call_target="tpu_custom_call" | custom-call | flops 2684354 | bytes 1024 | tf_op jit(solution)/shard_map/pallas_call | solution.py:62
  14.3 2.5 %collective-permute-start = (bf16[2,4,16,1024]{3,2,1,0:T(8,128)(2,1)}, bf16[2,4,16,1024]{3,2,1,0:T(8,128)(2,1)S(1)}, u32[]{:S(2)}, u32[]{:S(2)}) collective-permute-start(bf16[2,4,16,1024]{3,2,1,0:T(8,128)(2,1)} %get-tuple-element.73), channel_id=1, source_target_pairs={{0,2},{1,3},{2,4},{3,5},{4,6},{5,7},{6,0},{7,1},{8,10},{9,11},{10,... | collective-permute-start | bytes 786440 | tf_op jit(solution)/shard_map/ppermute | solution.py:45
  16.9 3.3 %collective-permute-start.1 = (bf16[2,4,16,1024]{3,2,1,0:T(8,128)(2,1)}, bf16[2,4,16,1024]{3,2,1,0:T(8,128)(2,1)S(1)}, u32[]{:S(2)}, u32[]{:S(2)}) collective-permute-start(bf16[2,4,16,1024]{3,2,1,0:T(8,128)(2,1)} %get-tuple-element.74), channel_id=1, source_target_pairs={{0,4},{1,5},{2,6},{3,7},{4,0},{5,1},{6,2},{7,3},{8,12},{9,13},{10,... | collective-permute-start | bytes 786440 | tf_op jit(solution)/shard_map/ppermute | solution.py:45
  20.9 1.5 %collective-permute-start.6 = (bf16[2,4,16,1024]{3,2,1,0:T(8,128)(2,1)}, bf16[2,4,16,1024]{3,2,1,0:T(8,128)(2,1)S(1)}, u32[]{:S(2)}, u32[]{:S(2)}) collective-permute-start(bf16[2,4,16,1024]{3,2,1,0:T(8,128)(2,1)} %get-tuple-element.80), channel_id=1, source_target_pairs={{0,1},{1,0},{2,3},{3,2},{4,5},{5,4},{6,7},{7,6},{8,9},{9,8},{10,11... | collective-permute-start | bytes 786440 | tf_op jit(solution)/shard_map/ppermute | solution.py:45
  23.0 2.2 %collective-permute-done.refs_1_ = bf16[2,4,16,1024]{3,2,1,0:T(8,128)(2,1)S(1)} collective-permute-done((bf16[2,4,16,1024]{3,2,1,0:T(8,128)(2,1)}, bf16[2,4,16,1024]{3,2,1,0:T(8,128)(2,1)S(1)}, u32[]{:S(2)}, u32[]{:S(2)}) %collective-permute-start) | collective-permute-done | bytes 262176 | tf_op jit(solution)/shard_map/ppermute | solution.py:45
  25.2 9.2 %collective-permute-start.8 = (bf16[2,4,16,1024]{3,2,1,0:T(8,128)(2,1)}, bf16[2,4,16,1024]{3,2,1,0:T(8,128)(2,1)S(1)}, u32[]{:S(2)}, u32[]{:S(2)}) collective-permute-start(bf16[2,4,16,1024]{3,2,1,0:T(8,128)(2,1)} %get-tuple-element.82), channel_id=1, source_target_pairs={{0,5},{1,4},{2,7},{3,6},{4,1},{5,0},{6,3},{7,2},{8,13},{9,12},{10,... | collective-permute-start | bytes 786440 | tf_op jit(solution)/shard_map/ppermute | solution.py:45
  35.5 1.3 collective-permute-start.3
  36.7 2.4 %collective-permute-start.4 = (bf16[2,64,1024]{2,1,0:T(8,128)(2,1)S(1)}, bf16[2,64,1024]{2,1,0:T(8,128)(2,1)S(1)}, u32[]{:S(2)}, u32[]{:S(2)}) collective-permute-start(bf16[2,64,1024]{2,1,0:T(8,128)(2,1)S(1)} %get-tuple-element.78), channel_id=1, source_target_pairs={{0,64},{1,17},{2,66},{3,19},{4,68},{5,21},{6,70},{7,23},{8,72},{9,... | collective-permute-start | bytes 786440 | tf_op jit(solution)/shard_map/ppermute | solution.py:39
  39.2 1.2 collective-permute-start.5
  40.4 3.5 %collective-permute-done.8.refs_2_ = bf16[2,4,16,1024]{3,2,1,0:T(8,128)(2,1)S(1)} collective-permute-done((bf16[2,4,16,1024]{3,2,1,0:T(8,128)(2,1)}, bf16[2,4,16,1024]{3,2,1,0:T(8,128)(2,1)S(1)}, u32[]{:S(2)}, u32[]{:S(2)}) %collective-permute-start.8) | collective-permute-done | bytes 262176 | tf_op jit(solution)/shard_map/ppermute | solution.py:45
  44.0 1.2 collective-permute-start.10
  45.2 2.5 %collective-permute-start.11 = (bf16[2,64,1024]{2,1,0:T(8,128)(2,1)S(1)}, bf16[2,64,1024]{2,1,0:T(8,128)(2,1)S(1)}, u32[]{:S(2)}, u32[]{:S(2)}) collective-permute-start(bf16[2,64,1024]{2,1,0:T(8,128)(2,1)S(1)} %get-tuple-element.86), channel_id=1, source_target_pairs={{0,64},{1,17},{2,66},{3,19},{4,68},{5,21},{6,70},{7,23},{8,72},{9,... | collective-permute-start | bytes 786440 | tf_op jit(solution)/shard_map/ppermute | solution.py:39
  47.7 1.1 collective-permute-start.12
  48.8 2.8 %collective-permute-done.4.refs_2_.refs_10_ = bf16[2,64,1024]{2,1,0:T(8,128)(2,1)S(1)} collective-permute-done((bf16[2,64,1024]{2,1,0:T(8,128)(2,1)S(1)}, bf16[2,64,1024]{2,1,0:T(8,128)(2,1)S(1)}, u32[]{:S(2)}, u32[]{:S(2)}) %collective-permute-start.4) | collective-permute-done | bytes 262176 | tf_op jit(solution)/shard_map/ppermute | solution.py:39
  51.7 3.6 %collective-permute-done.10.refs_5_.refs_13_ = bf16[2,64,1024]{2,1,0:T(8,128)(2,1)S(1)} collective-permute-done((bf16[2,64,1024]{2,1,0:T(8,128)(2,1)S(1)}, bf16[2,64,1024]{2,1,0:T(8,128)(2,1)S(1)}, u32[]{:S(2)}, u32[]{:S(2)}) %collective-permute-start.10) | collective-permute-done | bytes 262176 | tf_op jit(solution)/shard_map/ppermute | solution.py:39
  55.3 2.8 %collective-permute-done.11.refs_6_.refs_14_ = bf16[2,64,1024]{2,1,0:T(8,128)(2,1)S(1)} collective-permute-done((bf16[2,64,1024]{2,1,0:T(8,128)(2,1)S(1)}, bf16[2,64,1024]{2,1,0:T(8,128)(2,1)S(1)}, u32[]{:S(2)}, u32[]{:S(2)}) %collective-permute-start.11) | collective-permute-done | bytes 262176 | tf_op jit(solution)/shard_map/ppermute | solution.py:39
  58.1 2.3 %copy-done = bf16[12,256,768]{2,1,0:T(8,128)(2,1)S(1)} copy-done((bf16[12,256,768]{2,1,0:T(8,128)(2,1)S(1)}, bf16[12,256,768]{2,1,0:T(8,128)(2,1)}, u32[]{:S(2)}) %copy-start) | copy-done | bytes 4718616
  60.4 2.6 %shard_map.122 = (f32[64,2304]{1,0:T(8,128)S(1)}, bf16[64,2304]{1,0:T(8,128)(2,1)S(1)}, bf16[64,2304]{1,0:T(8,128)(2,1)S(1)}, bf16[64,2304]{1,0:T(8,128)(2,1)S(1...) custom-call(bf16[2,64,1024]{2,1,0:T(8,128)(2,1)S(1)} %get-tuple-elem, ...), custom_call_target="tpu_custom_call" | custom-call | flops 24159192 | bytes 1024 | tf_op jit(solution)/shard_map/pallas_call | solution.py:62
  63.9 1.4 collective-permute-start.20
  65.9 2.1 %collective-permute-start.13 = (bf16[64,2304]{1,0:T(8,128)(2,1)S(1)}, bf16[64,2304]{1,0:T(8,128)(2,1)S(1)}, u32[]{:S(2)}, u32[]{:S(2)}) collective-permute-start(bf16[64,2304]{1,0:T(8,128)(2,1)S(1)} %get-tuple-element.89), channel_id=1, source_target_pairs={{0,96},{1,25},{2,98},{3,27},{4,100},{5,29},{6,102},{7,31},{8,104},... | collective-permute-start | bytes 884744 | tf_op jit(solution)/shard_map/ppermute | solution.py:39
  69.4 1.9 %collective-permute-done.20.p2 = bf16[64,2304]{1,0:T(8,128)(2,1)S(1)} collective-permute-done((bf16[64,2304]{1,0:T(8,128)(2,1)S(1)}, bf16[64,2304]{1,0:T(8,128)(2,1)S(1)}, u32[]{:S(2)}, u32[]{:S(2)}) %collective-permute-start.20) | collective-permute-done | bytes 294944 | tf_op jit(solution)/shard_map/ppermute | solution.py:39
  71.4 3.1 %collective-permute-done.21.p3 = bf16[64,2304]{1,0:T(8,128)(2,1)S(1)} collective-permute-done((bf16[64,2304]{1,0:T(8,128)(2,1)S(1)}, bf16[64,2304]{1,0:T(8,128)(2,1)S(1)}, u32[]{:S(2)}, u32[]{:S(2)}) %collective-permute-start.21) | collective-permute-done | bytes 294944 | tf_op jit(solution)/shard_map/ppermute | solution.py:39
  75.1 1.4 collective-permute-start.23
  77.7 3.1 %collective-permute-done.15.p3 = bf16[64,2304]{1,0:T(8,128)(2,1)S(1)} collective-permute-done((bf16[64,2304]{1,0:T(8,128)(2,1)S(1)}, bf16[64,2304]{1,0:T(8,128)(2,1)S(1)}, u32[]{:S(2)}, u32[]{:S(2)}) %collective-permute-start.15) | collective-permute-done | bytes 294944 | tf_op jit(solution)/shard_map/ppermute | solution.py:39
  81.5 1.4 collective-permute-start.17
  84.1 3.0 %collective-permute-done.22.refs_1_ = bf16[64,2304]{1,0:T(8,128)(2,1)S(1)} collective-permute-done((bf16[64,2304]{1,0:T(8,128)(2,1)S(1)}, bf16[64,2304]{1,0:T(8,128)(2,1)S(1)}, u32[]{:S(2)}, u32[]{:S(2)}) %collective-permute-start.22) | collective-permute-done | bytes 294944 | tf_op jit(solution)/shard_map/ppermute | solution.py:39
  87.1 1.4 shard_map.125
  89.0 1.4 collective-permute-start.29
  90.9 2.6 %collective-permute-done.16.refs_1_.refs_5_ = bf16[64,2304]{1,0:T(8,128)(2,1)S(1)} collective-permute-done((bf16[64,2304]{1,0:T(8,128)(2,1)S(1)}, bf16[64,2304]{1,0:T(8,128)(2,1)S(1)}, u32[]{:S(2)}, u32[]{:S(2)}) %collective-permute-start.16) | collective-permute-done | bytes 294944 | tf_op jit(solution)/shard_map/ppermute | solution.py:39
  93.4 2.1 %shard_map.126 = (bf16[2,64,1024]{2,1,0:T(8,128)(2,1)S(1)}, bf16[2,64,1024]{2,1,0:T(8,128)(2,1)}, bf16[2,64,1024]{2,1,0:T(8,128)(2,1)S(1)}, bf16[2,64,1024]{2,1,0:T(8,128)(2,1)S(1)}) custom-call(bf16[64,2304]{1,0:T(8,128)(2,1)S(1)} %shard_map.123.refs_0_.refs_4_, bf16[64,2304]{1,0:T(8,128)(2,1)S(1)} %collective-permute-done.16.refs_1_.refs_5_, ...), custom_call_target="tpu_custom_call" | custom-call | flops 12079595 | bytes 1024 | tf_op jit(solution)/shard_map/pallas_call | solution.py:62
  96.5 2.8 %collective-permute-done.30.refs_3_ = bf16[2,64,1024]{2,1,0:T(8,128)(2,1)S(1)} collective-permute-done((bf16[2,64,1024]{2,1,0:T(8,128)(2,1)S(1)}, bf16[2,64,1024]{2,1,0:T(8,128)(2,1)S(1)}, u32[]{:S(2)}, u32[]{:S(2)}) %collective-permute-start.30) | collective-permute-done | bytes 262176 | tf_op jit(solution)/shard_map/ppermute | solution.py:39
  99.3 2.6 %shard_map.128 = bf16[4,3,256,768]{3,2,1,0:T(8,128)(2,1)S(1)} custom-call(bf16[64,2304]{1,0:T(8,128)(2,1)S(1)} %shard_map.124.refs_0_, bf16[64,2304]{1,0:T(8,128)(2,1)S(1)} %collective-permute-done.22.refs_1_, bf16[64,2304]{1,0:T(8,128)(2,1)S(1)} %collective-permute-done.23.refs_2_, bf16[64,2304]{1,0:T(8,128)(2,1)S(1)} %collective-permute-done.24.refs_3_, ...), custom_call_target="tpu_custom_call" | custom-call | flops 24159192 | bytes 1024 | tf_op jit(solution)/shard_map/pallas_call | solution.py:62
  102.0 2.2 %copy-done.2 = bf16[4,3,256,768]{3,2,1,0:T(8,128)(2,1)} copy-done((bf16[4,3,256,768]{3,2,1,0:T(8,128)(2,1)}, bf16[4,3,256,768]{3,2,1,0:T(8,128)(2,1)S(1)}, u32[]{:S(2)}) %copy-start.2) | copy-done | bytes 4718616
  105.1 1.2 collective-permute-start.26
  106.4 2.6 %collective-permute-start.35 = (bf16[2,4,16,1024]{3,2,1,0:T(8,128)(2,1)S(1)}, bf16[2,4,16,1024]{3,2,1,0:T(8,128)(2,1)S(1)}, u32[]{:S(2)}, u32[]{:S(2)}) collective-permute-start(bf16[2,4,16,1024]{3,2,1,0:T(8,128)(2,1)S(1)} %get-tuple-element.125), channel_id=1, source_target_pairs={{0,6},{1,7},{2,0},{3,1},{4,2},{5,3},{6,4},{7,5},{8,14},{9,15},{10,... | collective-permute-start | bytes 786440 | tf_op jit(solution)/shard_map/ppermute | solution.py:45
  109.7 2.2 %collective-permute-done.26.refs_2_ = bf16[2,64,1024]{2,1,0:T(8,128)(2,1)S(1)} collective-permute-done((bf16[2,64,1024]{2,1,0:T(8,128)(2,1)S(1)}, bf16[2,64,1024]{2,1,0:T(8,128)(2,1)S(1)}, u32[]{:S(2)}, u32[]{:S(2)}) %collective-permute-start.26) | collective-permute-done | bytes 262176 | tf_op jit(solution)/shard_map/ppermute | solution.py:39
  111.9 3.0 %collective-permute-done.27.refs_3_ = bf16[2,64,1024]{2,1,0:T(8,128)(2,1)S(1)} collective-permute-done((bf16[2,64,1024]{2,1,0:T(8,128)(2,1)S(1)}, bf16[2,64,1024]{2,1,0:T(8,128)(2,1)S(1)}, u32[]{:S(2)}, u32[]{:S(2)}) %collective-permute-start.27) | collective-permute-done | bytes 262176 | tf_op jit(solution)/shard_map/ppermute | solution.py:39
  114.9 1.4 collective-permute-start.37
  116.4 4.5 %collective-permute-start.31 = (bf16[2,4,16,1024]{3,2,1,0:T(8,128)(2,1)S(1)}, bf16[2,4,16,1024]{3,2,1,0:T(8,128)(2,1)S(1)}, u32[]{:S(2)}, u32[]{:S(2)}) collective-permute-start(bf16[2,4,16,1024]{3,2,1,0:T(8,128)(2,1)S(1)} %get-tuple-element.121), channel_id=1, source_target_pairs={{0,1},{1,0},{2,3},{3,2},{4,5},{5,4},{6,7},{7,6},{8,9},{9,8},{10,11... | collective-permute-start | bytes 786440 | tf_op jit(solution)/shard_map/ppermute | solution.py:45
  121.4 2.6 %collective-permute-start.33 = (bf16[2,4,16,1024]{3,2,1,0:T(8,128)(2,1)S(1)}, bf16[2,4,16,1024]{3,2,1,0:T(8,128)(2,1)S(1)}, u32[]{:S(2)}, u32[]{:S(2)}) collective-permute-start(bf16[2,4,16,1024]{3,2,1,0:T(8,128)(2,1)S(1)} %get-tuple-element.123), channel_id=1, source_target_pairs={{0,5},{1,4},{2,7},{3,6},{4,1},{5,0},{6,3},{7,2},{8,13},{9,12},{10,... | collective-permute-start | bytes 786440 | tf_op jit(solution)/shard_map/ppermute | solution.py:45
  124.1 2.0 %shard_map.130 = (f32[128,4096]{1,0:T(8,128)S(1)}, f32[128,4096]{1,0:T(8,128)S(1)}, f32[8,128]{1,0:T(8,128)S(1)}) custom-call(s32[4]{0:T(128)S(1)} %copy-done.8, s32[8,128]{1,0:T(8,128)S(1)} %bitcast.14, f32[8,128]{1,0:T(8,128)S(1)} %bitcast.17, bf16[128,4096]{1,0:T(8,128)(2,1)S(1)} %copy-done.3, bf16[2,4,16,1024]{3,2,1,0:T(8,128)(2,1)S(1)} %get-tuple-element.112.refs_0_, ...), custom_call_target="tpu_custom_call" | custom-call | flops 2684354 | bytes 1024 | tf_op jit(solution)/shard_map/pallas_call | solution.py:62
  126.1 3.7 %collective-permute-done.32.refs_1_ = bf16[2,4,16,1024]{3,2,1,0:T(8,128)(2,1)S(1)} collective-permute-done((bf16[2,4,16,1024]{3,2,1,0:T(8,128)(2,1)S(1)}, bf16[2,4,16,1024]{3,2,1,0:T(8,128)(2,1)S(1)}, u32[]{:S(2)}, u32[]{:S(2)}) %collective-permute-start.32) | collective-permute-done | bytes 262176 | tf_op jit(solution)/shard_map/ppermute | solution.py:45
  129.8 3.5 %collective-permute-done.33.refs_2_ = bf16[2,4,16,1024]{3,2,1,0:T(8,128)(2,1)S(1)} collective-permute-done((bf16[2,4,16,1024]{3,2,1,0:T(8,128)(2,1)S(1)}, bf16[2,4,16,1024]{3,2,1,0:T(8,128)(2,1)S(1)}, u32[]{:S(2)}, u32[]{:S(2)}) %collective-permute-start.33) | collective-permute-done | bytes 262176 | tf_op jit(solution)/shard_map/ppermute | solution.py:45
  133.3 4.8 %collective-permute-done.34.refs_3_ = bf16[2,4,16,1024]{3,2,1,0:T(8,128)(2,1)S(1)} collective-permute-done((bf16[2,4,16,1024]{3,2,1,0:T(8,128)(2,1)S(1)}, bf16[2,4,16,1024]{3,2,1,0:T(8,128)(2,1)S(1)}, u32[]{:S(2)}, u32[]{:S(2)}) %collective-permute-start.34) | collective-permute-done | bytes 262176 | tf_op jit(solution)/shard_map/ppermute | solution.py:45
  138.1 3.3 %shard_map.131 = (bf16[128,4096]{1,0:T(8,128)(2,1)}, bf16[128,4096]{1,0:T(8,128)(2,1)}, f32[8,128]{1,0:T(8,128)}) custom-call(s32[4]{0:T(128)S(1)} %copy-done.8, s32[8,128]{1,0:T(8,128)S(1)} %bitcast.15, f32[8,128]{1,0:T(8,128)S(1)} %bitcast.18, bf16[128,4096]{1,0:T(8,128)(2,1)S(1)} %copy-done.3, ...), custom_call_target="tpu_custom_call" | custom-call | flops 2684354 | bytes 1024 | tf_op jit(solution)/shard_map/pallas_call | solution.py:62
  141.4 1.3 copy-done.4
  142.7 1.5 shard_map.132
  (76 shorter events, 14.1 us)
Async XLA Ops:
  7.2 50.9 %all-gather.3.cloned.1.call-start = ((), (), s32[]{:S(2)}) async-start(), calls=%async_computation.2 | async-start | bytes 5898240 | tf_op jit(solution)/shard_map/all_gather | solution.py:281
  9.5 131.8 %reduce-scatter.2.cloned.1.call-start = ((), (), s32[]{:S(2)}) async-start(), calls=%async_computation.1 | async-start | bytes 5898240 | tf_op jit(solution)/shard_map/reduce_scatter | solution.py:338
  14.3 10.9 %collective-permute-start = (bf16[2,4,16,1024]{3,2,1,0:T(8,128)(2,1)}, bf16[2,4,16,1024]{3,2,1,0:T(8,128)(2,1)S(1)}, u32[]{:S(2)}, u32[]{:S(2)}) collective-permute-start(bf16[2,4,16,1024]{3,2,1,0:T(8,128)(2,1)} %get-tuple-element.73), channel_id=1, source_target_pairs={{0,2},{1,3},{2,4},{3,5},{4,6},{5,7},{6,0},{7,1},{8,10},{9,11},{10,... | collective-permute-start | bytes 786440 | tf_op jit(solution)/shard_map/ppermute | solution.py:45
  16.9 17.5 %collective-permute-start.1 = (bf16[2,4,16,1024]{3,2,1,0:T(8,128)(2,1)}, bf16[2,4,16,1024]{3,2,1,0:T(8,128)(2,1)S(1)}, u32[]{:S(2)}, u32[]{:S(2)}) collective-permute-start(bf16[2,4,16,1024]{3,2,1,0:T(8,128)(2,1)} %get-tuple-element.74), channel_id=1, source_target_pairs={{0,4},{1,5},{2,6},{3,7},{4,0},{5,1},{6,2},{7,3},{8,12},{9,13},{10,... | collective-permute-start | bytes 786440 | tf_op jit(solution)/shard_map/ppermute | solution.py:45
  20.2 14.2 %collective-permute-start.2 = (bf16[2,4,16,1024]{3,2,1,0:T(8,128)(2,1)}, bf16[2,4,16,1024]{3,2,1,0:T(8,128)(2,1)S(1)}, u32[]{:S(2)}, u32[]{:S(2)}) collective-permute-start(bf16[2,4,16,1024]{3,2,1,0:T(8,128)(2,1)} %get-tuple-element.75), channel_id=1, source_target_pairs={{0,6},{1,7},{2,0},{3,1},{4,2},{5,3},{6,4},{7,5},{8,14},{9,15},{10,... | collective-permute-start | bytes 786440 | tf_op jit(solution)/shard_map/ppermute | solution.py:45
  20.9 15.8 %collective-permute-start.6 = (bf16[2,4,16,1024]{3,2,1,0:T(8,128)(2,1)}, bf16[2,4,16,1024]{3,2,1,0:T(8,128)(2,1)S(1)}, u32[]{:S(2)}, u32[]{:S(2)}) collective-permute-start(bf16[2,4,16,1024]{3,2,1,0:T(8,128)(2,1)} %get-tuple-element.80), channel_id=1, source_target_pairs={{0,1},{1,0},{2,3},{3,2},{4,5},{5,4},{6,7},{7,6},{8,9},{9,8},{10,11... | collective-permute-start | bytes 786440 | tf_op jit(solution)/shard_map/ppermute | solution.py:45
  22.4 16.8 %collective-permute-start.7 = (bf16[2,4,16,1024]{3,2,1,0:T(8,128)(2,1)}, bf16[2,4,16,1024]{3,2,1,0:T(8,128)(2,1)S(1)}, u32[]{:S(2)}, u32[]{:S(2)}) collective-permute-start(bf16[2,4,16,1024]{3,2,1,0:T(8,128)(2,1)} %get-tuple-element.81), channel_id=1, source_target_pairs={{0,3},{1,2},{2,5},{3,4},{4,7},{5,6},{6,1},{7,0},{8,11},{9,10},{10,... | collective-permute-start | bytes 786440 | tf_op jit(solution)/shard_map/ppermute | solution.py:45
  25.2 18.7 %collective-permute-start.8 = (bf16[2,4,16,1024]{3,2,1,0:T(8,128)(2,1)}, bf16[2,4,16,1024]{3,2,1,0:T(8,128)(2,1)S(1)}, u32[]{:S(2)}, u32[]{:S(2)}) collective-permute-start(bf16[2,4,16,1024]{3,2,1,0:T(8,128)(2,1)} %get-tuple-element.82), channel_id=1, source_target_pairs={{0,5},{1,4},{2,7},{3,6},{4,1},{5,0},{6,3},{7,2},{8,13},{9,12},{10,... | collective-permute-start | bytes 786440 | tf_op jit(solution)/shard_map/ppermute | solution.py:45
  34.4 9.5 %collective-permute-start.9 = (bf16[2,4,16,1024]{3,2,1,0:T(8,128)(2,1)}, bf16[2,4,16,1024]{3,2,1,0:T(8,128)(2,1)S(1)}, u32[]{:S(2)}, u32[]{:S(2)}) collective-permute-start(bf16[2,4,16,1024]{3,2,1,0:T(8,128)(2,1)} %get-tuple-element.83), channel_id=1, source_target_pairs={{0,7},{1,6},{2,1},{3,0},{4,3},{5,2},{6,5},{7,4},{8,15},{9,14},{10,... | collective-permute-start | bytes 786440 | tf_op jit(solution)/shard_map/ppermute | solution.py:45
  35.5 12.2 %collective-permute-start.3 = (bf16[2,64,1024]{2,1,0:T(8,128)(2,1)S(1)}, bf16[2,64,1024]{2,1,0:T(8,128)(2,1)S(1)}, u32[]{:S(2)}, u32[]{:S(2)}) collective-permute-start(bf16[2,64,1024]{2,1,0:T(8,128)(2,1)S(1)} %get-tuple-element.77), channel_id=1, source_target_pairs={{0,32},{1,9},{2,34},{3,11},{4,36},{5,13},{6,38},{7,15},{8,40},{9,1... | collective-permute-start | bytes 786440 | tf_op jit(solution)/shard_map/ppermute | solution.py:39
  36.7 14.9 %collective-permute-start.4 = (bf16[2,64,1024]{2,1,0:T(8,128)(2,1)S(1)}, bf16[2,64,1024]{2,1,0:T(8,128)(2,1)S(1)}, u32[]{:S(2)}, u32[]{:S(2)}) collective-permute-start(bf16[2,64,1024]{2,1,0:T(8,128)(2,1)S(1)} %get-tuple-element.78), channel_id=1, source_target_pairs={{0,64},{1,17},{2,66},{3,19},{4,68},{5,21},{6,70},{7,23},{8,72},{9,... | collective-permute-start | bytes 786440 | tf_op jit(solution)/shard_map/ppermute | solution.py:39
  39.2 12.5 %collective-permute-start.5 = (bf16[2,64,1024]{2,1,0:T(8,128)(2,1)S(1)}, bf16[2,64,1024]{2,1,0:T(8,128)(2,1)S(1)}, u32[]{:S(2)}, u32[]{:S(2)}) collective-permute-start(bf16[2,64,1024]{2,1,0:T(8,128)(2,1)S(1)} %get-tuple-element.79), channel_id=1, source_target_pairs={{0,96},{1,25},{2,98},{3,27},{4,100},{5,29},{6,102},{7,31},{8,104},... | collective-permute-start | bytes 786440 | tf_op jit(solution)/shard_map/ppermute | solution.py:39
  44.0 11.3 %collective-permute-start.10 = (bf16[2,64,1024]{2,1,0:T(8,128)(2,1)S(1)}, bf16[2,64,1024]{2,1,0:T(8,128)(2,1)S(1)}, u32[]{:S(2)}, u32[]{:S(2)}) collective-permute-start(bf16[2,64,1024]{2,1,0:T(8,128)(2,1)S(1)} %get-tuple-element.85), channel_id=1, source_target_pairs={{0,32},{1,9},{2,34},{3,11},{4,36},{5,13},{6,38},{7,15},{8,40},{9,1... | collective-permute-start | bytes 786440 | tf_op jit(solution)/shard_map/ppermute | solution.py:39
  45.2 12.8 %collective-permute-start.11 = (bf16[2,64,1024]{2,1,0:T(8,128)(2,1)S(1)}, bf16[2,64,1024]{2,1,0:T(8,128)(2,1)S(1)}, u32[]{:S(2)}, u32[]{:S(2)}) collective-permute-start(bf16[2,64,1024]{2,1,0:T(8,128)(2,1)S(1)} %get-tuple-element.86), channel_id=1, source_target_pairs={{0,64},{1,17},{2,66},{3,19},{4,68},{5,21},{6,70},{7,23},{8,72},{9,... | collective-permute-start | bytes 786440 | tf_op jit(solution)/shard_map/ppermute | solution.py:39
  47.7 10.4 %collective-permute-start.12 = (bf16[2,64,1024]{2,1,0:T(8,128)(2,1)S(1)}, bf16[2,64,1024]{2,1,0:T(8,128)(2,1)S(1)}, u32[]{:S(2)}, u32[]{:S(2)}) collective-permute-start(bf16[2,64,1024]{2,1,0:T(8,128)(2,1)S(1)} %get-tuple-element.87), channel_id=1, source_target_pairs={{0,96},{1,25},{2,98},{3,27},{4,100},{5,29},{6,102},{7,31},{8,104},... | collective-permute-start | bytes 786440 | tf_op jit(solution)/shard_map/ppermute | solution.py:39
  58.1 2.3 %copy-start = (bf16[12,256,768]{2,1,0:T(8,128)(2,1)S(1)}, bf16[12,256,768]{2,1,0:T(8,128)(2,1)}, u32[]{:S(2)}) copy-start(bf16[12,256,768]{2,1,0:T(8,128)(2,1)} %all-gather.3.cloned.1.call-done) | copy-start | bytes 14155780
  60.4 26.7 %copy-start.1 = (bf16[12,256,768]{2,1,0:T(8,128)(2,1)S(1)}, bf16[12,256,768]{2,1,0:T(8,128)(2,1)}, u32[]{:S(2)}) copy-start(bf16[12,256,768]{2,1,0:T(8,128)(2,1)} %all-gather.3.cloned.1.call-done) | copy-start | bytes 14155780
  63.0 5.9 %collective-permute-start.19 = (bf16[64,2304]{1,0:T(8,128)(2,1)S(1)}, bf16[64,2304]{1,0:T(8,128)(2,1)S(1)}, u32[]{:S(2)}, u32[]{:S(2)}) collective-permute-start(bf16[64,2304]{1,0:T(8,128)(2,1)S(1)} %get-tuple-element.93), channel_id=1, source_target_pairs={{0,96},{1,25},{2,98},{3,27},{4,100},{5,29},{6,102},{7,31},{8,104},... | collective-permute-start | bytes 884744 | tf_op jit(solution)/shard_map/ppermute | solution.py:39
  63.9 7.4 %collective-permute-start.20 = (bf16[64,2304]{1,0:T(8,128)(2,1)S(1)}, bf16[64,2304]{1,0:T(8,128)(2,1)S(1)}, u32[]{:S(2)}, u32[]{:S(2)}) collective-permute-start(bf16[64,2304]{1,0:T(8,128)(2,1)S(1)} %get-tuple-element.94), channel_id=1, source_target_pairs={{0,64},{1,17},{2,66},{3,19},{4,68},{5,21},{6,70},{7,23},{8,72},{9,... | collective-permute-start | bytes 884744 | tf_op jit(solution)/shard_map/ppermute | solution.py:39
  65.3 9.1 %collective-permute-start.21 = (bf16[64,2304]{1,0:T(8,128)(2,1)S(1)}, bf16[64,2304]{1,0:T(8,128)(2,1)S(1)}, u32[]{:S(2)}, u32[]{:S(2)}) collective-permute-start(bf16[64,2304]{1,0:T(8,128)(2,1)S(1)} %get-tuple-element.95), channel_id=1, source_target_pairs={{0,32},{1,9},{2,34},{3,11},{4,36},{5,13},{6,38},{7,15},{8,40},{9,1... | collective-permute-start | bytes 884744 | tf_op jit(solution)/shard_map/ppermute | solution.py:39
  65.9 10.6 %collective-permute-start.13 = (bf16[64,2304]{1,0:T(8,128)(2,1)S(1)}, bf16[64,2304]{1,0:T(8,128)(2,1)S(1)}, u32[]{:S(2)}, u32[]{:S(2)}) collective-permute-start(bf16[64,2304]{1,0:T(8,128)(2,1)S(1)} %get-tuple-element.89), channel_id=1, source_target_pairs={{0,96},{1,25},{2,98},{3,27},{4,100},{5,29},{6,102},{7,31},{8,104},... | collective-permute-start | bytes 884744 | tf_op jit(solution)/shard_map/ppermute | solution.py:39
  68.0 9.7 %collective-permute-start.14 = (bf16[64,2304]{1,0:T(8,128)(2,1)S(1)}, bf16[64,2304]{1,0:T(8,128)(2,1)S(1)}, u32[]{:S(2)}, u32[]{:S(2)}) collective-permute-start(bf16[64,2304]{1,0:T(8,128)(2,1)S(1)} %get-tuple-element.90), channel_id=1, source_target_pairs={{0,64},{1,17},{2,66},{3,19},{4,68},{5,21},{6,70},{7,23},{8,72},{9,... | collective-permute-start | bytes 884744 | tf_op jit(solution)/shard_map/ppermute | solution.py:39
  69.0 11.8 %collective-permute-start.15 = (bf16[64,2304]{1,0:T(8,128)(2,1)S(1)}, bf16[64,2304]{1,0:T(8,128)(2,1)S(1)}, u32[]{:S(2)}, u32[]{:S(2)}) collective-permute-start(bf16[64,2304]{1,0:T(8,128)(2,1)S(1)} %get-tuple-element.91), channel_id=1, source_target_pairs={{0,32},{1,9},{2,34},{3,11},{4,36},{5,13},{6,38},{7,15},{8,40},{9,1... | collective-permute-start | bytes 884744 | tf_op jit(solution)/shard_map/ppermute | solution.py:39
  74.7 8.2 %collective-permute-start.24 = (bf16[64,2304]{1,0:T(8,128)(2,1)S(1)}, bf16[64,2304]{1,0:T(8,128)(2,1)S(1)}, u32[]{:S(2)}, u32[]{:S(2)}) collective-permute-start(bf16[64,2304]{1,0:T(8,128)(2,1)S(1)} %shard_map.124.refs_0_), channel_id=1, source_target_pairs={{0,96},{1,25},{2,98},{3,27},{4,100},{5,29},{6,102},{7,31},{8,104},... | collective-permute-start | bytes 884744 | tf_op jit(solution)/shard_map/ppermute | solution.py:39
  75.1 9.0 %collective-permute-start.23 = (bf16[64,2304]{1,0:T(8,128)(2,1)S(1)}, bf16[64,2304]{1,0:T(8,128)(2,1)S(1)}, u32[]{:S(2)}, u32[]{:S(2)}) collective-permute-start(bf16[64,2304]{1,0:T(8,128)(2,1)S(1)} %shard_map.124.refs_0_), channel_id=1, source_target_pairs={{0,64},{1,17},{2,66},{3,19},{4,68},{5,21},{6,70},{7,23},{8,72},{9,... | collective-permute-start | bytes 884744 | tf_op jit(solution)/shard_map/ppermute | solution.py:39
  76.5 10.6 %collective-permute-start.22 = (bf16[64,2304]{1,0:T(8,128)(2,1)S(1)}, bf16[64,2304]{1,0:T(8,128)(2,1)S(1)}, u32[]{:S(2)}, u32[]{:S(2)}) collective-permute-start(bf16[64,2304]{1,0:T(8,128)(2,1)S(1)} %shard_map.124.refs_0_), channel_id=1, source_target_pairs={{0,32},{1,9},{2,34},{3,11},{4,36},{5,13},{6,38},{7,15},{8,40},{9,1... | collective-permute-start | bytes 884744 | tf_op jit(solution)/shard_map/ppermute | solution.py:39
  81.0 9.4 %collective-permute-start.18 = (bf16[64,2304]{1,0:T(8,128)(2,1)S(1)}, bf16[64,2304]{1,0:T(8,128)(2,1)S(1)}, u32[]{:S(2)}, u32[]{:S(2)}) collective-permute-start(bf16[64,2304]{1,0:T(8,128)(2,1)S(1)} %shard_map.123.refs_0_.refs_4_), channel_id=1, source_target_pairs={{0,96},{1,25},{2,98},{3,27},{4,100},{5,29},{6,102},{7,31},{8,104},... | collective-permute-start | bytes 884744 | tf_op jit(solution)/shard_map/ppermute | solution.py:39
  81.5 9.4 %collective-permute-start.17 = (bf16[64,2304]{1,0:T(8,128)(2,1)S(1)}, bf16[64,2304]{1,0:T(8,128)(2,1)S(1)}, u32[]{:S(2)}, u32[]{:S(2)}) collective-permute-start(bf16[64,2304]{1,0:T(8,128)(2,1)S(1)} %shard_map.123.refs_0_.refs_4_), channel_id=1, source_target_pairs={{0,64},{1,17},{2,66},{3,19},{4,68},{5,21},{6,70},{7,23},{8,72},{9,... | collective-permute-start | bytes 884744 | tf_op jit(solution)/shard_map/ppermute | solution.py:39
  82.9 10.6 %collective-permute-start.16 = (bf16[64,2304]{1,0:T(8,128)(2,1)S(1)}, bf16[64,2304]{1,0:T(8,128)(2,1)S(1)}, u32[]{:S(2)}, u32[]{:S(2)}) collective-permute-start(bf16[64,2304]{1,0:T(8,128)(2,1)S(1)} %shard_map.123.refs_0_.refs_4_), channel_id=1, source_target_pairs={{0,32},{1,9},{2,34},{3,11},{4,36},{5,13},{6,38},{7,15},{8,40},{9,1... | collective-permute-start | bytes 884744 | tf_op jit(solution)/shard_map/ppermute | solution.py:39
  88.5 7.0 %collective-permute-start.28 = (bf16[2,64,1024]{2,1,0:T(8,128)(2,1)S(1)}, bf16[2,64,1024]{2,1,0:T(8,128)(2,1)S(1)}, u32[]{:S(2)}, u32[]{:S(2)}) collective-permute-start(bf16[2,64,1024]{2,1,0:T(8,128)(2,1)S(1)} %get-tuple-element.105), channel_id=1, source_target_pairs={{0,96},{1,25},{2,98},{3,27},{4,100},{5,29},{6,102},{7,31},{8,104},... | collective-permute-start | bytes 786440 | tf_op jit(solution)/shard_map/ppermute | solution.py:39
  89.0 7.4 %collective-permute-start.29 = (bf16[2,64,1024]{2,1,0:T(8,128)(2,1)S(1)}, bf16[2,64,1024]{2,1,0:T(8,128)(2,1)S(1)}, u32[]{:S(2)}, u32[]{:S(2)}) collective-permute-start(bf16[2,64,1024]{2,1,0:T(8,128)(2,1)S(1)} %get-tuple-element.106), channel_id=1, source_target_pairs={{0,64},{1,17},{2,66},{3,19},{4,68},{5,21},{6,70},{7,23},{8,72},{9,... | collective-permute-start | bytes 786440 | tf_op jit(solution)/shard_map/ppermute | solution.py:39
  90.4 8.8 %collective-permute-start.30 = (bf16[2,64,1024]{2,1,0:T(8,128)(2,1)S(1)}, bf16[2,64,1024]{2,1,0:T(8,128)(2,1)S(1)}, u32[]{:S(2)}, u32[]{:S(2)}) collective-permute-start(bf16[2,64,1024]{2,1,0:T(8,128)(2,1)S(1)} %get-tuple-element.107), channel_id=1, source_target_pairs={{0,32},{1,9},{2,34},{3,11},{4,36},{5,13},{6,38},{7,15},{8,40},{9,1... | collective-permute-start | bytes 786440 | tf_op jit(solution)/shard_map/ppermute | solution.py:39
  95.5 3.8 %copy-start.9 = (bf16[2,64,1024]{2,1,0:T(8,128)(2,1)}, bf16[2,64,1024]{2,1,0:T(8,128)(2,1)S(1)}, u32[]{:S(2)}) copy-start(bf16[2,64,1024]{2,1,0:T(8,128)(2,1)S(1)} %get-tuple-element.104) | copy-start | bytes 786436
  95.5 3.8 %copy-start.11 = (bf16[2,64,1024]{2,1,0:T(8,128)(2,1)}, bf16[2,64,1024]{2,1,0:T(8,128)(2,1)S(1)}, u32[]{:S(2)}) copy-start(bf16[2,64,1024]{2,1,0:T(8,128)(2,1)S(1)} %get-tuple-element.103) | copy-start | bytes 786436
  104.2 19.9 %copy-start.3 = (bf16[128,4096]{1,0:T(8,128)(2,1)S(1)}, bf16[128,4096]{1,0:T(8,128)(2,1)}, u32[]{:S(2)}) copy-start(bf16[128,4096]{1,0:T(8,128)(2,1)} %cotangent.5) | copy-start | bytes 3145732
  104.2 19.9 %copy-start.6 = (s32[128,8]{0,1:T(8,128)S(1)}, s32[128,8]{0,1:T(8,128)}, u32[]{:S(2)}) copy-start(s32[128,8]{0,1:T(8,128)} %param.8) | copy-start | bytes 12292
  104.2 19.9 %copy-start.7 = (f32[128,8]{0,1:T(8,128)S(1)}, f32[128,8]{0,1:T(8,128)}, u32[]{:S(2)}) copy-start(f32[128,8]{0,1:T(8,128)} %param.9) | copy-start | bytes 12292
  104.2 19.9 %copy-start.8 = (s32[4]{0:T(128)S(1)}, s32[4]{0:T(128)}, u32[]{:S(2)}) copy-start(s32[4]{0:T(128)} %pad_add_fusion.place) | copy-start | bytes 52
  104.2 5.5 %collective-permute-start.25 = (bf16[2,64,1024]{2,1,0:T(8,128)(2,1)}, bf16[2,64,1024]{2,1,0:T(8,128)(2,1)S(1)}, u32[]{:S(2)}, u32[]{:S(2)}) collective-permute-start(bf16[2,64,1024]{2,1,0:T(8,128)(2,1)} %get-tuple-element.102), channel_id=1, source_target_pairs={{0,96},{1,25},{2,98},{3,27},{4,100},{5,29},{6,102},{7,31},{8,104},... | collective-permute-start | bytes 786440 | tf_op jit(solution)/shard_map/ppermute | solution.py:39
  105.1 6.8 %collective-permute-start.26 = (bf16[2,64,1024]{2,1,0:T(8,128)(2,1)S(1)}, bf16[2,64,1024]{2,1,0:T(8,128)(2,1)S(1)}, u32[]{:S(2)}, u32[]{:S(2)}) collective-permute-start(bf16[2,64,1024]{2,1,0:T(8,128)(2,1)S(1)} %copy-done.12), channel_id=1, source_target_pairs={{0,64},{1,17},{2,66},{3,19},{4,68},{5,21},{6,70},{7,23},{8,72},{9,... | collective-permute-start | bytes 786440 | tf_op jit(solution)/shard_map/ppermute | solution.py:39
  106.3 8.6 %collective-permute-start.27 = (bf16[2,64,1024]{2,1,0:T(8,128)(2,1)S(1)}, bf16[2,64,1024]{2,1,0:T(8,128)(2,1)S(1)}, u32[]{:S(2)}, u32[]{:S(2)}) collective-permute-start(bf16[2,64,1024]{2,1,0:T(8,128)(2,1)S(1)} %copy-done.10), channel_id=1, source_target_pairs={{0,32},{1,9},{2,34},{3,11},{4,36},{5,13},{6,38},{7,15},{8,40},{9,1... | collective-permute-start | bytes 786440 | tf_op jit(solution)/shard_map/ppermute | solution.py:39
  106.4 15.1 %collective-permute-start.35 = (bf16[2,4,16,1024]{3,2,1,0:T(8,128)(2,1)S(1)}, bf16[2,4,16,1024]{3,2,1,0:T(8,128)(2,1)S(1)}, u32[]{:S(2)}, u32[]{:S(2)}) collective-permute-start(bf16[2,4,16,1024]{3,2,1,0:T(8,128)(2,1)S(1)} %get-tuple-element.125), channel_id=1, source_target_pairs={{0,6},{1,7},{2,0},{3,1},{4,2},{5,3},{6,4},{7,5},{8,14},{9,15},{10,... | collective-permute-start | bytes 786440 | tf_op jit(solution)/shard_map/ppermute | solution.py:45
  109.0 15.1 %collective-permute-start.36 = (bf16[2,4,16,1024]{3,2,1,0:T(8,128)(2,1)S(1)}, bf16[2,4,16,1024]{3,2,1,0:T(8,128)(2,1)S(1)}, u32[]{:S(2)}, u32[]{:S(2)}) collective-permute-start(bf16[2,4,16,1024]{3,2,1,0:T(8,128)(2,1)S(1)} %get-tuple-element.126), channel_id=1, source_target_pairs={{0,4},{1,5},{2,6},{3,7},{4,0},{5,1},{6,2},{7,3},{8,12},{9,13},{10,... | collective-permute-start | bytes 786440 | tf_op jit(solution)/shard_map/ppermute | solution.py:45
  114.9 9.1 %collective-permute-start.37 = (bf16[2,4,16,1024]{3,2,1,0:T(8,128)(2,1)S(1)}, bf16[2,4,16,1024]{3,2,1,0:T(8,128)(2,1)S(1)}, u32[]{:S(2)}, u32[]{:S(2)}) collective-permute-start(bf16[2,4,16,1024]{3,2,1,0:T(8,128)(2,1)S(1)} %get-tuple-element.127), channel_id=1, source_target_pairs={{0,2},{1,3},{2,4},{3,5},{4,6},{5,7},{6,0},{7,1},{8,10},{9,11},{10,... | collective-permute-start | bytes 786440 | tf_op jit(solution)/shard_map/ppermute | solution.py:45
  116.4 9.7 %collective-permute-start.31 = (bf16[2,4,16,1024]{3,2,1,0:T(8,128)(2,1)S(1)}, bf16[2,4,16,1024]{3,2,1,0:T(8,128)(2,1)S(1)}, u32[]{:S(2)}, u32[]{:S(2)}) collective-permute-start(bf16[2,4,16,1024]{3,2,1,0:T(8,128)(2,1)S(1)} %get-tuple-element.121), channel_id=1, source_target_pairs={{0,1},{1,0},{2,3},{3,2},{4,5},{5,4},{6,7},{7,6},{8,9},{9,8},{10,11... | collective-permute-start | bytes 786440 | tf_op jit(solution)/shard_map/ppermute | solution.py:45
  120.9 9.0 %collective-permute-start.32 = (bf16[2,4,16,1024]{3,2,1,0:T(8,128)(2,1)S(1)}, bf16[2,4,16,1024]{3,2,1,0:T(8,128)(2,1)S(1)}, u32[]{:S(2)}, u32[]{:S(2)}) collective-permute-start(bf16[2,4,16,1024]{3,2,1,0:T(8,128)(2,1)S(1)} %get-tuple-element.122), channel_id=1, source_target_pairs={{0,7},{1,6},{2,1},{3,0},{4,3},{5,2},{6,5},{7,4},{8,15},{9,14},{10,... | collective-permute-start | bytes 786440 | tf_op jit(solution)/shard_map/ppermute | solution.py:45
  121.4 11.9 %collective-permute-start.33 = (bf16[2,4,16,1024]{3,2,1,0:T(8,128)(2,1)S(1)}, bf16[2,4,16,1024]{3,2,1,0:T(8,128)(2,1)S(1)}, u32[]{:S(2)}, u32[]{:S(2)}) collective-permute-start(bf16[2,4,16,1024]{3,2,1,0:T(8,128)(2,1)S(1)} %get-tuple-element.123), channel_id=1, source_target_pairs={{0,5},{1,4},{2,7},{3,6},{4,1},{5,0},{6,3},{7,2},{8,13},{9,12},{10,... | collective-permute-start | bytes 786440 | tf_op jit(solution)/shard_map/ppermute | solution.py:45
  124.1 14.0 %collective-permute-start.34 = (bf16[2,4,16,1024]{3,2,1,0:T(8,128)(2,1)S(1)}, bf16[2,4,16,1024]{3,2,1,0:T(8,128)(2,1)S(1)}, u32[]{:S(2)}, u32[]{:S(2)}) collective-permute-start(bf16[2,4,16,1024]{3,2,1,0:T(8,128)(2,1)S(1)} %get-tuple-element.124), channel_id=1, source_target_pairs={{0,3},{1,2},{2,5},{3,4},{4,7},{5,6},{6,1},{7,0},{8,11},{9,10},{10,... | collective-permute-start | bytes 786440 | tf_op jit(solution)/shard_map/ppermute | solution.py:45
  (5 other events, 7.5 us)
Sparse Core Ops, SparseCore 0:
  9.7 44.5 all-gather.2
  104.3 33.8 reduce-scatter.1

commit v5 on v4

--- a/solution.py
+++ b/solution.py
@@ -57,13 +57,13 @@
     return lax.dot_general(left, right, (((0,), (0,)), ((), ())), preferred_element_type=F32)
 
 
-def call(kernel, outs, ins, flops, smem=0, hbm=0, scratch=(), vmem=VMEM):
+def call(kernel, outs, ins, flops, smem=0, hbm=0, scratch=(), vmem=VMEM, out_space=pltpu.VMEM):
     spaces = [pltpu.SMEM] * smem + [pltpu.HBM] * hbm + [pltpu.VMEM] * (len(ins) - smem - hbm)
     return pl.pallas_call(
         kernel,
         out_shape=tuple(outs),
         in_specs=[pl.BlockSpec(memory_space=space) for space in spaces],
-        out_specs=tuple(pl.BlockSpec(memory_space=pltpu.VMEM) for _ in outs),
+        out_specs=tuple(pl.BlockSpec(memory_space=out_space) for _ in outs),
         scratch_shapes=list(scratch),
         compiler_params=pltpu.CompilerParams(vmem_limit_bytes=vmem),
         cost_estimate=pl.CostEstimate(flops=flops // 100, bytes_accessed=1024, transcendentals=0),
@@ -161,14 +161,26 @@
     return [jnp.concatenate([p[:, k * FW : k * FW + FW] for p in pieces], axis=0) for k in range(3)]
 
 
-def held_kernel(gate, up, down, out, sem):
-    copies = [
-        pltpu.make_async_copy(w.at[0], out.at[k], sem.at[k]) for k, w in enumerate((gate, up, down))
-    ]
-    for copy in copies:
-        copy.start()
-    for copy in copies:
-        copy.wait()
+def held_kernel(gate, up, down, out, block, sem):
+    half = COLS // 2
+    steps = []
+    for k, w in enumerate((gate, up, down)):
+        for h in range(2):
+            at = pl.ds(h * half, half)
+            took, gave = sem.at[0, 2 * k + h], sem.at[1, 2 * k + h]
+            steps.append(
+                (
+                    pltpu.make_async_copy(w.at[0, at], block.at[k, at], took),
+                    pltpu.make_async_copy(block.at[k, at], out.at[k, at], gave),
+                )
+            )
+    for take, _ in steps:
+        take.start()
+    for take, give in steps:
+        take.wait()
+        give.start()
+    for _, give in steps:
+        give.wait()
 
 
 def partial_kernel(*refs):
@@ -223,9 +235,18 @@
             out[a, k] = dot_first(left, right).astype(BF)
 
 
-def total_kernel(summed, *outs):
+def total_kernel(summed, *refs):
+    outs, (narrow, wide, sem) = refs[:3], refs[3:]
+    takes = [pltpu.make_async_copy(summed.at[k], narrow.at[k], sem.at[0, k]) for k in range(3)]
+    gives = [pltpu.make_async_copy(wide.at[k], outs[k].at[0], sem.at[1, k]) for k in range(3)]
+    for copy in takes:
+        copy.start()
     for k in range(3):
-        outs[k][0] = summed[k].astype(F32)
+        takes[k].wait()
+        wide[k] = narrow[k].astype(F32)
+        gives[k].start()
+    for copy in gives:
+        copy.wait()
 
 
 def combine_kernel(half, place, ids, gates, cotangent, *refs):
@@ -236,22 +257,26 @@
     labels, chosen, scale = labels[half * SIDE :][:SIDE], chosen[slots], scale[slots]
     spread = chosen.T.astype(BF)
     scores = jnp.zeros(chosen.shape, F32)
-    for blk in range(16):
-        cols = slice(blk * COLS, blk * COLS + COLS)
-        sb, sa = block_place(place, half, blk // 4, blk % 4)
-        lanes = pl.ds(pl.multiple_of(sa * COLS, COLS), COLS)
-        made, grads = (
-            jnp.concatenate([b[kind, sb, :, lanes] for b in backs], axis=0) for kind in range(2)
-        )
+    twice = jnp.concatenate([spread, spread], axis=1)
+    y, x, flip = place[0], place[1], place[3] ^ half
+    for sb in range(SIDE):
+        made, grads = (jnp.concatenate([b[kind, sb] for b in backs], axis=0) for kind in range(2))
         scaled = scale * made.astype(F32)
         upper = scaled.astype(BF)
         lower = (scaled - upper.astype(F32)).astype(BF)
-        mix, gto = dot(spread, upper) + dot(spread, lower), dot(spread, grads)
-        if held:
-            mix, gto = mix + held[0][:, cols], gto + held[1][:, cols]
-        mixed[:, cols] = mix.astype(mixed.dtype)
-        gtok[:, cols] = gto.astype(gtok.dtype)
-        scores += dot_last(made, cotangent[:, cols])
+        mix, gto = dot(twice, jnp.concatenate([upper, lower], axis=0)), dot(spread, grads)
+        given = []
+        for sa in range(SIDE):
+            blk = jnp.where(flip == 0, ((y + sb) & 3) * SIDE + sa, sa * SIDE + ((x + sb) & 3))
+            cols = pl.ds(pl.multiple_of(blk * COLS, COLS), COLS)
+            part = slice(sa * COLS, sa * COLS + COLS)
+            one, two = mix[:, part], gto[:, part]
+            if held:
+                one, two = one + held[0][:, cols], two + held[1][:, cols]
+            mixed[:, cols] = one.astype(mixed.dtype)
+            gtok[:, cols] = two.astype(gtok.dtype)
+            given.append(cotangent[:, cols])
+        scores += dot_last(made, jnp.concatenate(given, axis=1))
     picked = chosen * scores
     total = held[2][...] if held else jnp.zeros(ids.shape, F32)
     for r in range(SIDE):
@@ -276,7 +301,8 @@
         0,
         hbm=3,
         vmem=60 * 2**20,
-        scratch=[pltpu.SemaphoreType.DMA((3,))],
+        scratch=[pltpu.VMEM((3, COLS, FW), BF), pltpu.SemaphoreType.DMA((2, 6))],
+        out_space=pltpu.HBM,
     )
     ws = lax.all_gather(held, AXES, axis_index_groups=groups_a())
 
@@ -350,7 +376,20 @@
     sums = combine(0, F32, backs)
     mixed, gtok, gg_t = combine(1, BF, (*late, *sums))
     total, _ = lax.optimization_barrier((total, gg_t))
-    gw = call(total_kernel, [shape((1, COLS, FW), F32)] * 3, (total,), 0)
+    gw = call(
+        total_kernel,
+        [shape((1, COLS, FW), F32)] * 3,
+        (total,),
+        0,
+        hbm=1,
+        scratch=[
+            pltpu.VMEM((3, COLS, FW), BF),
+            pltpu.VMEM((3, COLS, FW), F32),
+            pltpu.SemaphoreType.DMA((2, 3)),
+        ],
+        vmem=60 * 2**20,
+        out_space=pltpu.HBM,
+    )
     return mixed, gtok, gg_t.T, *gw
 
 

time: 152 us -> 152 us (level)
    unnamed x26 -> x24, local copies, waits for them, and re-layouts: 7.26 us -> 5.99 us
where the time goes in v5:
time: 152 us; the launch traced here: 150 us
  starting transfers between devices  54.2 us (36%)
  waiting for transfers between devices  52.1 us (34%)
  Pallas kernels  23.2 us (15%)
  between operations  14.3 us (9%)
  local copies, waits for them, and re-layouts  5.99 us (4%)
    ppermute x24, waiting for transfers between devices, shift_b(): lax.ppermute(v, AXES, _perm(lambda y, x, z, c: (y + s, x, z, c) if c == 0...  34.7 us
    ppermute x14, starting transfers between devices, shift_z(): lax.ppermute(v, AXES, _perm(lambda y, x, z, c: (y, x, z + dz, c + dc)))  30.6 us
    ppermute x24, starting transfers between devices, shift_b(): lax.ppermute(v, AXES, _perm(lambda y, x, z, c: (y + s, x, z, c) if c == 0...  23.5 us
    pallas_call x15, Pallas kernels, call(): pl.pallas_call(kernel, out_shape=tuple(outs), in_specs=[pl.BlockSpec(memo...  23.2 us
    ppermute x14, waiting for transfers between devices, shift_z(): lax.ppermute(v, AXES, _perm(lambda y, x, z, c: (y, x, z + dz, c + dc)))  17.4 us
    unnamed x24, local copies, waits for them, and re-layouts  5.99 us
  transfers between devices with their start and end apart: 40, of which 21 were waited for; matrix products, arithmetic and copies ran while one was open for 0% of the time, Pallas kernels for 9%

profile of v5, /device:TPU:1, one launch (start us, length us, event | category | flops | bytes accessed | tf_op | source)
XLA Modules:
  0.0 150.4 jit_solution(1545922521486331708)
XLA Ops:
  7.2 2.2 %shard_map.121 = bf16[3,256,768]{2,1,0:T(8,128)(2,1)} custom-call(bf16[1,256,768]{2,1,0:T(8,128)(2,1)} %gate.1, bf16[1,256,768]{2,1,0:T(8,128)(2,1)} %up.1, bf16[1,256,768]{2,1,0:T(8,128)(2,1)} %down.1), custom_call_target="tpu_custom_call" | custom-call | bytes 1024 | tf_op jit(solution)/shard_map/pallas_call | solution.py:62
  10.1 4.1 %shard_map.118 = (bf16[2,4,16,1024]{3,2,1,0:T(8,128)(2,1)}, bf16[2,4,16,1024]{3,2,1,0:T(8,128)(2,1)}, bf16[2,4,16,1024]{3,2,1,0:T(8,128)(2,1)}, bf16[2,4,16,1024...) custom-call(s32[4]{0:T(128)} %pad_add_fusion.place, ...), custom_call_target="tpu_custom_call" | custom-call | flops 2684354 | bytes 1024 | tf_op jit(solution)/shard_map/pallas_call | solution.py:62
  14.2 2.5 %collective-permute-start = (bf16[2,4,16,1024]{3,2,1,0:T(8,128)(2,1)}, bf16[2,4,16,1024]{3,2,1,0:T(8,128)(2,1)S(1)}, u32[]{:S(2)}, u32[]{:S(2)}) collective-permute-start(bf16[2,4,16,1024]{3,2,1,0:T(8,128)(2,1)} %get-tuple-element.73), channel_id=1, source_target_pairs={{0,2},{1,3},{2,4},{3,5},{4,6},{5,7},{6,0},{7,1},{8,10},{9,11},{10,... | collective-permute-start | bytes 786440 | tf_op jit(solution)/shard_map/ppermute | solution.py:45
  16.7 3.3 %collective-permute-start.1 = (bf16[2,4,16,1024]{3,2,1,0:T(8,128)(2,1)}, bf16[2,4,16,1024]{3,2,1,0:T(8,128)(2,1)S(1)}, u32[]{:S(2)}, u32[]{:S(2)}) collective-permute-start(bf16[2,4,16,1024]{3,2,1,0:T(8,128)(2,1)} %get-tuple-element.74), channel_id=1, source_target_pairs={{0,4},{1,5},{2,6},{3,7},{4,0},{5,1},{6,2},{7,3},{8,12},{9,13},{10,... | collective-permute-start | bytes 786440 | tf_op jit(solution)/shard_map/ppermute | solution.py:45
  20.8 1.5 %collective-permute-start.6 = (bf16[2,4,16,1024]{3,2,1,0:T(8,128)(2,1)}, bf16[2,4,16,1024]{3,2,1,0:T(8,128)(2,1)S(1)}, u32[]{:S(2)}, u32[]{:S(2)}) collective-permute-start(bf16[2,4,16,1024]{3,2,1,0:T(8,128)(2,1)} %get-tuple-element.80), channel_id=1, source_target_pairs={{0,1},{1,0},{2,3},{3,2},{4,5},{5,4},{6,7},{7,6},{8,9},{9,8},{10,11... | collective-permute-start | bytes 786440 | tf_op jit(solution)/shard_map/ppermute | solution.py:45
  22.9 2.2 %collective-permute-done.refs_1_ = bf16[2,4,16,1024]{3,2,1,0:T(8,128)(2,1)S(1)} collective-permute-done((bf16[2,4,16,1024]{3,2,1,0:T(8,128)(2,1)}, bf16[2,4,16,1024]{3,2,1,0:T(8,128)(2,1)S(1)}, u32[]{:S(2)}, u32[]{:S(2)}) %collective-permute-start) | collective-permute-done | bytes 262176 | tf_op jit(solution)/shard_map/ppermute | solution.py:45
  25.1 9.2 %collective-permute-start.8 = (bf16[2,4,16,1024]{3,2,1,0:T(8,128)(2,1)}, bf16[2,4,16,1024]{3,2,1,0:T(8,128)(2,1)S(1)}, u32[]{:S(2)}, u32[]{:S(2)}) collective-permute-start(bf16[2,4,16,1024]{3,2,1,0:T(8,128)(2,1)} %get-tuple-element.82), channel_id=1, source_target_pairs={{0,5},{1,4},{2,7},{3,6},{4,1},{5,0},{6,3},{7,2},{8,13},{9,12},{10,... | collective-permute-start | bytes 786440 | tf_op jit(solution)/shard_map/ppermute | solution.py:45
  34.3 0.9 copy-done.4
  35.3 1.3 collective-permute-start.3
  36.6 2.5 %collective-permute-start.4 = (bf16[2,64,1024]{2,1,0:T(8,128)(2,1)S(1)}, bf16[2,64,1024]{2,1,0:T(8,128)(2,1)S(1)}, u32[]{:S(2)}, u32[]{:S(2)}) collective-permute-start(bf16[2,64,1024]{2,1,0:T(8,128)(2,1)S(1)} %get-tuple-element.78), channel_id=1, source_target_pairs={{0,64},{1,17},{2,66},{3,19},{4,68},{5,21},{6,70},{7,23},{8,72},{9,... | collective-permute-start | bytes 786440 | tf_op jit(solution)/shard_map/ppermute | solution.py:39
  39.1 1.1 collective-permute-start.5
  40.2 3.5 %collective-permute-done.8.refs_2_ = bf16[2,4,16,1024]{3,2,1,0:T(8,128)(2,1)S(1)} collective-permute-done((bf16[2,4,16,1024]{3,2,1,0:T(8,128)(2,1)}, bf16[2,4,16,1024]{3,2,1,0:T(8,128)(2,1)S(1)}, u32[]{:S(2)}, u32[]{:S(2)}) %collective-permute-start.8) | collective-permute-done | bytes 262176 | tf_op jit(solution)/shard_map/ppermute | solution.py:45
  43.8 1.2 collective-permute-start.10
  45.1 2.5 %collective-permute-start.11 = (bf16[2,64,1024]{2,1,0:T(8,128)(2,1)S(1)}, bf16[2,64,1024]{2,1,0:T(8,128)(2,1)S(1)}, u32[]{:S(2)}, u32[]{:S(2)}) collective-permute-start(bf16[2,64,1024]{2,1,0:T(8,128)(2,1)S(1)} %get-tuple-element.86), channel_id=1, source_target_pairs={{0,64},{1,17},{2,66},{3,19},{4,68},{5,21},{6,70},{7,23},{8,72},{9,... | collective-permute-start | bytes 786440 | tf_op jit(solution)/shard_map/ppermute | solution.py:39
  47.6 1.1 collective-permute-start.12
  48.7 2.8 %collective-permute-done.4.refs_2_.refs_10_ = bf16[2,64,1024]{2,1,0:T(8,128)(2,1)S(1)} collective-permute-done((bf16[2,64,1024]{2,1,0:T(8,128)(2,1)S(1)}, bf16[2,64,1024]{2,1,0:T(8,128)(2,1)S(1)}, u32[]{:S(2)}, u32[]{:S(2)}) %collective-permute-start.4) | collective-permute-done | bytes 262176 | tf_op jit(solution)/shard_map/ppermute | solution.py:39
  51.5 3.8 %collective-permute-done.10.refs_5_.refs_13_ = bf16[2,64,1024]{2,1,0:T(8,128)(2,1)S(1)} collective-permute-done((bf16[2,64,1024]{2,1,0:T(8,128)(2,1)S(1)}, bf16[2,64,1024]{2,1,0:T(8,128)(2,1)S(1)}, u32[]{:S(2)}, u32[]{:S(2)}) %collective-permute-start.10) | collective-permute-done | bytes 262176 | tf_op jit(solution)/shard_map/ppermute | solution.py:39
  55.4 2.7 %collective-permute-done.11.refs_6_.refs_14_ = bf16[2,64,1024]{2,1,0:T(8,128)(2,1)S(1)} collective-permute-done((bf16[2,64,1024]{2,1,0:T(8,128)(2,1)S(1)}, bf16[2,64,1024]{2,1,0:T(8,128)(2,1)S(1)}, u32[]{:S(2)}, u32[]{:S(2)}) %collective-permute-start.11) | collective-permute-done | bytes 262176 | tf_op jit(solution)/shard_map/ppermute | solution.py:39
  58.1 2.3 %copy-done = bf16[12,256,768]{2,1,0:T(8,128)(2,1)S(1)} copy-done((bf16[12,256,768]{2,1,0:T(8,128)(2,1)S(1)}, bf16[12,256,768]{2,1,0:T(8,128)(2,1)}, u32[]{:S(2)}) %copy-start) | copy-done | bytes 4718616
  60.4 2.6 %shard_map.122 = (f32[64,2304]{1,0:T(8,128)S(1)}, bf16[64,2304]{1,0:T(8,128)(2,1)S(1)}, bf16[64,2304]{1,0:T(8,128)(2,1)S(1)}, bf16[64,2304]{1,0:T(8,128)(2,1)S(1...) custom-call(bf16[2,64,1024]{2,1,0:T(8,128)(2,1)S(1)} %get-tuple-elem, ...), custom_call_target="tpu_custom_call" | custom-call | flops 24159192 | bytes 1024 | tf_op jit(solution)/shard_map/pallas_call | solution.py:62
  63.9 1.3 collective-permute-start.20
  65.9 2.0 %collective-permute-start.13 = (bf16[64,2304]{1,0:T(8,128)(2,1)S(1)}, bf16[64,2304]{1,0:T(8,128)(2,1)S(1)}, u32[]{:S(2)}, u32[]{:S(2)}) collective-permute-start(bf16[64,2304]{1,0:T(8,128)(2,1)S(1)} %get-tuple-element.89), channel_id=1, source_target_pairs={{0,96},{1,25},{2,98},{3,27},{4,100},{5,29},{6,102},{7,31},{8,104},... | collective-permute-start | bytes 884744 | tf_op jit(solution)/shard_map/ppermute | solution.py:39
  69.3 2.1 %collective-permute-done.20.p2 = bf16[64,2304]{1,0:T(8,128)(2,1)S(1)} collective-permute-done((bf16[64,2304]{1,0:T(8,128)(2,1)S(1)}, bf16[64,2304]{1,0:T(8,128)(2,1)S(1)}, u32[]{:S(2)}, u32[]{:S(2)}) %collective-permute-start.20) | collective-permute-done | bytes 294944 | tf_op jit(solution)/shard_map/ppermute | solution.py:39
  71.4 3.1 %collective-permute-done.21.p3 = bf16[64,2304]{1,0:T(8,128)(2,1)S(1)} collective-permute-done((bf16[64,2304]{1,0:T(8,128)(2,1)S(1)}, bf16[64,2304]{1,0:T(8,128)(2,1)S(1)}, u32[]{:S(2)}, u32[]{:S(2)}) %collective-permute-start.21) | collective-permute-done | bytes 294944 | tf_op jit(solution)/shard_map/ppermute | solution.py:39
  75.1 1.3 collective-permute-start.23
  77.7 3.1 %collective-permute-done.15.p3 = bf16[64,2304]{1,0:T(8,128)(2,1)S(1)} collective-permute-done((bf16[64,2304]{1,0:T(8,128)(2,1)S(1)}, bf16[64,2304]{1,0:T(8,128)(2,1)S(1)}, u32[]{:S(2)}, u32[]{:S(2)}) %collective-permute-start.15) | collective-permute-done | bytes 294944 | tf_op jit(solution)/shard_map/ppermute | solution.py:39
  81.5 1.3 collective-permute-start.17
  84.1 3.0 %collective-permute-done.22.refs_1_ = bf16[64,2304]{1,0:T(8,128)(2,1)S(1)} collective-permute-done((bf16[64,2304]{1,0:T(8,128)(2,1)S(1)}, bf16[64,2304]{1,0:T(8,128)(2,1)S(1)}, u32[]{:S(2)}, u32[]{:S(2)}) %collective-permute-start.22) | collective-permute-done | bytes 294944 | tf_op jit(solution)/shard_map/ppermute | solution.py:39
  87.1 1.4 shard_map.125
  89.0 1.3 collective-permute-start.29
  90.7 2.7 %collective-permute-done.16.refs_1_.refs_5_ = bf16[64,2304]{1,0:T(8,128)(2,1)S(1)} collective-permute-done((bf16[64,2304]{1,0:T(8,128)(2,1)S(1)}, bf16[64,2304]{1,0:T(8,128)(2,1)S(1)}, u32[]{:S(2)}, u32[]{:S(2)}) %collective-permute-start.16) | collective-permute-done | bytes 294944 | tf_op jit(solution)/shard_map/ppermute | solution.py:39
  93.4 2.1 %shard_map.126 = (bf16[2,64,1024]{2,1,0:T(8,128)(2,1)S(1)}, bf16[2,64,1024]{2,1,0:T(8,128)(2,1)}, bf16[2,64,1024]{2,1,0:T(8,128)(2,1)S(1)}, bf16[2,64,1024]{2,1,0:T(8,128)(2,1)S(1)}) custom-call(bf16[64,2304]{1,0:T(8,128)(2,1)S(1)} %shard_map.123.refs_0_.refs_4_, bf16[64,2304]{1,0:T(8,128)(2,1)S(1)} %collective-permute-done.16.refs_1_.refs_5_, ...), custom_call_target="tpu_custom_call" | custom-call | flops 12079595 | bytes 1024 | tf_op jit(solution)/shard_map/pallas_call | solution.py:62
  96.5 2.8 %collective-permute-done.30.refs_3_ = bf16[2,64,1024]{2,1,0:T(8,128)(2,1)S(1)} collective-permute-done((bf16[2,64,1024]{2,1,0:T(8,128)(2,1)S(1)}, bf16[2,64,1024]{2,1,0:T(8,128)(2,1)S(1)}, u32[]{:S(2)}, u32[]{:S(2)}) %collective-permute-start.30) | collective-permute-done | bytes 262176 | tf_op jit(solution)/shard_map/ppermute | solution.py:39
  99.3 2.6 %shard_map.128 = bf16[4,3,256,768]{3,2,1,0:T(8,128)(2,1)S(1)} custom-call(bf16[64,2304]{1,0:T(8,128)(2,1)S(1)} %shard_map.124.refs_0_, bf16[64,2304]{1,0:T(8,128)(2,1)S(1)} %collective-permute-done.22.refs_1_, bf16[64,2304]{1,0:T(8,128)(2,1)S(1)} %collective-permute-done.23.refs_2_, bf16[64,2304]{1,0:T(8,128)(2,1)S(1)} %collective-permute-done.24.refs_3_, ...), custom_call_target="tpu_custom_call" | custom-call | flops 24159192 | bytes 1024 | tf_op jit(solution)/shard_map/pallas_call | solution.py:62
  102.0 2.2 %copy-done.2 = bf16[4,3,256,768]{3,2,1,0:T(8,128)(2,1)} copy-done((bf16[4,3,256,768]{3,2,1,0:T(8,128)(2,1)}, bf16[4,3,256,768]{3,2,1,0:T(8,128)(2,1)S(1)}, u32[]{:S(2)}) %copy-start.2) | copy-done | bytes 4718616
  105.1 1.1 collective-permute-start.26
  106.2 2.7 %collective-permute-start.35 = (bf16[2,4,16,1024]{3,2,1,0:T(8,128)(2,1)S(1)}, bf16[2,4,16,1024]{3,2,1,0:T(8,128)(2,1)S(1)}, u32[]{:S(2)}, u32[]{:S(2)}) collective-permute-start(bf16[2,4,16,1024]{3,2,1,0:T(8,128)(2,1)S(1)} %get-tuple-element.125), channel_id=1, source_target_pairs={{0,6},{1,7},{2,0},{3,1},{4,2},{5,3},{6,4},{7,5},{8,14},{9,15},{10,... | collective-permute-start | bytes 786440 | tf_op jit(solution)/shard_map/ppermute | solution.py:45
  110.0 2.2 %collective-permute-done.26.refs_2_ = bf16[2,64,1024]{2,1,0:T(8,128)(2,1)S(1)} collective-permute-done((bf16[2,64,1024]{2,1,0:T(8,128)(2,1)S(1)}, bf16[2,64,1024]{2,1,0:T(8,128)(2,1)S(1)}, u32[]{:S(2)}, u32[]{:S(2)}) %collective-permute-start.26) | collective-permute-done | bytes 262176 | tf_op jit(solution)/shard_map/ppermute | solution.py:39
  112.2 2.8 %collective-permute-done.27.refs_3_ = bf16[2,64,1024]{2,1,0:T(8,128)(2,1)S(1)} collective-permute-done((bf16[2,64,1024]{2,1,0:T(8,128)(2,1)S(1)}, bf16[2,64,1024]{2,1,0:T(8,128)(2,1)S(1)}, u32[]{:S(2)}, u32[]{:S(2)}) %collective-permute-start.27) | collective-permute-done | bytes 262176 | tf_op jit(solution)/shard_map/ppermute | solution.py:39
  114.9 1.4 collective-permute-start.37
  116.4 4.5 %collective-permute-start.31 = (bf16[2,4,16,1024]{3,2,1,0:T(8,128)(2,1)S(1)}, bf16[2,4,16,1024]{3,2,1,0:T(8,128)(2,1)S(1)}, u32[]{:S(2)}, u32[]{:S(2)}) collective-permute-start(bf16[2,4,16,1024]{3,2,1,0:T(8,128)(2,1)S(1)} %get-tuple-element.121), channel_id=1, source_target_pairs={{0,1},{1,0},{2,3},{3,2},{4,5},{5,4},{6,7},{7,6},{8,9},{9,8},{10,11... | collective-permute-start | bytes 786440 | tf_op jit(solution)/shard_map/ppermute | solution.py:45
  121.2 3.1 %collective-permute-start.33 = (bf16[2,4,16,1024]{3,2,1,0:T(8,128)(2,1)S(1)}, bf16[2,4,16,1024]{3,2,1,0:T(8,128)(2,1)S(1)}, u32[]{:S(2)}, u32[]{:S(2)}) collective-permute-start(bf16[2,4,16,1024]{3,2,1,0:T(8,128)(2,1)S(1)} %get-tuple-element.123), channel_id=1, source_target_pairs={{0,5},{1,4},{2,7},{3,6},{4,1},{5,0},{6,3},{7,2},{8,13},{9,12},{10,... | collective-permute-start | bytes 786440 | tf_op jit(solution)/shard_map/ppermute | solution.py:45
  124.4 1.9 %shard_map.130 = (f32[128,4096]{1,0:T(8,128)S(1)}, f32[128,4096]{1,0:T(8,128)S(1)}, f32[8,128]{1,0:T(8,128)S(1)}) custom-call(s32[4]{0:T(128)S(1)} %copy-done.7, s32[8,128]{1,0:T(8,128)S(1)} %bitcast.13, f32[8,128]{1,0:T(8,128)S(1)} %bitcast.16, bf16[128,4096]{1,0:T(8,128)(2,1)S(1)} %copy-done.3, bf16[2,4,16,1024]{3,2,1,0:T(8,128)(2,1)S(1)} %get-tuple-element.112.refs_0_, ...), custom_call_target="tpu_custom_call" | custom-call | flops 2684354 | bytes 1024 | tf_op jit(solution)/shard_map/pallas_call | solution.py:62
  126.3 3.6 %collective-permute-done.32.refs_1_ = bf16[2,4,16,1024]{3,2,1,0:T(8,128)(2,1)S(1)} collective-permute-done((bf16[2,4,16,1024]{3,2,1,0:T(8,128)(2,1)S(1)}, bf16[2,4,16,1024]{3,2,1,0:T(8,128)(2,1)S(1)}, u32[]{:S(2)}, u32[]{:S(2)}) %collective-permute-start.32) | collective-permute-done | bytes 262176 | tf_op jit(solution)/shard_map/ppermute | solution.py:45
  129.8 3.2 %collective-permute-done.33.refs_2_ = bf16[2,4,16,1024]{3,2,1,0:T(8,128)(2,1)S(1)} collective-permute-done((bf16[2,4,16,1024]{3,2,1,0:T(8,128)(2,1)S(1)}, bf16[2,4,16,1024]{3,2,1,0:T(8,128)(2,1)S(1)}, u32[]{:S(2)}, u32[]{:S(2)}) %collective-permute-start.33) | collective-permute-done | bytes 262176 | tf_op jit(solution)/shard_map/ppermute | solution.py:45
  133.0 4.9 %collective-permute-done.34.refs_3_ = bf16[2,4,16,1024]{3,2,1,0:T(8,128)(2,1)S(1)} collective-permute-done((bf16[2,4,16,1024]{3,2,1,0:T(8,128)(2,1)S(1)}, bf16[2,4,16,1024]{3,2,1,0:T(8,128)(2,1)S(1)}, u32[]{:S(2)}, u32[]{:S(2)}) %collective-permute-start.34) | collective-permute-done | bytes 262176 | tf_op jit(solution)/shard_map/ppermute | solution.py:45
  137.9 3.1 %shard_map.131 = (bf16[128,4096]{1,0:T(8,128)(2,1)}, bf16[128,4096]{1,0:T(8,128)(2,1)}, f32[8,128]{1,0:T(8,128)}) custom-call(s32[4]{0:T(128)S(1)} %copy-done.7, s32[8,128]{1,0:T(8,128)S(1)} %bitcast.14, f32[8,128]{1,0:T(8,128)S(1)} %bitcast.17, bf16[128,4096]{1,0:T(8,128)(2,1)S(1)} %copy-done.3, ...), custom_call_target="tpu_custom_call" | custom-call | flops 2684354 | bytes 1024 | tf_op jit(solution)/shard_map/pallas_call | solution.py:62
  141.1 2.5 %shard_map.132 = (f32[1,256,768]{2,1,0:T(8,128)}, f32[1,256,768]{2,1,0:T(8,128)}, f32[1,256,768]{2,1,0:T(8,128)}) custom-call(bf16[3,256,768]{2,1,0:T(8,128)(2,1)} %bitcast.18), custom_call_target="tpu_custom_call" | custom-call | bytes 1024 | tf_op jit(solution)/shard_map/pallas_call | solution.py:62
  (74 shorter events, 13.7 us)
Async XLA Ops:
  7.2 50.9 %all-gather.3.cloned.1.call-start = ((), (), s32[]{:S(2)}) async-start(), calls=%async_computation.2 | async-start | bytes 5898240 | tf_op jit(solution)/shard_map/all_gather | solution.py:307
  9.4 131.7 %reduce-scatter.2.cloned.1.call-start = ((), (), s32[]{:S(2)}) async-start(), calls=%async_computation.1 | async-start | bytes 5898240 | tf_op jit(solution)/shard_map/reduce_scatter | solution.py:364
  14.2 10.9 %collective-permute-start = (bf16[2,4,16,1024]{3,2,1,0:T(8,128)(2,1)}, bf16[2,4,16,1024]{3,2,1,0:T(8,128)(2,1)S(1)}, u32[]{:S(2)}, u32[]{:S(2)}) collective-permute-start(bf16[2,4,16,1024]{3,2,1,0:T(8,128)(2,1)} %get-tuple-element.73), channel_id=1, source_target_pairs={{0,2},{1,3},{2,4},{3,5},{4,6},{5,7},{6,0},{7,1},{8,10},{9,11},{10,... | collective-permute-start | bytes 786440 | tf_op jit(solution)/shard_map/ppermute | solution.py:45
  16.7 17.5 %collective-permute-start.1 = (bf16[2,4,16,1024]{3,2,1,0:T(8,128)(2,1)}, bf16[2,4,16,1024]{3,2,1,0:T(8,128)(2,1)S(1)}, u32[]{:S(2)}, u32[]{:S(2)}) collective-permute-start(bf16[2,4,16,1024]{3,2,1,0:T(8,128)(2,1)} %get-tuple-element.74), channel_id=1, source_target_pairs={{0,4},{1,5},{2,6},{3,7},{4,0},{5,1},{6,2},{7,3},{8,12},{9,13},{10,... | collective-permute-start | bytes 786440 | tf_op jit(solution)/shard_map/ppermute | solution.py:45
  20.0 14.3 %collective-permute-start.2 = (bf16[2,4,16,1024]{3,2,1,0:T(8,128)(2,1)}, bf16[2,4,16,1024]{3,2,1,0:T(8,128)(2,1)S(1)}, u32[]{:S(2)}, u32[]{:S(2)}) collective-permute-start(bf16[2,4,16,1024]{3,2,1,0:T(8,128)(2,1)} %get-tuple-element.75), channel_id=1, source_target_pairs={{0,6},{1,7},{2,0},{3,1},{4,2},{5,3},{6,4},{7,5},{8,14},{9,15},{10,... | collective-permute-start | bytes 786440 | tf_op jit(solution)/shard_map/ppermute | solution.py:45
  20.8 15.8 %collective-permute-start.6 = (bf16[2,4,16,1024]{3,2,1,0:T(8,128)(2,1)}, bf16[2,4,16,1024]{3,2,1,0:T(8,128)(2,1)S(1)}, u32[]{:S(2)}, u32[]{:S(2)}) collective-permute-start(bf16[2,4,16,1024]{3,2,1,0:T(8,128)(2,1)} %get-tuple-element.80), channel_id=1, source_target_pairs={{0,1},{1,0},{2,3},{3,2},{4,5},{5,4},{6,7},{7,6},{8,9},{9,8},{10,11... | collective-permute-start | bytes 786440 | tf_op jit(solution)/shard_map/ppermute | solution.py:45
  22.3 16.8 %collective-permute-start.7 = (bf16[2,4,16,1024]{3,2,1,0:T(8,128)(2,1)}, bf16[2,4,16,1024]{3,2,1,0:T(8,128)(2,1)S(1)}, u32[]{:S(2)}, u32[]{:S(2)}) collective-permute-start(bf16[2,4,16,1024]{3,2,1,0:T(8,128)(2,1)} %get-tuple-element.81), channel_id=1, source_target_pairs={{0,3},{1,2},{2,5},{3,4},{4,7},{5,6},{6,1},{7,0},{8,11},{9,10},{10,... | collective-permute-start | bytes 786440 | tf_op jit(solution)/shard_map/ppermute | solution.py:45
  25.1 18.7 %collective-permute-start.8 = (bf16[2,4,16,1024]{3,2,1,0:T(8,128)(2,1)}, bf16[2,4,16,1024]{3,2,1,0:T(8,128)(2,1)S(1)}, u32[]{:S(2)}, u32[]{:S(2)}) collective-permute-start(bf16[2,4,16,1024]{3,2,1,0:T(8,128)(2,1)} %get-tuple-element.82), channel_id=1, source_target_pairs={{0,5},{1,4},{2,7},{3,6},{4,1},{5,0},{6,3},{7,2},{8,13},{9,12},{10,... | collective-permute-start | bytes 786440 | tf_op jit(solution)/shard_map/ppermute | solution.py:45
  34.3 9.5 %collective-permute-start.9 = (bf16[2,4,16,1024]{3,2,1,0:T(8,128)(2,1)}, bf16[2,4,16,1024]{3,2,1,0:T(8,128)(2,1)S(1)}, u32[]{:S(2)}, u32[]{:S(2)}) collective-permute-start(bf16[2,4,16,1024]{3,2,1,0:T(8,128)(2,1)} %get-tuple-element.83), channel_id=1, source_target_pairs={{0,7},{1,6},{2,1},{3,0},{4,3},{5,2},{6,5},{7,4},{8,15},{9,14},{10,... | collective-permute-start | bytes 786440 | tf_op jit(solution)/shard_map/ppermute | solution.py:45
  35.3 12.2 %collective-permute-start.3 = (bf16[2,64,1024]{2,1,0:T(8,128)(2,1)S(1)}, bf16[2,64,1024]{2,1,0:T(8,128)(2,1)S(1)}, u32[]{:S(2)}, u32[]{:S(2)}) collective-permute-start(bf16[2,64,1024]{2,1,0:T(8,128)(2,1)S(1)} %get-tuple-element.77), channel_id=1, source_target_pairs={{0,32},{1,9},{2,34},{3,11},{4,36},{5,13},{6,38},{7,15},{8,40},{9,1... | collective-permute-start | bytes 786440 | tf_op jit(solution)/shard_map/ppermute | solution.py:39
  36.6 14.9 %collective-permute-start.4 = (bf16[2,64,1024]{2,1,0:T(8,128)(2,1)S(1)}, bf16[2,64,1024]{2,1,0:T(8,128)(2,1)S(1)}, u32[]{:S(2)}, u32[]{:S(2)}) collective-permute-start(bf16[2,64,1024]{2,1,0:T(8,128)(2,1)S(1)} %get-tuple-element.78), channel_id=1, source_target_pairs={{0,64},{1,17},{2,66},{3,19},{4,68},{5,21},{6,70},{7,23},{8,72},{9,... | collective-permute-start | bytes 786440 | tf_op jit(solution)/shard_map/ppermute | solution.py:39
  39.1 12.5 %collective-permute-start.5 = (bf16[2,64,1024]{2,1,0:T(8,128)(2,1)S(1)}, bf16[2,64,1024]{2,1,0:T(8,128)(2,1)S(1)}, u32[]{:S(2)}, u32[]{:S(2)}) collective-permute-start(bf16[2,64,1024]{2,1,0:T(8,128)(2,1)S(1)} %get-tuple-element.79), channel_id=1, source_target_pairs={{0,96},{1,25},{2,98},{3,27},{4,100},{5,29},{6,102},{7,31},{8,104},... | collective-permute-start | bytes 786440 | tf_op jit(solution)/shard_map/ppermute | solution.py:39
  43.8 11.5 %collective-permute-start.10 = (bf16[2,64,1024]{2,1,0:T(8,128)(2,1)S(1)}, bf16[2,64,1024]{2,1,0:T(8,128)(2,1)S(1)}, u32[]{:S(2)}, u32[]{:S(2)}) collective-permute-start(bf16[2,64,1024]{2,1,0:T(8,128)(2,1)S(1)} %get-tuple-element.85), channel_id=1, source_target_pairs={{0,32},{1,9},{2,34},{3,11},{4,36},{5,13},{6,38},{7,15},{8,40},{9,1... | collective-permute-start | bytes 786440 | tf_op jit(solution)/shard_map/ppermute | solution.py:39
  45.1 13.0 %collective-permute-start.11 = (bf16[2,64,1024]{2,1,0:T(8,128)(2,1)S(1)}, bf16[2,64,1024]{2,1,0:T(8,128)(2,1)S(1)}, u32[]{:S(2)}, u32[]{:S(2)}) collective-permute-start(bf16[2,64,1024]{2,1,0:T(8,128)(2,1)S(1)} %get-tuple-element.86), channel_id=1, source_target_pairs={{0,64},{1,17},{2,66},{3,19},{4,68},{5,21},{6,70},{7,23},{8,72},{9,... | collective-permute-start | bytes 786440 | tf_op jit(solution)/shard_map/ppermute | solution.py:39
  47.6 10.5 %collective-permute-start.12 = (bf16[2,64,1024]{2,1,0:T(8,128)(2,1)S(1)}, bf16[2,64,1024]{2,1,0:T(8,128)(2,1)S(1)}, u32[]{:S(2)}, u32[]{:S(2)}) collective-permute-start(bf16[2,64,1024]{2,1,0:T(8,128)(2,1)S(1)} %get-tuple-element.87), channel_id=1, source_target_pairs={{0,96},{1,25},{2,98},{3,27},{4,100},{5,29},{6,102},{7,31},{8,104},... | collective-permute-start | bytes 786440 | tf_op jit(solution)/shard_map/ppermute | solution.py:39
  58.1 2.3 %copy-start = (bf16[12,256,768]{2,1,0:T(8,128)(2,1)S(1)}, bf16[12,256,768]{2,1,0:T(8,128)(2,1)}, u32[]{:S(2)}) copy-start(bf16[12,256,768]{2,1,0:T(8,128)(2,1)} %all-gather.3.cloned.1.call-done) | copy-start | bytes 14155780
  60.4 26.7 %copy-start.1 = (bf16[12,256,768]{2,1,0:T(8,128)(2,1)S(1)}, bf16[12,256,768]{2,1,0:T(8,128)(2,1)}, u32[]{:S(2)}) copy-start(bf16[12,256,768]{2,1,0:T(8,128)(2,1)} %all-gather.3.cloned.1.call-done) | copy-start | bytes 14155780
  63.0 5.9 %collective-permute-start.19 = (bf16[64,2304]{1,0:T(8,128)(2,1)S(1)}, bf16[64,2304]{1,0:T(8,128)(2,1)S(1)}, u32[]{:S(2)}, u32[]{:S(2)}) collective-permute-start(bf16[64,2304]{1,0:T(8,128)(2,1)S(1)} %get-tuple-element.93), channel_id=1, source_target_pairs={{0,96},{1,25},{2,98},{3,27},{4,100},{5,29},{6,102},{7,31},{8,104},... | collective-permute-start | bytes 884744 | tf_op jit(solution)/shard_map/ppermute | solution.py:39
  63.9 7.4 %collective-permute-start.20 = (bf16[64,2304]{1,0:T(8,128)(2,1)S(1)}, bf16[64,2304]{1,0:T(8,128)(2,1)S(1)}, u32[]{:S(2)}, u32[]{:S(2)}) collective-permute-start(bf16[64,2304]{1,0:T(8,128)(2,1)S(1)} %get-tuple-element.94), channel_id=1, source_target_pairs={{0,64},{1,17},{2,66},{3,19},{4,68},{5,21},{6,70},{7,23},{8,72},{9,... | collective-permute-start | bytes 884744 | tf_op jit(solution)/shard_map/ppermute | solution.py:39
  65.2 9.3 %collective-permute-start.21 = (bf16[64,2304]{1,0:T(8,128)(2,1)S(1)}, bf16[64,2304]{1,0:T(8,128)(2,1)S(1)}, u32[]{:S(2)}, u32[]{:S(2)}) collective-permute-start(bf16[64,2304]{1,0:T(8,128)(2,1)S(1)} %get-tuple-element.95), channel_id=1, source_target_pairs={{0,32},{1,9},{2,34},{3,11},{4,36},{5,13},{6,38},{7,15},{8,40},{9,1... | collective-permute-start | bytes 884744 | tf_op jit(solution)/shard_map/ppermute | solution.py:39
  65.9 10.5 %collective-permute-start.13 = (bf16[64,2304]{1,0:T(8,128)(2,1)S(1)}, bf16[64,2304]{1,0:T(8,128)(2,1)S(1)}, u32[]{:S(2)}, u32[]{:S(2)}) collective-permute-start(bf16[64,2304]{1,0:T(8,128)(2,1)S(1)} %get-tuple-element.89), channel_id=1, source_target_pairs={{0,96},{1,25},{2,98},{3,27},{4,100},{5,29},{6,102},{7,31},{8,104},... | collective-permute-start | bytes 884744 | tf_op jit(solution)/shard_map/ppermute | solution.py:39
  67.9 9.8 %collective-permute-start.14 = (bf16[64,2304]{1,0:T(8,128)(2,1)S(1)}, bf16[64,2304]{1,0:T(8,128)(2,1)S(1)}, u32[]{:S(2)}, u32[]{:S(2)}) collective-permute-start(bf16[64,2304]{1,0:T(8,128)(2,1)S(1)} %get-tuple-element.90), channel_id=1, source_target_pairs={{0,64},{1,17},{2,66},{3,19},{4,68},{5,21},{6,70},{7,23},{8,72},{9,... | collective-permute-start | bytes 884744 | tf_op jit(solution)/shard_map/ppermute | solution.py:39
  69.0 11.8 %collective-permute-start.15 = (bf16[64,2304]{1,0:T(8,128)(2,1)S(1)}, bf16[64,2304]{1,0:T(8,128)(2,1)S(1)}, u32[]{:S(2)}, u32[]{:S(2)}) collective-permute-start(bf16[64,2304]{1,0:T(8,128)(2,1)S(1)} %get-tuple-element.91), channel_id=1, source_target_pairs={{0,32},{1,9},{2,34},{3,11},{4,36},{5,13},{6,38},{7,15},{8,40},{9,1... | collective-permute-start | bytes 884744 | tf_op jit(solution)/shard_map/ppermute | solution.py:39
  74.7 8.0 %collective-permute-start.24 = (bf16[64,2304]{1,0:T(8,128)(2,1)S(1)}, bf16[64,2304]{1,0:T(8,128)(2,1)S(1)}, u32[]{:S(2)}, u32[]{:S(2)}) collective-permute-start(bf16[64,2304]{1,0:T(8,128)(2,1)S(1)} %shard_map.124.refs_0_), channel_id=1, source_target_pairs={{0,96},{1,25},{2,98},{3,27},{4,100},{5,29},{6,102},{7,31},{8,104},... | collective-permute-start | bytes 884744 | tf_op jit(solution)/shard_map/ppermute | solution.py:39
  75.1 9.0 %collective-permute-start.23 = (bf16[64,2304]{1,0:T(8,128)(2,1)S(1)}, bf16[64,2304]{1,0:T(8,128)(2,1)S(1)}, u32[]{:S(2)}, u32[]{:S(2)}) collective-permute-start(bf16[64,2304]{1,0:T(8,128)(2,1)S(1)} %shard_map.124.refs_0_), channel_id=1, source_target_pairs={{0,64},{1,17},{2,66},{3,19},{4,68},{5,21},{6,70},{7,23},{8,72},{9,... | collective-permute-start | bytes 884744 | tf_op jit(solution)/shard_map/ppermute | solution.py:39
  76.4 10.8 %collective-permute-start.22 = (bf16[64,2304]{1,0:T(8,128)(2,1)S(1)}, bf16[64,2304]{1,0:T(8,128)(2,1)S(1)}, u32[]{:S(2)}, u32[]{:S(2)}) collective-permute-start(bf16[64,2304]{1,0:T(8,128)(2,1)S(1)} %shard_map.124.refs_0_), channel_id=1, source_target_pairs={{0,32},{1,9},{2,34},{3,11},{4,36},{5,13},{6,38},{7,15},{8,40},{9,1... | collective-permute-start | bytes 884744 | tf_op jit(solution)/shard_map/ppermute | solution.py:39
  81.0 9.3 %collective-permute-start.18 = (bf16[64,2304]{1,0:T(8,128)(2,1)S(1)}, bf16[64,2304]{1,0:T(8,128)(2,1)S(1)}, u32[]{:S(2)}, u32[]{:S(2)}) collective-permute-start(bf16[64,2304]{1,0:T(8,128)(2,1)S(1)} %shard_map.123.refs_0_.refs_4_), channel_id=1, source_target_pairs={{0,96},{1,25},{2,98},{3,27},{4,100},{5,29},{6,102},{7,31},{8,104},... | collective-permute-start | bytes 884744 | tf_op jit(solution)/shard_map/ppermute | solution.py:39
  81.5 9.3 %collective-permute-start.17 = (bf16[64,2304]{1,0:T(8,128)(2,1)S(1)}, bf16[64,2304]{1,0:T(8,128)(2,1)S(1)}, u32[]{:S(2)}, u32[]{:S(2)}) collective-permute-start(bf16[64,2304]{1,0:T(8,128)(2,1)S(1)} %shard_map.123.refs_0_.refs_4_), channel_id=1, source_target_pairs={{0,64},{1,17},{2,66},{3,19},{4,68},{5,21},{6,70},{7,23},{8,72},{9,... | collective-permute-start | bytes 884744 | tf_op jit(solution)/shard_map/ppermute | solution.py:39
  82.7 10.7 %collective-permute-start.16 = (bf16[64,2304]{1,0:T(8,128)(2,1)S(1)}, bf16[64,2304]{1,0:T(8,128)(2,1)S(1)}, u32[]{:S(2)}, u32[]{:S(2)}) collective-permute-start(bf16[64,2304]{1,0:T(8,128)(2,1)S(1)} %shard_map.123.refs_0_.refs_4_), channel_id=1, source_target_pairs={{0,32},{1,9},{2,34},{3,11},{4,36},{5,13},{6,38},{7,15},{8,40},{9,1... | collective-permute-start | bytes 884744 | tf_op jit(solution)/shard_map/ppermute | solution.py:39
  88.5 7.0 %collective-permute-start.28 = (bf16[2,64,1024]{2,1,0:T(8,128)(2,1)S(1)}, bf16[2,64,1024]{2,1,0:T(8,128)(2,1)S(1)}, u32[]{:S(2)}, u32[]{:S(2)}) collective-permute-start(bf16[2,64,1024]{2,1,0:T(8,128)(2,1)S(1)} %get-tuple-element.105), channel_id=1, source_target_pairs={{0,96},{1,25},{2,98},{3,27},{4,100},{5,29},{6,102},{7,31},{8,104},... | collective-permute-start | bytes 786440 | tf_op jit(solution)/shard_map/ppermute | solution.py:39
  89.0 7.4 %collective-permute-start.29 = (bf16[2,64,1024]{2,1,0:T(8,128)(2,1)S(1)}, bf16[2,64,1024]{2,1,0:T(8,128)(2,1)S(1)}, u32[]{:S(2)}, u32[]{:S(2)}) collective-permute-start(bf16[2,64,1024]{2,1,0:T(8,128)(2,1)S(1)} %get-tuple-element.106), channel_id=1, source_target_pairs={{0,64},{1,17},{2,66},{3,19},{4,68},{5,21},{6,70},{7,23},{8,72},{9,... | collective-permute-start | bytes 786440 | tf_op jit(solution)/shard_map/ppermute | solution.py:39
  90.3 8.9 %collective-permute-start.30 = (bf16[2,64,1024]{2,1,0:T(8,128)(2,1)S(1)}, bf16[2,64,1024]{2,1,0:T(8,128)(2,1)S(1)}, u32[]{:S(2)}, u32[]{:S(2)}) collective-permute-start(bf16[2,64,1024]{2,1,0:T(8,128)(2,1)S(1)} %get-tuple-element.107), channel_id=1, source_target_pairs={{0,32},{1,9},{2,34},{3,11},{4,36},{5,13},{6,38},{7,15},{8,40},{9,1... | collective-permute-start | bytes 786440 | tf_op jit(solution)/shard_map/ppermute | solution.py:39
  95.5 3.8 %copy-start.8 = (bf16[2,64,1024]{2,1,0:T(8,128)(2,1)}, bf16[2,64,1024]{2,1,0:T(8,128)(2,1)S(1)}, u32[]{:S(2)}) copy-start(bf16[2,64,1024]{2,1,0:T(8,128)(2,1)S(1)} %get-tuple-element.104) | copy-start | bytes 786436
  95.5 3.8 %copy-start.10 = (bf16[2,64,1024]{2,1,0:T(8,128)(2,1)}, bf16[2,64,1024]{2,1,0:T(8,128)(2,1)S(1)}, u32[]{:S(2)}) copy-start(bf16[2,64,1024]{2,1,0:T(8,128)(2,1)S(1)} %get-tuple-element.103) | copy-start | bytes 786436
  104.2 20.2 %copy-start.3 = (bf16[128,4096]{1,0:T(8,128)(2,1)S(1)}, bf16[128,4096]{1,0:T(8,128)(2,1)}, u32[]{:S(2)}) copy-start(bf16[128,4096]{1,0:T(8,128)(2,1)} %cotangent.5) | copy-start | bytes 3145732
  104.2 20.2 %copy-start.5 = (s32[128,8]{0,1:T(8,128)S(1)}, s32[128,8]{0,1:T(8,128)}, u32[]{:S(2)}) copy-start(s32[128,8]{0,1:T(8,128)} %param.8) | copy-start | bytes 12292
  104.2 20.2 %copy-start.6 = (f32[128,8]{0,1:T(8,128)S(1)}, f32[128,8]{0,1:T(8,128)}, u32[]{:S(2)}) copy-start(f32[128,8]{0,1:T(8,128)} %param.9) | copy-start | bytes 12292
  104.2 20.2 %copy-start.7 = (s32[4]{0:T(128)S(1)}, s32[4]{0:T(128)}, u32[]{:S(2)}) copy-start(s32[4]{0:T(128)} %pad_add_fusion.place) | copy-start | bytes 52
  104.2 5.8 %collective-permute-start.25 = (bf16[2,64,1024]{2,1,0:T(8,128)(2,1)}, bf16[2,64,1024]{2,1,0:T(8,128)(2,1)S(1)}, u32[]{:S(2)}, u32[]{:S(2)}) collective-permute-start(bf16[2,64,1024]{2,1,0:T(8,128)(2,1)} %get-tuple-element.102), channel_id=1, source_target_pairs={{0,96},{1,25},{2,98},{3,27},{4,100},{5,29},{6,102},{7,31},{8,104},... | collective-permute-start | bytes 786440 | tf_op jit(solution)/shard_map/ppermute | solution.py:39
  105.1 7.1 %collective-permute-start.26 = (bf16[2,64,1024]{2,1,0:T(8,128)(2,1)S(1)}, bf16[2,64,1024]{2,1,0:T(8,128)(2,1)S(1)}, u32[]{:S(2)}, u32[]{:S(2)}) collective-permute-start(bf16[2,64,1024]{2,1,0:T(8,128)(2,1)S(1)} %copy-done.11), channel_id=1, source_target_pairs={{0,64},{1,17},{2,66},{3,19},{4,68},{5,21},{6,70},{7,23},{8,72},{9,... | collective-permute-start | bytes 786440 | tf_op jit(solution)/shard_map/ppermute | solution.py:39
  106.2 8.7 %collective-permute-start.27 = (bf16[2,64,1024]{2,1,0:T(8,128)(2,1)S(1)}, bf16[2,64,1024]{2,1,0:T(8,128)(2,1)S(1)}, u32[]{:S(2)}, u32[]{:S(2)}) collective-permute-start(bf16[2,64,1024]{2,1,0:T(8,128)(2,1)S(1)} %copy-done.9), channel_id=1, source_target_pairs={{0,32},{1,9},{2,34},{3,11},{4,36},{5,13},{6,38},{7,15},{8,40},{9,1... | collective-permute-start | bytes 786440 | tf_op jit(solution)/shard_map/ppermute | solution.py:39
  106.2 14.9 %collective-permute-start.35 = (bf16[2,4,16,1024]{3,2,1,0:T(8,128)(2,1)S(1)}, bf16[2,4,16,1024]{3,2,1,0:T(8,128)(2,1)S(1)}, u32[]{:S(2)}, u32[]{:S(2)}) collective-permute-start(bf16[2,4,16,1024]{3,2,1,0:T(8,128)(2,1)S(1)} %get-tuple-element.125), channel_id=1, source_target_pairs={{0,6},{1,7},{2,0},{3,1},{4,2},{5,3},{6,4},{7,5},{8,14},{9,15},{10,... | collective-permute-start | bytes 786440 | tf_op jit(solution)/shard_map/ppermute | solution.py:45
  108.9 15.4 %collective-permute-start.36 = (bf16[2,4,16,1024]{3,2,1,0:T(8,128)(2,1)S(1)}, bf16[2,4,16,1024]{3,2,1,0:T(8,128)(2,1)S(1)}, u32[]{:S(2)}, u32[]{:S(2)}) collective-permute-start(bf16[2,4,16,1024]{3,2,1,0:T(8,128)(2,1)S(1)} %get-tuple-element.126), channel_id=1, source_target_pairs={{0,4},{1,5},{2,6},{3,7},{4,0},{5,1},{6,2},{7,3},{8,12},{9,13},{10,... | collective-permute-start | bytes 786440 | tf_op jit(solution)/shard_map/ppermute | solution.py:45
  114.9 9.4 %collective-permute-start.37 = (bf16[2,4,16,1024]{3,2,1,0:T(8,128)(2,1)S(1)}, bf16[2,4,16,1024]{3,2,1,0:T(8,128)(2,1)S(1)}, u32[]{:S(2)}, u32[]{:S(2)}) collective-permute-start(bf16[2,4,16,1024]{3,2,1,0:T(8,128)(2,1)S(1)} %get-tuple-element.127), channel_id=1, source_target_pairs={{0,2},{1,3},{2,4},{3,5},{4,6},{5,7},{6,0},{7,1},{8,10},{9,11},{10,... | collective-permute-start | bytes 786440 | tf_op jit(solution)/shard_map/ppermute | solution.py:45
  116.4 9.9 %collective-permute-start.31 = (bf16[2,4,16,1024]{3,2,1,0:T(8,128)(2,1)S(1)}, bf16[2,4,16,1024]{3,2,1,0:T(8,128)(2,1)S(1)}, u32[]{:S(2)}, u32[]{:S(2)}) collective-permute-start(bf16[2,4,16,1024]{3,2,1,0:T(8,128)(2,1)S(1)} %get-tuple-element.121), channel_id=1, source_target_pairs={{0,1},{1,0},{2,3},{3,2},{4,5},{5,4},{6,7},{7,6},{8,9},{9,8},{10,11... | collective-permute-start | bytes 786440 | tf_op jit(solution)/shard_map/ppermute | solution.py:45
  120.9 9.0 %collective-permute-start.32 = (bf16[2,4,16,1024]{3,2,1,0:T(8,128)(2,1)S(1)}, bf16[2,4,16,1024]{3,2,1,0:T(8,128)(2,1)S(1)}, u32[]{:S(2)}, u32[]{:S(2)}) collective-permute-start(bf16[2,4,16,1024]{3,2,1,0:T(8,128)(2,1)S(1)} %get-tuple-element.122), channel_id=1, source_target_pairs={{0,7},{1,6},{2,1},{3,0},{4,3},{5,2},{6,5},{7,4},{8,15},{9,14},{10,... | collective-permute-start | bytes 786440 | tf_op jit(solution)/shard_map/ppermute | solution.py:45
  121.2 11.9 %collective-permute-start.33 = (bf16[2,4,16,1024]{3,2,1,0:T(8,128)(2,1)S(1)}, bf16[2,4,16,1024]{3,2,1,0:T(8,128)(2,1)S(1)}, u32[]{:S(2)}, u32[]{:S(2)}) collective-permute-start(bf16[2,4,16,1024]{3,2,1,0:T(8,128)(2,1)S(1)} %get-tuple-element.123), channel_id=1, source_target_pairs={{0,5},{1,4},{2,7},{3,6},{4,1},{5,0},{6,3},{7,2},{8,13},{9,12},{10,... | collective-permute-start | bytes 786440 | tf_op jit(solution)/shard_map/ppermute | solution.py:45
  124.3 13.6 %collective-permute-start.34 = (bf16[2,4,16,1024]{3,2,1,0:T(8,128)(2,1)S(1)}, bf16[2,4,16,1024]{3,2,1,0:T(8,128)(2,1)S(1)}, u32[]{:S(2)}, u32[]{:S(2)}) collective-permute-start(bf16[2,4,16,1024]{3,2,1,0:T(8,128)(2,1)S(1)} %get-tuple-element.124), channel_id=1, source_target_pairs={{0,3},{1,2},{2,5},{3,4},{4,7},{5,6},{6,1},{7,0},{8,11},{9,10},{10,... | collective-permute-start | bytes 786440 | tf_op jit(solution)/shard_map/ppermute | solution.py:45
  (4 other events, 6.1 us)
Sparse Core Ops, SparseCore 0:
  9.7 44.7 all-gather.2
  104.3 33.8 reduce-scatter.1
